TPU v7x, 128 devices: a whole 4x4x4 slice. The times are simulated.
128 devices in a mesh: grp: 2 (over core), elem: 64 (over x, y, z).
Axes of the slice: x: 4, y: 4, z: 4, core: 2. Of those that a mesh axis runs over, the one named last changes fastest.
Arguments:
- state: float32 [2, 4, 512, 16384], P('grp', None, None, 'elem'), may hold values from -4 to 4
- mean_flow: float32 [3, 512, 16384], P(None, None, 'elem'), may hold values from -3 to 3
- jacobian: float32 [2, 512, 16384], P('grp', None, 'elem'), may hold values from 0.5 to 2
- send_elem: int32 [64, 64, 4], P('elem'), may hold values from 0 to 255
- recv_elem: int32 [64, 64, 4], P('elem'), may hold values from 0 to 255
- recv_count: int32 [64, 64], P('elem'), may hold values from 0 to 4, as said below
Outputs:
- state_out: float32 [2, 4, 512, 16384], P('grp', None, None, 'elem')
Inputs may be any that keep to these rules, and one draw needn't show every extreme that they name: `recv_count`: live slots per pair; in every draw some acoustic device has all 4 slots live from every LES device.
All inputs are finite; a program needn't handle non-finite values.
Results may differ from a plain program's by a relative error of at most 0.0003.
Values sent between devices are 32-bit elements; how exact they have to be, the bound alone decides.
No kernel may reach another device: no remote copies, remote signals or barrier semaphores. Data moves between devices by JAX's collectives and lax.ppermute only.
A program may use at most 128 MiB of HBM per device.

v0:
```python
import jax
import jax.numpy as jnp
import numpy as np
from jax import lax
from jax.experimental import pallas as pl
from jax.experimental.pallas import tpu as pltpu
from jax.sharding import PartitionSpec as P

NP = 8
NA = 6
EX = 16
EY = 8
LAYER = EX * EY
NODES = NP**3
PLANE = NP * NP
FIELDS = 4
COMP = NA**3
EDGE = 40
BLOCK = 1024
TILES = BLOCK // LAYER
EDGE_LO = 768
EDGE_HI = 896

les_speed_sq = 9.0
ape_speed_sq = 4.0
time_step = 0.004
f32 = jnp.float32
bf16 = jnp.bfloat16


def legendre_pair(points, node_pos):
    degree = points - 1
    before = np.ones(node_pos.shape[0])
    current = node_pos.copy()
    for order in range(2, degree + 1):
        after = ((2 * order - 1) * node_pos * current - (order - 1) * before) / order
        before = current
        current = after
    return (current, before)


def lobatto_tables(points):
    degree = points - 1
    node_pos = -np.cos(np.pi * np.arange(points) / degree)
    for sweep in range(100):
        top_vals, prev_vals = legendre_pair(points, node_pos)
        node_pos = node_pos - (node_pos * top_vals - prev_vals) / (points * top_vals)
    node_pos[0] = -1.0
    node_pos[points - 1] = 1.0
    node_vals, unused_vals = legendre_pair(points, node_pos)
    weights = 2.0 / (points * (points - 1) * node_vals**2)
    derivative = np.zeros((points, points))
    for target in range(points):
        for source in range(points):
            if target != source:
                derivative[target, source] = node_vals[target] / (
                    node_vals[source] * (node_pos[target] - node_pos[source])
                )
    derivative[0, 0] = -points * (points - 1) / 4.0
    derivative[points - 1, points - 1] = points * (points - 1) / 4.0
    return (node_pos, weights, derivative)


def split_np(table):
    high = table.astype(np.float32).astype(jnp.bfloat16)
    low = (table - high.astype(np.float64)).astype(np.float32).astype(jnp.bfloat16)
    return high, low


def tables():
    les_pos, les_wts, les_deriv = lobatto_tables(NP)
    ape_pos, ape_wts, ape_deriv = lobatto_tables(NA)
    deriv_pad = np.zeros((NP, NP))
    deriv_pad[:NA, :NA] = ape_deriv
    wts_pad = np.ones(NP)
    wts_pad[:NA] = ape_wts
    inside = np.zeros(NP)
    inside[:NA] = 1.0
    derivs = [les_deriv, deriv_pad]
    wts = [les_wts, wts_pad]
    masks = [np.ones(NP), inside]
    speeds = [les_speed_sq, ape_speed_sq]
    mats = []
    scalars = np.zeros((2, 128), np.float32)
    wtile = np.zeros((2, 2, NP, LAYER), np.float32)
    for g in range(2):
        both = np.concatenate(
            [np.kron(np.eye(NP), derivs[g]), np.kron(derivs[g], np.eye(NP))], axis=0
        )
        high, low = split_np(both)
        mats.append(np.concatenate([high, high, low], axis=1))
        scalars[g, :64] = derivs[g].reshape(-1)
        scalars[g, 64:72] = wts[g]
        scalars[g, 72:80] = masks[g]
        scalars[g, 80] = speeds[g]
        wtile[g, 0] = wts[g][:, None]
        wtile[g, 1] = masks[g][:, None]
    lagrange = np.ones((NA, NP))
    for target in range(NA):
        for source in range(NP):
            for pivot_id in range(NP):
                if pivot_id != source:
                    lagrange[target, source] *= (ape_pos[target] - les_pos[pivot_id]) / (
                        les_pos[source] - les_pos[pivot_id]
                    )
    compact = np.kron(lagrange, np.kron(lagrange, lagrange))
    interp = np.zeros((COMP + 2 * EDGE, NODES))
    interp[:COMP] = compact
    interp[COMP : COMP + NA * NA] = compact[: NA * NA]
    interp[COMP + EDGE : COMP + EDGE + NA * NA] = compact[COMP - NA * NA :]
    high, low = split_np(interp)
    interp_mats = np.stack([high, low])
    place = np.zeros((NA * PLANE, COMP))
    for slot in range(COMP):
        k, j, i = slot // (NA * NA), slot // NA % NA, slot % NA
        place[(k * NP + j) * NP + i, slot] = 1.0
    place_edge = np.zeros((PLANE, EDGE))
    place_edge[:, : NA * NA] = place[:PLANE, : NA * NA]
    return dict(
        mats=np.stack(mats),
        scalars=scalars,
        wtile=wtile,
        interp=interp_mats,
        place=np.concatenate([place, place], axis=1).astype(jnp.bfloat16),
        place_edge=np.concatenate([place_edge, place_edge], axis=1).astype(jnp.bfloat16),
    )


def dot(a, b):
    return lax.dot_general(a, b, (((1,), (0,)), ((), ())), preferred_element_type=f32)


def dot_nt(a, b):
    return lax.dot_general(a, b, (((1,), (1,)), ((), ())), preferred_element_type=f32)


def split(x):
    high = x.astype(bf16)
    return high, (x - high.astype(f32)).astype(bf16)


def lane_masks():
    lane = lax.broadcasted_iota(jnp.int32, (1, LAYER), 1)
    east = lane % EX
    return (
        (east > 0).astype(f32),
        (east < EX - 1).astype(f32),
        (lane >= EX).astype(f32),
        (lane < LAYER - EX).astype(f32),
    )


def pair_sum(lo, hi, stride, has_prev, has_next):
    return (
        lo + pltpu.roll(hi, stride, 1) * has_prev,
        hi + pltpu.roll(lo, LAYER - stride, 1) * has_next,
    )


def rows(start, size=NP):
    return pl.ds(pl.multiple_of(start, 8), size)


def sum_in_plane(ref, blocks, up, masks):
    px, nx, py, ny = masks
    for group in range(0, blocks, NP):
        count = min(NP, blocks - group)
        lo_at = pl.ds(group * PLANE, count * NP, stride=NP)
        hi_at = pl.ds(group * PLANE + up, count * NP, stride=NP)
        lo, hi = pair_sum(ref[lo_at, :], ref[hi_at, :], 1, px, nx)
        ref[lo_at, :] = lo
        ref[hi_at, :] = hi
        for k in range(group, group + count):
            lo_rows = rows(k * PLANE)
            hi_rows = rows(k * PLANE + up * NP)
            lo, hi = pair_sum(ref[lo_rows, :], ref[hi_rows, :], EX, py, ny)
            ref[lo_rows, :] = lo
            ref[hi_rows, :] = hi


def sum_inner(ref, fields, up):
    for f in range(fields):
        hi_rows = rows(f * NODES + up * PLANE, PLANE)
        lo_rows = rows((fields + f) * NODES, PLANE)
        both = ref[hi_rows, :] + ref[lo_rows, :]
        ref[hi_rows, :] = both
        ref[lo_rows, :] = both


def put_layers(ref, fields, row, value):
    ref[rows(row), :] = value[:, :LAYER]
    ref[rows(fields * NODES + row), :] = value[:, LAYER:]


def get_layers(ref, fields, at):
    low = ref[at, :]
    high = ref[slice(at.start + fields * NODES, at.stop + fields * NODES), :]
    return jnp.concatenate([low, high], axis=1)


def raw_stage(gid, up, scal, mats, v, w, flow, g, wr, lamb=None):
    is_les = gid == 0
    speed = scal[gid, 80]

    def body(k, carry):
        base = k * PLANE
        mat = mats[gid]
        for f in range(FIELDS):
            high, low = split(v[rows(f * NODES + base, PLANE), :])
            g[f] = dot(mat, jnp.concatenate([high, low, high], axis=0))
        d = [scal[gid, k * NP + q] for q in range(NP)]
        for j in range(NP):
            at = base + j * NP
            u = [v[rows(f * NODES + at), :] for f in range(FIELDS)]
            gx = [g[f, j * NP : (j + 1) * NP, :] for f in range(FIELDS)]
            gy = [g[f, PLANE + j * NP : PLANE + (j + 1) * NP, :] for f in range(FIELDS)]
            gz = []
            for f in range(FIELDS):
                total = d[0] * v[f * NODES + j * NP : f * NODES + (j + 1) * NP, :]
                for q in range(1, NP):
                    start = f * NODES + q * PLANE + j * NP
                    total = total + d[q] * v[start : start + NP, :]
                gz.append(total)
            a = [jnp.where(is_les, u[m], flow[rows(m * NODES + at), :]) for m in range(3)]
            carried = [a[0] * gx[f] + a[1] * gy[f] + a[2] * gz[f] for f in range(FIELDS)]
            weight = w[rows(at), :]
            press = (gx[3], gy[3], gz[3])
            for m in range(3):
                put_layers(wr, FIELDS, m * NODES + at, -weight * (carried[m] + press[m]))
            total = -weight * (carried[3] + speed * (gx[0] + gy[1] + gz[2]))
            put_layers(wr, FIELDS, 3 * NODES + at, total)
            if lamb is not None:
                vx = gy[2] - gz[1]
                vy = gz[0] - gx[2]
                vz = gx[1] - gy[0]
                lamb[rows(at), :] = vy * u[2] - vz * u[1]
                lamb[rows(NODES + at), :] = vz * u[0] - vx * u[2]
                lamb[rows(2 * NODES + at), :] = vx * u[1] - vy * u[0]
        return carry

    lax.fori_loop(0, NP, body, 0)


def put_planes(wr, up, up_out, down_out, fields):
    for f in range(fields):
        at = slice(f * PLANE, (f + 1) * PLANE)
        up_out[at, :] = wr[rows((fields + f) * NODES + up * PLANE, PLANE), :]
        down_out[at, :] = wr[f * NODES : f * NODES + PLANE, :]


def first_kernel(
    ids, scal, state, jac, flow, mats, wtile, interp, send, recv, count,
    block_out, wr_out, w_out, qw_out, up_out, down_out, g, lamb, comp,
):
    gid = ids[0]
    up = ids[1]
    masks = lane_masks()
    wi = wtile[gid, 0]
    wi = jnp.concatenate([wi, wi], axis=1)
    for k in range(NP):
        for j in range(NP):
            at = slice(k * PLANE + j * NP, k * PLANE + (j + 1) * NP)
            value = wi * (scal[gid, 64 + k] * scal[gid, 64 + j]) * jac[at, :]
            w_out[at, :] = value
            put_layers(qw_out, 1, k * PLANE + j * NP, value)
    raw_stage(gid, up, scal, mats, state, w_out, flow, g, wr_out, lamb)

    sum_in_plane(wr_out, 2 * FIELDS * NP, up, masks)
    put_planes(wr_out, up, up_out, down_out, FIELDS)
    sum_inner(wr_out, FIELDS, up)
    at = slice(FIELDS * PLANE, (FIELDS + 1) * PLANE)
    up_out[at, :] = w_out[rows(up * PLANE, PLANE), LAYER : 2 * LAYER]
    down_out[at, :] = w_out[0:PLANE, 0:LAYER]
    sum_in_plane(qw_out, 2 * NP, up, masks)
    sum_inner(qw_out, 1, up)
    peers = recv.shape[0]
    cap = recv.shape[1]
    slot = lax.broadcasted_iota(jnp.int32, (peers, cap), 1)
    target = jnp.where(slot < count[...], recv[...], -1).astype(f32)
    at = slice((FIELDS + 1) * PLANE, (FIELDS + 1) * PLANE + peers)
    up_out[at, :] = jnp.zeros((peers, LAYER), f32)
    down_out[at, :] = jnp.zeros((peers, LAYER), f32)
    up_out[at, 0:cap] = target
    down_out[at, 0:cap] = target

    @pl.when(gid == 0)
    def _():
        comp[3 * COMP : EDGE_LO, :] = jnp.zeros((EDGE_LO - 3 * COMP, 2 * LAYER), f32)
        comp[EDGE_LO + 3 * EDGE : EDGE_HI, :] = jnp.zeros((8, 2 * LAYER), f32)
        comp[EDGE_HI + 3 * EDGE : BLOCK, :] = jnp.zeros((8, 2 * LAYER), f32)
        for m in range(3):
            high, low = split(lamb[m * NODES : (m + 1) * NODES, :])
            got = dot(interp[0], high) + dot(interp[0], low) + dot(interp[1], high)
            comp[m * COMP : (m + 1) * COMP, :] = got[:COMP]
            comp[EDGE_LO + m * EDGE : EDGE_LO + (m + 1) * EDGE, :] = got[COMP : COMP + EDGE]
            comp[EDGE_HI + m * EDGE : EDGE_HI + (m + 1) * EDGE, :] = got[COMP + EDGE :]
        elem = lax.broadcasted_iota(jnp.int32, (peers, 2 * LAYER), 1)
        high, low = split(comp[...])
        for c in range(cap):
            pick = (send[:, c : c + 1] == elem).astype(f32).astype(bf16)
            got = dot_nt(pick, high) + dot_nt(pick, low)
            for t in range(TILES):
                value = got[:, t * LAYER : (t + 1) * LAYER]
                if t >= TILES - 2:
                    value = pltpu.roll(value, peers - 1 if t == TILES - 2 else 1, 0)
                block_out[pl.ds(t * cap + c, peers, stride=TILES * cap), :] = value


def add_planes(wr, up, from_below, from_above, fields):
    for f in range(fields):
        at = slice(f * PLANE, (f + 1) * PLANE)
        lo_rows = slice(f * NODES, f * NODES + PLANE)
        hi_rows = rows((fields + f) * NODES + up * PLANE, PLANE)
        wr[lo_rows, :] = wr[lo_rows, :] + from_below[at, :]
        wr[hi_rows, :] = wr[hi_rows, :] + from_above[at, :]


def pick_sum(blocks, target_cols, lanes):
    elem = lax.broadcasted_iota(jnp.int32, (target_cols[0].shape[0], 2 * LAYER), 1)
    pick = [(t == elem)[:, lanes].astype(f32).astype(bf16) for t in target_cols]
    high, low = split(jnp.transpose(blocks))
    pick = jnp.concatenate(pick, axis=0)
    return dot(high, pick) + dot(low, pick)


def second_kernel(
    ids, scal, block, recv, count, from_below, from_above, state, w, qw, flow, mats, place,
    place_edge, wr_in,
    wr_out, inv_out, acc_out, half_out, up_out, down_out, g, wr, v, src, edge,
):
    gid = ids[0]
    up = ids[1]
    masks = lane_masks()
    peers = recv.shape[0]
    cap = recv.shape[1]
    wr[...] = wr_in[...]
    inv_out[...] = qw[...]
    weights_at = slice(FIELDS * PLANE, (FIELDS + 1) * PLANE)
    edge[0:PLANE, :] = from_below[weights_at, :]
    edge[PLANE : 2 * PLANE, :] = from_above[weights_at, :]
    sum_in_plane(edge, 2, up, masks)
    add_planes(inv_out, up, edge.at[0:PLANE], edge.at[PLANE : 2 * PLANE], 1)
    inv_out[...] = 1.0 / inv_out[...]
    add_planes(wr, up, from_below, from_above, FIELDS)

    half_out[...] = state[...]

    @pl.when(gid == 1)
    def _():
        apeak = NA - 1
        slot = lax.broadcasted_iota(jnp.int32, (peers, cap), 1)
        target = jnp.where(slot < count[...], recv[...], -1)
        tiles = []
        for t in range(TILES):
            parts = [
                block[pl.ds(t * cap + c, peers, stride=TILES * cap), :] for c in range(cap)
            ]
            tiles.append(jnp.concatenate(parts, axis=0))
        cols = [target[:, c : c + 1] for c in range(cap)]
        own = pick_sum(jnp.concatenate(tiles[: TILES - 2], axis=1), cols, slice(0, 2 * LAYER))
        tables_at = slice((FIELDS + 1) * PLANE, (FIELDS + 1) * PLANE + peers)
        below = from_below[tables_at, :].astype(jnp.int32)
        above = from_above[tables_at, :].astype(jnp.int32)
        lo_edge = pick_sum(
            tiles[TILES - 2],
            [above[:, c : c + 1] for c in range(cap)],
            slice(0, LAYER),
        )
        hi_edge = pick_sum(
            tiles[TILES - 1],
            [below[:, c : c + 1] for c in range(cap)],
            slice(LAYER, 2 * LAYER),
        )
        for m in range(3):
            high, low = split(own[m * COMP : (m + 1) * COMP])
            full = dot(place[...], jnp.concatenate([high, low], axis=0))
            size = NA * PLANE
            full = full * w[0:size, :]
            for layer in range(2):
                start = (3 * layer + m) * NODES
                src[start : start + size, :] = full[:, layer * LAYER : (layer + 1) * LAYER]
                src[start + size : start + NODES, :] = jnp.zeros((NODES - size, LAYER), f32)
            high, low = split(hi_edge[m * EDGE : (m + 1) * EDGE])
            full = dot(place_edge[...], jnp.concatenate([high, low], axis=0))
            edge[m * PLANE : (m + 1) * PLANE, :] = full * from_below[weights_at, :]
            high, low = split(lo_edge[m * EDGE : (m + 1) * EDGE])
            full = dot(place_edge[...], jnp.concatenate([high, low], axis=0))
            edge[(3 + m) * PLANE : (4 + m) * PLANE, :] = full * from_above[weights_at, :]
        sum_in_plane(src, 6 * NP, apeak, masks)
        sum_in_plane(edge, 6, apeak, masks)
        sum_inner(src, 3, apeak)
        add_planes(src, apeak, edge.at[0 : 3 * PLANE], edge.at[3 * PLANE : 6 * PLANE], 3)
        for m in range(3):
            at = slice(m * NODES, (m + 1) * NODES)
            sigma = get_layers(src, 3, at) * get_layers(inv_out, 1, slice(0, NODES))
            half_out[at, :] = state[at, :] + (0.5 * time_step) * sigma

    for f in range(FIELDS):
        at = slice(f * NODES, (f + 1) * NODES)
        rate = get_layers(wr, FIELDS, at) * get_layers(inv_out, 1, slice(0, NODES))
        half = half_out[at, :]
        v[at, :] = half + (0.5 * time_step) * rate
        acc_out[at, :] = half + (half - state[at, :]) + (time_step / 6.0) * rate
    raw_stage(gid, up, scal, mats, v, w, flow, g, wr_out)
    sum_in_plane(wr_out, 2 * FIELDS * NP, up, masks)
    put_planes(wr_out, up, up_out, down_out, FIELDS)
    sum_inner(wr_out, FIELDS, up)


def later_kernel(step, share, ids, scal, from_below, from_above, state, half, w, inv, flow, mats, wr_in, acc_in,
                 wr_out, acc_out, up_out, down_out, g, wr, v):
    gid = ids[0]
    up = ids[1]
    masks = lane_masks()
    wr[...] = wr_in[...]
    add_planes(wr, up, from_below, from_above, FIELDS)
    for f in range(FIELDS):
        at = slice(f * NODES, (f + 1) * NODES)
        rate = get_layers(wr, FIELDS, at) * get_layers(inv, 1, slice(0, NODES))
        base = half[at, :]
        if step == time_step:
            base = base + (base - state[at, :])
        v[at, :] = base + step * rate
        acc_out[at, :] = acc_in[at, :] + share * rate
    raw_stage(gid, up, scal, mats, v, w, flow, g, wr_out)
    sum_in_plane(wr_out, 2 * FIELDS * NP, up, masks)
    put_planes(wr_out, up, up_out, down_out, FIELDS)
    sum_inner(wr_out, FIELDS, up)


def last_kernel(ids, scal, wtile, from_below, from_above, inv, wr_in, acc_in, out, wr):
    gid = ids[0]
    up = ids[1]
    wr[...] = wr_in[...]
    add_planes(wr, up, from_below, from_above, FIELDS)
    mi = wtile[gid, 1]
    mi = jnp.concatenate([mi, mi], axis=1)
    for k in range(NP):
        for j in range(NP):
            keep = mi * (scal[gid, 72 + k] * scal[gid, 72 + j])
            at = k * PLANE + j * NP
            scale = get_layers(inv, 1, slice(at, at + NP)) * (time_step / 6.0)
            for f in range(FIELDS):
                where = slice(f * NODES + at, f * NODES + at + NP)
                rate = scale * get_layers(wr, FIELDS, where)
                out[where, :] = keep * (acc_in[where, :] + rate)


SMEM = pl.BlockSpec(memory_space=pltpu.SMEM)
VMEM = pl.BlockSpec(memory_space=pltpu.VMEM)


def call(kernel, smem, args, outs, scratch):
    return pl.pallas_call(
        kernel,
        out_shape=[jax.ShapeDtypeStruct(s, f32) for s in outs],
        in_specs=[SMEM] * smem + [VMEM] * (len(args) - smem),
        out_specs=[VMEM] * len(outs),
        scratch_shapes=[pltpu.VMEM(s, f32) for s in scratch],
        compiler_params=pltpu.CompilerParams(vmem_limit_bytes=52 * 1024 * 1024),
    )(*args)


def on_device(state, mean_flow, jacobian, send_elem, recv_elem, recv_count):
    consts = tables()
    gid = lax.axis_index("grp").astype(jnp.int32)
    ids = jnp.stack([gid, jnp.where(gid == 0, NP - 1, NA - 1).astype(jnp.int32)])
    width = state.shape[-1]
    peers, cap = send_elem.shape[1:]
    state = state.reshape(FIELDS * NODES, width)
    flow = mean_flow.reshape(3 * NODES, width)
    jac = jacobian.reshape(NODES, width)
    send = send_elem.reshape(peers, cap)
    recv = recv_elem.reshape(peers, cap)
    count = recv_count.reshape(peers, 1)
    scal = jnp.asarray(consts["scalars"])
    mats = jnp.asarray(consts["mats"])
    wtile = jnp.asarray(consts["wtile"])
    interp = jnp.asarray(consts["interp"])
    place = jnp.asarray(consts["place"])
    place_edge = jnp.asarray(consts["place_edge"])
    full = (FIELDS * NODES, width)
    one = (NODES, width)
    layered = (2 * FIELDS * NODES, LAYER)
    one_layered = (2 * NODES, LAYER)
    thin = (FIELDS * PLANE, LAYER)
    grads = (FIELDS, 2 * PLANE, width)
    size = lax.axis_size("elem")
    up_pairs = [(i, (i + 1) % size) for i in range(size)]
    down_pairs = [(j, i) for i, j in up_pairs]

    def exchange(up_planes, down_planes):
        return (
            lax.ppermute(up_planes, "elem", up_pairs),
            lax.ppermute(down_planes, "elem", down_pairs),
        )

    thick = ((FIELDS + 1) * PLANE + peers, LAYER)
    block, wr, w, qw, up_planes, down_planes = call(
        first_kernel, 2,
        (ids, scal, state, jac, flow, mats, wtile, interp, send, recv, count),
        [(TILES * cap * peers, LAYER), layered, one, one_layered, thick, thick],
        [grads, (3 * NODES, width), (BLOCK, width)],
    )
    from_below, from_above = exchange(up_planes, down_planes)
    block = lax.all_to_all(block, "elem", split_axis=0, concat_axis=0, tiled=True)
    block = lax.ppermute(block, "grp", [(0, 1)])
    wr, inv, acc, half, up_planes, down_planes = call(
        second_kernel, 2,
        (ids, scal, block, recv, count, from_below, from_above, state, w, qw, flow, mats,
         place, place_edge, wr),
        [layered, one_layered, full, full, thin, thin],
        [grads, layered, full, (6 * NODES, LAYER), (6 * PLANE, LAYER)],
    )
    for step, share in ((0.5 * time_step, time_step / 3.0), (time_step, time_step / 3.0)):
        from_below, from_above = exchange(up_planes, down_planes)

        def kernel(*refs, step=step, share=share):
            later_kernel(step, share, *refs)

        wr, acc, up_planes, down_planes = call(
            kernel, 2,
            (ids, scal, from_below, from_above, state, half, w, inv, flow, mats, wr, acc),
            [layered, full, thin, thin],
            [grads, layered, full],
        )
    from_below, from_above = exchange(up_planes, down_planes)
    (out,) = call(
        last_kernel, 2,
        (ids, scal, wtile, from_below, from_above, inv, wr, acc),
        [full],
        [layered],
    )
    return out.reshape(1, FIELDS, NODES, width)


def solution(mesh):
    placed = (
        P("grp", None, None, "elem"),
        P(None, None, "elem"),
        P("grp", None, "elem"),
        P("elem", None, None),
        P("elem", None, None),
        P("elem", None),
    )
    return jax.shard_map(
        on_device,
        mesh=mesh,
        in_specs=placed,
        out_specs=P("grp", None, None, "elem"),
        check_vma=False,
    )
```

profile of v0, /device:TPU:0, one launch (start us, length us, event | category | flops | bytes accessed | tf_op | source)
XLA Modules:
  0.0 139.5 jit_solution(10770126172569111678)
XLA Ops:
  0.0 0.7 copy.15.count
  0.7 0.8 copy.13
  1.5 0.8 copy.14
  2.3 0.1 pad_add_fusion.ids.refs_0_
  2.4 0.9 copy-done.2
  3.3 0.7 copy-done.5
  4.0 0.7 copy-done.7
  4.7 15.1 %shard_map.118 = (f32[2048,128]{1,0:T(8,128)}, f32[4096,128]{1,0:T(8,128)}, f32[512,256]{1,0:T(8,128)S(1)}, f32[1024,128]{1,0:T(8,128)S(1)}, f32[384,128]{1,0:T(8,128)S(1)}, /*index=5*/f32[384,128]{1,0:T(8,128)S(1)}) custom-call(s32[2]{0:T(128)S(1)} %pad_add_fusion.ids.refs_0_, f32[2,128]{1,0:T(2,128)S(1)} %copy-done.7, f32[2048,256]{1,0:T(8,128)} %bitcast.14, ...), custom_call_target="tpu_custom_call" | custom-call | tf_op jit(solution)/shard_map/pallas_call | solution.py:454
  19.8 0.8 copy-done
  20.6 27.5 %all_to_all.12 = f32[64,32,128]{2,1,0:T(8,128)S(1)} all-to-all(f32[64,32,128]{2,1,0:T(8,128)} %bitcast.23), channel_id=1, replica_groups=mesh['grp'=2,'elem'=64] {'elem'}, dimensions={0} | all-to-all | bytes 2097152 | tf_op jit(solution)/shard_map/all_to_all | solution.py:506
  48.1 1.3 collective-permute-start
  49.4 0.6 collective-permute-start.1
  50.1 6.9 %collective-permute-start.2 = (f32[384,128]{1,0:T(8,128)S(1)}, f32[384,128]{1,0:T(8,128)S(1)}, u32[]{:S(2)}, u32[]{:S(2)}) collective-permute-start(f32[384,128]{1,0:T(8,128)S(1)} %get-tuple-element.27), channel_id=1, source_target_pairs={{1,0},{2,1},{3,2},{4,3},{5,4},{6,5},{7,6},{8,7},{9,8},{10,9},{11,1... | collective-permute-start | bytes 589832 | tf_op jit(solution)/shard_map/ppermute | solution.py:495
  57.0 3.6 %collective-permute-done.1.from_below = f32[384,128]{1,0:T(8,128)S(1)} collective-permute-done((f32[384,128]{1,0:T(8,128)S(1)}, f32[384,128]{1,0:T(8,128)S(1)}, u32[]{:S(2)}, u32[]{:S(2)}) %collective-permute-start.1) | collective-permute-done | bytes 196640 | tf_op jit(solution)/shard_map/ppermute | solution.py:494
  60.6 0.0 collective-permute-done.2.from_above
  60.6 0.0 collective-permute-done.block
  60.6 1.0 copy-done.9
  61.6 13.8 %shard_map.119 = (f32[4096,128]{1,0:T(8,128)}, f32[1024,128]{1,0:T(8,128)S(1)}, f32[2048,256]{1,0:T(8,128)}, f32[2048,256]{1,0:T(8,128)}, f32[256,128]{1,0:T(8,128)S(1)}, /*index=5*/f32[256,128]{1,0:T(8,128)S(1)}) custom-call(s32[2]{0:T(128)S(1)} %pad_add_fusion.ids.refs_0_, f32[2,128]{1,0:T(2,128)S(1)} %copy-done.7, f32[2048,128]{1,0:T(8,128)} %copy-done.9, ...), custom_call_target="tpu_custom_call" | custom-call | tf_op jit(solution)/shard_map/pallas_call | solution.py:454
  75.4 0.0 collective-permute-start.3
  75.4 7.5 %collective-permute-start.4 = (f32[256,128]{1,0:T(8,128)S(1)}, f32[256,128]{1,0:T(8,128)S(1)}, u32[]{:S(2)}, u32[]{:S(2)}) collective-permute-start(f32[256,128]{1,0:T(8,128)S(1)} %get-tuple-element.32), channel_id=1, source_target_pairs={{1,0},{2,1},{3,2},{4,3},{5,4},{6,5},{7,6},{8,7},{9,8},{10,9},{11,1... | collective-permute-start | bytes 393224 | tf_op jit(solution)/shard_map/ppermute | solution.py:495
  82.9 2.9 %collective-permute-done.3.refs_2_ = f32[256,128]{1,0:T(8,128)S(1)} collective-permute-done((f32[256,128]{1,0:T(8,128)S(1)}, f32[256,128]{1,0:T(8,128)S(1)}, u32[]{:S(2)}, u32[]{:S(2)}) %collective-permute-start.3) | collective-permute-done | bytes 131104 | tf_op jit(solution)/shard_map/ppermute | solution.py:494
  85.8 0.0 collective-permute-done.4.refs_3_
  85.8 14.1 %shard_map.120 = (f32[4096,128]{1,0:T(8,128)}, f32[2048,256]{1,0:T(8,128)}, f32[256,128]{1,0:T(8,128)S(1)}, f32[256,128]{1,0:T(8,128)S(1)}) custom-call(s32[2]{0:T(128)S(1)} %pad_add_fusion.ids.refs_0_, f32[2,128]{1,0:T(2,128)S(1)} %copy-done.7, f32[256,128]{1,0:T(8,128)S(1)} %collective-permute-done.3.refs_2_, ...), custom_call_target="tpu_custom_call" | custom-call | tf_op jit(solution)/shard_map/pallas_call | solution.py:454
  100.0 0.0 collective-permute-start.5
  100.0 7.6 %collective-permute-start.6 = (f32[256,128]{1,0:T(8,128)S(1)}, f32[256,128]{1,0:T(8,128)S(1)}, u32[]{:S(2)}, u32[]{:S(2)}) collective-permute-start(f32[256,128]{1,0:T(8,128)S(1)} %get-tuple-element.38), channel_id=1, source_target_pairs={{1,0},{2,1},{3,2},{4,3},{5,4},{6,5},{7,6},{8,7},{9,8},{10,9},{11,1... | collective-permute-start | bytes 393224 | tf_op jit(solution)/shard_map/ppermute | solution.py:495
  107.5 2.9 %collective-permute-done.5.refs_2_ = f32[256,128]{1,0:T(8,128)S(1)} collective-permute-done((f32[256,128]{1,0:T(8,128)S(1)}, f32[256,128]{1,0:T(8,128)S(1)}, u32[]{:S(2)}, u32[]{:S(2)}) %collective-permute-start.5) | collective-permute-done | bytes 131104 | tf_op jit(solution)/shard_map/ppermute | solution.py:494
  110.4 0.0 collective-permute-done.6.refs_3_
  110.4 14.6 %shard_map.121 = (f32[4096,128]{1,0:T(8,128)}, f32[2048,256]{1,0:T(8,128)}, f32[256,128]{1,0:T(8,128)S(1)}, f32[256,128]{1,0:T(8,128)S(1)}) custom-call(s32[2]{0:T(128)S(1)} %pad_add_fusion.ids.refs_0_, f32[2,128]{1,0:T(2,128)S(1)} %copy-done.7, f32[256,128]{1,0:T(8,128)S(1)} %collective-permute-done.5.refs_2_, ...), custom_call_target="tpu_custom_call" | custom-call | tf_op jit(solution)/shard_map/pallas_call | solution.py:454
  125.0 0.0 collective-permute-start.7
  125.0 7.5 %collective-permute-start.8 = (f32[256,128]{1,0:T(8,128)S(1)}, f32[256,128]{1,0:T(8,128)S(1)}, u32[]{:S(2)}, u32[]{:S(2)}) collective-permute-start(f32[256,128]{1,0:T(8,128)S(1)} %get-tuple-element.42), channel_id=1, source_target_pairs={{1,0},{2,1},{3,2},{4,3},{5,4},{6,5},{7,6},{8,7},{9,8},{10,9},{11,1... | collective-permute-start | bytes 393224 | tf_op jit(solution)/shard_map/ppermute | solution.py:495
  132.5 2.9 %collective-permute-done.7.from_below = f32[256,128]{1,0:T(8,128)S(1)} collective-permute-done((f32[256,128]{1,0:T(8,128)S(1)}, f32[256,128]{1,0:T(8,128)S(1)}, u32[]{:S(2)}, u32[]{:S(2)}) %collective-permute-start.7) | collective-permute-done | bytes 131104 | tf_op jit(solution)/shard_map/ppermute | solution.py:494
  135.5 4.0 %shard_map.122 = f32[2048,256]{1,0:T(8,128)} custom-call(s32[2]{0:T(128)S(1)} %pad_add_fusion.ids.refs_0_, f32[2,128]{1,0:T(2,128)S(1)} %copy-done.7, f32[2,2,8,128]{3,2,1,0:T(8,128)S(1)} %copy-done.6, f32[256,128]{1,0:T(8,128)S(1)} %collective-permute-done.7.from_below, f32[256,128]{1,0:T(8,128)S(1)} %collective-permute-done.8.from_above, ...), custom_call_target="tpu_custom_call" | custom-call | tf_op jit(solution)/shard_map/pallas_call | solution.py:454
  (16 shorter events, 0.0 us)
Async XLA Ops:
  2.4 0.9 copy-start.2
  3.3 0.7 copy-start.5
  4.0 0.7 copy-start.7
  19.8 0.8 copy-start
  20.5 40.1 %copy-start.3 = (f32[1024,128]{1,0:T(8,128)}, f32[1024,128]{1,0:T(8,128)S(1)}, u32[]{:S(2)}) copy-start(f32[1024,128]{1,0:T(8,128)S(1)} %get-tuple-element.29.qw) | copy-start | bytes 1572868
  20.5 41.0 %copy-start.4 = (bf16[384,432]{1,0:T(8,128)(2,1)S(1)}, bf16[384,432]{1,0:T(8,128)(2,1)}, u32[]{:S(2)}) copy-start(bf16[384,432]{1,0:T(8,128)(2,1)} %constant.28.clone.place) | copy-start | bytes 995332
  20.6 41.0 %copy-start.8 = (bf16[64,80]{1,0:T(8,128)(2,1)S(1)}, bf16[64,80]{1,0:T(8,128)(2,1)}, u32[]{:S(2)}) copy-start(bf16[64,80]{1,0:T(8,128)(2,1)} %constant.29.clone.place_edge) | copy-start | bytes 30724
  48.1 12.5 %collective-permute-start = (f32[2048,128]{1,0:T(8,128)S(1)}, f32[2048,128]{1,0:T(8,128)S(1)}, u32[]{:S(2)}, u32[]{:S(2)}) collective-permute-start(f32[2048,128]{1,0:T(8,128)S(1)} %bitcast.22), channel_id=1, source_target_pairs={{0,64},{1,65},{2,66},{3,67},{4,68},{5,69},{6,70},{7,71},{8,72},{9,... | collective-permute-start | bytes 3145736 | tf_op jit(solution)/shard_map/ppermute | solution.py:507
  49.4 11.2 %collective-permute-start.1 = (f32[384,128]{1,0:T(8,128)S(1)}, f32[384,128]{1,0:T(8,128)S(1)}, u32[]{:S(2)}, u32[]{:S(2)}) collective-permute-start(f32[384,128]{1,0:T(8,128)S(1)} %get-tuple-element.26), channel_id=1, source_target_pairs={{0,1},{1,2},{2,3},{3,4},{4,5},{5,6},{6,7},{7,8},{8,9},{9,10},{10,1... | collective-permute-start | bytes 589832 | tf_op jit(solution)/shard_map/ppermute | solution.py:494
  50.1 10.5 %collective-permute-start.2 = (f32[384,128]{1,0:T(8,128)S(1)}, f32[384,128]{1,0:T(8,128)S(1)}, u32[]{:S(2)}, u32[]{:S(2)}) collective-permute-start(f32[384,128]{1,0:T(8,128)S(1)} %get-tuple-element.27), channel_id=1, source_target_pairs={{1,0},{2,1},{3,2},{4,3},{5,4},{6,5},{7,6},{8,7},{9,8},{10,9},{11,1... | collective-permute-start | bytes 589832 | tf_op jit(solution)/shard_map/ppermute | solution.py:495
  60.6 1.0 copy-start.9
  61.6 24.2 %copy-start.1 = (f32[512,256]{1,0:T(8,128)S(1)}, f32[512,256]{1,0:T(8,128)}, u32[]{:S(2)}) copy-start(f32[512,256]{1,0:T(8,128)} %copy-done) | copy-start | bytes 1572868
  75.4 10.4 %collective-permute-start.3 = (f32[256,128]{1,0:T(8,128)S(1)}, f32[256,128]{1,0:T(8,128)S(1)}, u32[]{:S(2)}, u32[]{:S(2)}) collective-permute-start(f32[256,128]{1,0:T(8,128)S(1)} %get-tuple-element.31), channel_id=1, source_target_pairs={{0,1},{1,2},{2,3},{3,4},{4,5},{5,6},{6,7},{7,8},{8,9},{9,10},{10,1... | collective-permute-start | bytes 393224 | tf_op jit(solution)/shard_map/ppermute | solution.py:494
  75.4 10.4 %collective-permute-start.4 = (f32[256,128]{1,0:T(8,128)S(1)}, f32[256,128]{1,0:T(8,128)S(1)}, u32[]{:S(2)}, u32[]{:S(2)}) collective-permute-start(f32[256,128]{1,0:T(8,128)S(1)} %get-tuple-element.32), channel_id=1, source_target_pairs={{1,0},{2,1},{3,2},{4,3},{5,4},{6,5},{7,6},{8,7},{9,8},{10,9},{11,1... | collective-permute-start | bytes 393224 | tf_op jit(solution)/shard_map/ppermute | solution.py:495
  100.0 10.5 %collective-permute-start.5 = (f32[256,128]{1,0:T(8,128)S(1)}, f32[256,128]{1,0:T(8,128)S(1)}, u32[]{:S(2)}, u32[]{:S(2)}) collective-permute-start(f32[256,128]{1,0:T(8,128)S(1)} %get-tuple-element.37), channel_id=1, source_target_pairs={{0,1},{1,2},{2,3},{3,4},{4,5},{5,6},{6,7},{7,8},{8,9},{9,10},{10,1... | collective-permute-start | bytes 393224 | tf_op jit(solution)/shard_map/ppermute | solution.py:494
  100.0 10.5 %collective-permute-start.6 = (f32[256,128]{1,0:T(8,128)S(1)}, f32[256,128]{1,0:T(8,128)S(1)}, u32[]{:S(2)}, u32[]{:S(2)}) collective-permute-start(f32[256,128]{1,0:T(8,128)S(1)} %get-tuple-element.38), channel_id=1, source_target_pairs={{1,0},{2,1},{3,2},{4,3},{5,4},{6,5},{7,6},{8,7},{9,8},{10,9},{11,1... | collective-permute-start | bytes 393224 | tf_op jit(solution)/shard_map/ppermute | solution.py:495
  110.4 25.0 %copy-start.6 = (f32[2,2,8,128]{3,2,1,0:T(8,128)S(1)}, f32[2,2,8,128]{3,2,1,0:T(8,128)}, u32[]{:S(2)}) copy-start(f32[2,2,8,128]{3,2,1,0:T(8,128)} %constant.26.clone.wtile) | copy-start | bytes 49156
  125.0 10.5 %collective-permute-start.7 = (f32[256,128]{1,0:T(8,128)S(1)}, f32[256,128]{1,0:T(8,128)S(1)}, u32[]{:S(2)}, u32[]{:S(2)}) collective-permute-start(f32[256,128]{1,0:T(8,128)S(1)} %get-tuple-element.41), channel_id=1, source_target_pairs={{0,1},{1,2},{2,3},{3,4},{4,5},{5,6},{6,7},{7,8},{8,9},{9,10},{10,1... | collective-permute-start | bytes 393224 | tf_op jit(solution)/shard_map/ppermute | solution.py:494
  125.0 10.5 %collective-permute-start.8 = (f32[256,128]{1,0:T(8,128)S(1)}, f32[256,128]{1,0:T(8,128)S(1)}, u32[]{:S(2)}, u32[]{:S(2)}) collective-permute-start(f32[256,128]{1,0:T(8,128)S(1)} %get-tuple-element.42), channel_id=1, source_target_pairs={{1,0},{2,1},{3,2},{4,3},{5,4},{6,5},{7,6},{8,7},{9,8},{10,9},{11,1... | collective-permute-start | bytes 393224 | tf_op jit(solution)/shard_map/ppermute | solution.py:495
where the time goes:
time: 140 us; the launch traced here: 139 us
  Pallas kernels  61.6 us (44%)
  starting transfers between devices  31.5 us (22%)
  blocking collectives  27.5 us (20%)
  waiting for transfers between devices  12.4 us (9%)
  local copies, waits for them, and re-layouts  6.35 us (5%)
    pallas_call x5, Pallas kernels, call(): pl.pallas_call(kernel, out_shape=[jax.ShapeDtypeStruct(s, f32) for s in o...  61.6 us
    ppermute x4, starting transfers between devices, exchange(): lax.ppermute(down_planes, 'elem', down_pairs)  29.5 us
    all_to_all x1, blocking collectives, on_device(): lax.all_to_all(block, 'elem', split_axis=0, concat_axis=0, tiled=True)  27.5 us
    ppermute x4, waiting for transfers between devices, exchange(): lax.ppermute(up_planes, 'elem', up_pairs)  12.3 us
    unnamed x22, local copies, waits for them, and re-layouts  5.61 us
  transfers between devices with their start and end apart: 9, of which 4 were waited for; matrix products, arithmetic and copies ran while one was open for 0% of the time, Pallas kernels for 0%

commit v1 on v0

v1 whole, which is shorter than its diff:
```python
import jax
import jax.numpy as jnp
import numpy as np
from jax import lax
from jax.experimental import pallas as pl
from jax.experimental.pallas import tpu as pltpu
from jax.sharding import PartitionSpec as P

NP = 8
NA = 6
EX = 16
EY = 8
LAYER = EX * EY
NODES = NP**3
PLANE = NP * NP
FIELDS = 4
COMP = NA**3
EDGE = 40
BLOCK = 1024
TILES = BLOCK // LAYER
EDGE_LO = 768
EDGE_HI = 896

les_speed_sq = 9.0
ape_speed_sq = 4.0
time_step = 0.004
f32 = jnp.float32
bf16 = jnp.bfloat16


def legendre_pair(points, node_pos):
    degree = points - 1
    before = np.ones(node_pos.shape[0])
    current = node_pos.copy()
    for order in range(2, degree + 1):
        after = ((2 * order - 1) * node_pos * current - (order - 1) * before) / order
        before = current
        current = after
    return (current, before)


def lobatto_tables(points):
    degree = points - 1
    node_pos = -np.cos(np.pi * np.arange(points) / degree)
    for sweep in range(100):
        top_vals, prev_vals = legendre_pair(points, node_pos)
        node_pos = node_pos - (node_pos * top_vals - prev_vals) / (points * top_vals)
    node_pos[0] = -1.0
    node_pos[points - 1] = 1.0
    node_vals, unused_vals = legendre_pair(points, node_pos)
    weights = 2.0 / (points * (points - 1) * node_vals**2)
    derivative = np.zeros((points, points))
    for target in range(points):
        for source in range(points):
            if target != source:
                derivative[target, source] = node_vals[target] / (
                    node_vals[source] * (node_pos[target] - node_pos[source])
                )
    derivative[0, 0] = -points * (points - 1) / 4.0
    derivative[points - 1, points - 1] = points * (points - 1) / 4.0
    return (node_pos, weights, derivative)


def split_np(table):
    high = table.astype(np.float32).astype(jnp.bfloat16)
    low = (table - high.astype(np.float64)).astype(np.float32).astype(jnp.bfloat16)
    return high, low


def tables():
    les_pos, les_wts, les_deriv = lobatto_tables(NP)
    ape_pos, ape_wts, ape_deriv = lobatto_tables(NA)
    mats = []
    for points, deriv in ((NP, les_deriv), (NA, ape_deriv)):
        wide = np.zeros((NP, NP))
        wide[:points, :points] = deriv
        both = np.concatenate(
            [np.kron(np.eye(points), wide), np.kron(deriv, np.eye(NP))], axis=0
        )
        high, low = split_np(both)
        mats.append(np.concatenate([high, high, low], axis=1))
    lagrange = np.ones((NA, NP))
    for target in range(NA):
        for source in range(NP):
            for pivot_id in range(NP):
                if pivot_id != source:
                    lagrange[target, source] *= (ape_pos[target] - les_pos[pivot_id]) / (
                        les_pos[source] - les_pos[pivot_id]
                    )
    compact = np.kron(lagrange, np.kron(lagrange, lagrange))
    interp = np.zeros((COMP + 2 * EDGE, NODES))
    interp[:COMP] = compact
    interp[COMP : COMP + NA * NA] = compact[: NA * NA]
    interp[COMP + EDGE : COMP + EDGE + NA * NA] = compact[COMP - NA * NA :]
    high, low = split_np(interp)
    place = np.zeros((NA * PLANE, COMP))
    for slot in range(COMP):
        k, j, i = slot // (NA * NA), slot // NA % NA, slot % NA
        place[(k * NP + j) * NP + i, slot] = 1.0
    place_edge = np.zeros((PLANE, EDGE))
    place_edge[:, : NA * NA] = place[:PLANE, : NA * NA]
    return dict(
        derivs=(les_deriv, ape_deriv),
        weights=(les_wts, ape_wts),
        mats=mats,
        interp=np.stack([high, low]),
        place=np.concatenate([place, place], axis=1).astype(jnp.bfloat16),
        place_edge=np.concatenate([place_edge, place_edge], axis=1).astype(jnp.bfloat16),
    )


CONSTS = tables()
POINTS = (NP, NA)
SPEEDS = (les_speed_sq, ape_speed_sq)


def dot(a, b):
    return lax.dot_general(a, b, (((1,), (0,)), ((), ())), preferred_element_type=f32)


def dot_nt(a, b):
    return lax.dot_general(a, b, (((1,), (1,)), ((), ())), preferred_element_type=f32)


def split(x):
    high = x.astype(bf16)
    return high, (x - high.astype(f32)).astype(bf16)


def lane_masks():
    lane = lax.broadcasted_iota(jnp.int32, (1, LAYER), 1)
    east = lane % EX
    return (
        (east > 0).astype(f32),
        (east < EX - 1).astype(f32),
        (lane >= EX).astype(f32),
        (lane < LAYER - EX).astype(f32),
    )


def pair_sum(lo, hi, stride, has_prev, has_next):
    return (
        lo + pltpu.roll(hi, stride, 1) * has_prev,
        hi + pltpu.roll(lo, LAYER - stride, 1) * has_next,
    )


def sum_in_plane(ref, blocks, up, masks):
    px, nx, py, ny = masks
    for group in range(0, blocks, NP):
        count = min(NP, blocks - group)
        lo_at = pl.ds(group * PLANE, count * NP, stride=NP)
        hi_at = pl.ds(group * PLANE + up, count * NP, stride=NP)
        lo, hi = pair_sum(ref[lo_at, :], ref[hi_at, :], 1, px, nx)
        ref[lo_at, :] = lo
        ref[hi_at, :] = hi
        for k in range(group, group + count):
            lo_rows = slice(k * PLANE, k * PLANE + NP)
            hi_rows = slice(k * PLANE + up * NP, k * PLANE + (up + 1) * NP)
            lo, hi = pair_sum(ref[lo_rows, :], ref[hi_rows, :], EX, py, ny)
            ref[lo_rows, :] = lo
            ref[hi_rows, :] = hi


def sum_inner(ref, fields, up):
    for f in range(fields):
        hi_rows = span(f * NODES + up * PLANE, PLANE)
        lo_rows = span((fields + f) * NODES, PLANE)
        both = ref[hi_rows, :] + ref[lo_rows, :]
        ref[hi_rows, :] = both
        ref[lo_rows, :] = both


def span(start, size=NP):
    return slice(start, start + size)


def put_layers(ref, fields, row, value):
    size = value.shape[0]
    ref[span(row, size), :] = value[:, :LAYER]
    ref[span(fields * NODES + row, size), :] = value[:, LAYER:]


def get_layers(ref, fields, row, size):
    return jnp.concatenate(
        [ref[span(row, size), :], ref[span(fields * NODES + row, size), :]], axis=1
    )


def z_derivative(d, k, points, v, f, j):
    total = None
    for q in range(points):
        if d[k, q] != 0.0:
            part = float(d[k, q]) * v[span(f * NODES + q * PLANE + j * NP), :]
            total = part if total is None else total + part
    return total


def raw_stage(group, mat, v, w, flow, g, wr, lamb=None):
    points = POINTS[group]
    d = CONSTS["derivs"][group]
    size = points * NP
    for k in range(points):
        base = k * PLANE
        for f in range(FIELDS):
            high, low = split(v[span(f * NODES + base, size), :])
            g[k % 2, f, : 2 * size, :] = dot(mat[...], jnp.concatenate([high, low, high], axis=0))
        for j in range(points):
            at = base + j * NP
            gx = [g[k % 2, f, span(j * NP), :] for f in range(FIELDS)]
            gy = [g[k % 2, f, span(size + j * NP), :] for f in range(FIELDS)]
            gz = [z_derivative(d, k, points, v, f, j) for f in range(FIELDS)]
            u = [v[span(m * NODES + at), :] for m in range(3)]
            a = u if group == 0 else [flow[span(m * NODES + at), :] for m in range(3)]
            carried = [a[0] * gx[f] + a[1] * gy[f] + a[2] * gz[f] for f in range(FIELDS)]
            weight = -w[span(at), :]
            press = (gx[3], gy[3], gz[3])
            for m in range(3):
                put_layers(wr, FIELDS, m * NODES + at, weight * (carried[m] + press[m]))
            total = weight * (carried[3] + SPEEDS[group] * (gx[0] + gy[1] + gz[2]))
            put_layers(wr, FIELDS, 3 * NODES + at, total)
            if lamb is not None:
                vx = gy[2] - gz[1]
                vy = gz[0] - gx[2]
                vz = gx[1] - gy[0]
                lamb[span(at), :] = vy * u[2] - vz * u[1]
                lamb[span(NODES + at), :] = vz * u[0] - vx * u[2]
                lamb[span(2 * NODES + at), :] = vx * u[1] - vy * u[0]


def put_planes(wr, up, up_out, down_out, fields):
    for f in range(fields):
        at = span(f * PLANE, PLANE)
        up_out[at, :] = wr[span((fields + f) * NODES + up * PLANE, PLANE), :]
        down_out[at, :] = wr[span(f * NODES, PLANE), :]


def finish_stage(group, mat, v, w, flow, g, wr, up_out, down_out, lamb=None):
    up = POINTS[group] - 1
    raw_stage(group, mat, v, w, flow, g, wr, lamb)
    sum_in_plane(wr, 2 * FIELDS * NP, up, lane_masks())
    put_planes(wr, up, up_out, down_out, FIELDS)
    sum_inner(wr, FIELDS, up)


def each_group(ids, body):
    for group in range(2):
        pl.when(ids[0] == group)(lambda group=group: body(group))


def columns(row_table):
    cap, peers = row_table.shape
    tile = jnp.concatenate([row_table, jnp.zeros((cap, LAYER - peers), f32)], axis=1)
    tile = jnp.concatenate([tile, jnp.zeros((NP - cap, LAYER), f32)], axis=0)
    return jnp.transpose(tile)[:peers, :]


def targets(recv, count):
    slot = lax.broadcasted_iota(jnp.int32, recv.shape, 0)
    return jnp.where(slot < count[...], recv[...], -1).astype(f32)


def first_kernel(
    ids, state, jac, flow, les_mat, ape_mat, recv, count,
    lamb_out, wr_out, w_out, qw_out, up_out, down_out, g,
):
    def body(group):
        up = POINTS[group] - 1
        points = POINTS[group]
        wts = np.ones(NP)
        wts[:points] = CONSTS["weights"][group]
        sub = lax.broadcasted_iota(jnp.int32, (NP, 2 * LAYER), 0)
        wi = jnp.zeros((NP, 2 * LAYER), f32)
        for i in range(NP):
            wi = jnp.where(sub == i, float(wts[i]), wi)
        for k in range(NP):
            for j in range(NP):
                at = k * PLANE + j * NP
                value = (wi * float(wts[k] * wts[j])) * jac[span(at), :]
                w_out[span(at), :] = value
                put_layers(qw_out, 1, at, value)
        finish_stage(
            group, (les_mat, ape_mat)[group], state, w_out, flow, g, wr_out, up_out, down_out,
            lamb_out if group == 0 else None,
        )
        at = span(FIELDS * PLANE, PLANE)
        up_out[at, :] = w_out[span(up * PLANE, PLANE), LAYER : 2 * LAYER]
        down_out[at, :] = w_out[0:PLANE, 0:LAYER]
        sum_in_plane(qw_out, 2 * NP, up, lane_masks())
        sum_inner(qw_out, 1, up)

    each_group(ids, body)
    cap, peers = recv.shape
    at = span((FIELDS + 1) * PLANE, NP)
    up_out[at, :] = jnp.zeros((NP, LAYER), f32)
    down_out[at, :] = jnp.zeros((NP, LAYER), f32)
    at = span((FIELDS + 1) * PLANE, cap)
    target = targets(recv, count)
    up_out[at, 0:peers] = target
    down_out[at, 0:peers] = target


def block_kernel(ids, lamb, interp, send, block_out, comp):
    cap, peers = send.shape

    @pl.when(ids[0] == 0)
    def _():
        comp[3 * COMP : EDGE_LO, :] = jnp.zeros((EDGE_LO - 3 * COMP, 2 * LAYER), f32)
        comp[EDGE_LO + 3 * EDGE : EDGE_HI, :] = jnp.zeros((8, 2 * LAYER), f32)
        comp[EDGE_HI + 3 * EDGE : BLOCK, :] = jnp.zeros((8, 2 * LAYER), f32)
        for m in range(3):
            high, low = split(lamb[m * NODES : (m + 1) * NODES, :])
            got = dot(interp[0], high) + dot(interp[0], low) + dot(interp[1], high)
            comp[m * COMP : (m + 1) * COMP, :] = got[:COMP]
            comp[EDGE_LO + m * EDGE : EDGE_LO + (m + 1) * EDGE, :] = got[COMP : COMP + EDGE]
            comp[EDGE_HI + m * EDGE : EDGE_HI + (m + 1) * EDGE, :] = got[COMP + EDGE :]
        elem = lax.broadcasted_iota(jnp.int32, (peers, 2 * LAYER), 1)
        high, low = split(comp[...])
        table = columns(send[...].astype(f32)).astype(jnp.int32)
        for c in range(cap):
            pick = (table[:, c : c + 1] == elem).astype(f32).astype(bf16)
            got = dot_nt(pick, high) + dot_nt(pick, low)
            for t in range(TILES):
                value = got[:, t * LAYER : (t + 1) * LAYER]
                if t >= TILES - 2:
                    value = pltpu.roll(value, peers - 1 if t == TILES - 2 else 1, 0)
                block_out[pl.ds(t * cap + c, peers, stride=TILES * cap), :] = value


def add_planes(wr, up, from_below, from_above, fields):
    for f in range(fields):
        at = span(f * PLANE, PLANE)
        lo_rows = span(f * NODES, PLANE)
        hi_rows = span((fields + f) * NODES + up * PLANE, PLANE)
        wr[lo_rows, :] = wr[lo_rows, :] + from_below[at, :]
        wr[hi_rows, :] = wr[hi_rows, :] + from_above[at, :]


def pick_sum(blocks, table, cap, lanes):
    elem = lax.broadcasted_iota(jnp.int32, (table.shape[0], 2 * LAYER), 1).astype(f32)
    pick = [(table[:, c : c + 1] == elem)[:, lanes].astype(f32).astype(bf16) for c in range(cap)]
    high, low = split(jnp.transpose(blocks))
    pick = jnp.concatenate(pick, axis=0)
    return dot(high, pick) + dot(low, pick)


def update(group, half, state, wr, inv, v, step, acc_in, acc_out, share):
    points = POINTS[group]
    size = points * NP
    for k in range(points):
        scale = get_layers(inv, 1, k * PLANE, size)
        for f in range(FIELDS):
            at = f * NODES + k * PLANE
            rate = get_layers(wr, FIELDS, at, size) * scale
            base = half[span(at, size), :]
            if state is not None:
                start = state[span(at, size), :]
            if step == time_step:
                base = base + (base - start)
            v[span(at, size), :] = base + step * rate
            if acc_in is None:
                before = base + (base - start)
            else:
                before = acc_in[span(at, size), :]
            acc_out[span(at, size), :] = before + share * rate


def second_kernel(
    ids, block, recv, count, from_below, from_above, state, w, qw, flow, les_mat, ape_mat, place,
    place_edge, wr_in,
    wr_out, inv_out, acc_out, half_out, up_out, down_out, g, wr, v, src, edge,
):
    cap, peers = recv.shape
    weights_at = span(FIELDS * PLANE, PLANE)

    def source():
        up = NA - 1
        masks = lane_masks()
        tiles = []
        for t in range(TILES):
            parts = [
                block[pl.ds(t * cap + c, peers, stride=TILES * cap), :] for c in range(cap)
            ]
            tiles.append(jnp.concatenate(parts, axis=0))
        tables_at = span((FIELDS + 1) * PLANE, cap)
        own = columns(targets(recv, count))
        below = columns(from_below[tables_at, 0:peers])
        above = columns(from_above[tables_at, 0:peers])
        own = pick_sum(
            jnp.concatenate(tiles[: TILES - 2], axis=1), own, cap, slice(0, 2 * LAYER)
        )
        lo_edge = pick_sum(tiles[TILES - 2], above, cap, slice(0, LAYER))
        hi_edge = pick_sum(tiles[TILES - 1], below, cap, slice(LAYER, 2 * LAYER))
        for m in range(3):
            high, low = split(own[m * COMP : (m + 1) * COMP])
            full = dot(place[...], jnp.concatenate([high, low], axis=0))
            size = NA * PLANE
            put_layers(src, 3, m * NODES, full * w[0:size, :])
            high, low = split(hi_edge[m * EDGE : (m + 1) * EDGE])
            full = dot(place_edge[...], jnp.concatenate([high, low], axis=0))
            edge[span(m * PLANE, PLANE), :] = full * from_below[weights_at, :]
            high, low = split(lo_edge[m * EDGE : (m + 1) * EDGE])
            full = dot(place_edge[...], jnp.concatenate([high, low], axis=0))
            edge[span((3 + m) * PLANE, PLANE), :] = full * from_above[weights_at, :]
        sum_in_plane(src, 6 * NP, up, masks)
        sum_in_plane(edge, 6, up, masks)
        sum_inner(src, 3, up)
        add_planes(src, up, edge.at[0 : 3 * PLANE], edge.at[3 * PLANE : 6 * PLANE], 3)
        size = NA * NP
        for k in range(NA):
            scale = (0.5 * time_step) * get_layers(inv_out, 1, k * PLANE, size)
            for f in range(FIELDS):
                at = f * NODES + k * PLANE
                value = state[span(at, size), :]
                if f < 3:
                    value = value + scale * get_layers(src, 3, at, size)
                half_out[span(at, size), :] = value

    def body(group):
        up = POINTS[group] - 1
        wr[...] = wr_in[...]
        inv_out[...] = qw[...]
        edge[0:PLANE, :] = from_below[weights_at, :]
        edge[PLANE : 2 * PLANE, :] = from_above[weights_at, :]
        sum_in_plane(edge, 2, up, lane_masks())
        add_planes(inv_out, up, edge.at[0:PLANE], edge.at[PLANE : 2 * PLANE], 1)
        inv_out[...] = 1.0 / inv_out[...]
        add_planes(wr, up, from_below, from_above, FIELDS)
        if group == 1:
            source()
        else:
            half_out[...] = state[...]
        update(group, half_out, state, wr, inv_out, v, 0.5 * time_step, None, acc_out,
               time_step / 6.0)
        finish_stage(
            group, (les_mat, ape_mat)[group], v, w, flow, g, wr_out, up_out, down_out
        )

    each_group(ids, body)


def later_kernel(
    step, ids, from_below, from_above, state, half, w, inv, flow, les_mat, ape_mat, wr_in, acc_in,
    wr_out, acc_out, up_out, down_out, g, wr, v,
):
    def body(group):
        wr[...] = wr_in[...]
        add_planes(wr, POINTS[group] - 1, from_below, from_above, FIELDS)
        update(group, half, state, wr, inv, v, step, acc_in, acc_out, time_step / 3.0)
        finish_stage(
            group, (les_mat, ape_mat)[group], v, w, flow, g, wr_out, up_out, down_out
        )

    each_group(ids, body)


def last_kernel(ids, from_below, from_above, inv, wr_in, acc_in, out, wr):
    def body(group):
        points = POINTS[group]
        size = points * NP
        wr[...] = wr_in[...]
        add_planes(wr, points - 1, from_below, from_above, FIELDS)
        keep = lax.broadcasted_iota(jnp.int32, (size, 2 * LAYER), 0) % NP < points
        for k in range(NP):
            for f in range(FIELDS):
                at = f * NODES + k * PLANE
                done = 0
                if k < points:
                    scale = get_layers(inv, 1, k * PLANE, size) * (time_step / 6.0)
                    rate = get_layers(wr, FIELDS, at, size) * scale
                    value = acc_in[span(at, size), :] + rate
                    if points < NP:
                        value = jnp.where(keep, value, 0.0)
                    out[span(at, size), :] = value
                    done = size
                if done < PLANE:
                    out[span(at + done, PLANE - done), :] = jnp.zeros(
                        (PLANE - done, 2 * LAYER), f32
                    )

    each_group(ids, body)


SMEM = pl.BlockSpec(memory_space=pltpu.SMEM)
VMEM = pl.BlockSpec(memory_space=pltpu.VMEM)


def call(kernel, args, outs, scratch, megabytes=24):
    return pl.pallas_call(
        kernel,
        out_shape=[jax.ShapeDtypeStruct(s, f32) for s in outs],
        in_specs=[SMEM] + [VMEM] * (len(args) - 1),
        out_specs=[VMEM] * len(outs),
        scratch_shapes=[pltpu.VMEM(s, f32) for s in scratch],
        compiler_params=pltpu.CompilerParams(vmem_limit_bytes=megabytes * 1024 * 1024),
    )(*args)


def on_device(state, mean_flow, jacobian, send_elem, recv_elem, recv_count):
    ids = lax.axis_index("grp").astype(jnp.int32).reshape(1)
    width = state.shape[-1]
    peers, cap = send_elem.shape[1:]
    state = state.reshape(FIELDS * NODES, width)
    flow = mean_flow.reshape(3 * NODES, width)
    jac = jacobian.reshape(NODES, width)
    send = jnp.swapaxes(send_elem, 1, 2).reshape(cap, peers)
    recv = jnp.swapaxes(recv_elem, 1, 2).reshape(cap, peers)
    les_mat, ape_mat = (jnp.asarray(m) for m in CONSTS["mats"])
    interp = jnp.asarray(CONSTS["interp"])
    place = jnp.asarray(CONSTS["place"])
    place_edge = jnp.asarray(CONSTS["place_edge"])
    full = (FIELDS * NODES, width)
    one = (NODES, width)
    layered = (2 * FIELDS * NODES, LAYER)
    one_layered = (2 * NODES, LAYER)
    thin = (FIELDS * PLANE, LAYER)
    thick = ((FIELDS + 1) * PLANE + NP, LAYER)
    grads = (2, FIELDS, 2 * PLANE, width)
    size = lax.axis_size("elem")
    up_pairs = [(i, (i + 1) % size) for i in range(size)]
    down_pairs = [(j, i) for i, j in up_pairs]

    def exchange(up_planes, down_planes):
        return (
            lax.ppermute(up_planes, "elem", up_pairs),
            lax.ppermute(down_planes, "elem", down_pairs),
        )

    lamb, wr, w, qw, up_planes, down_planes = call(
        first_kernel,
        (ids, state, jac, flow, les_mat, ape_mat, recv, recv_count),
        [(3 * NODES, width), layered, one, one_layered, thick, thick],
        [grads],
    )
    from_below, from_above = exchange(up_planes, down_planes)
    (block,) = call(
        block_kernel,
        (ids, lamb, interp, send),
        [(TILES * cap * peers, LAYER)],
        [(BLOCK, width)],
    )
    block = lax.all_to_all(block, "elem", split_axis=0, concat_axis=0, tiled=True)
    block = lax.ppermute(block, "grp", [(0, 1)])
    wr, inv, acc, half, up_planes, down_planes = call(
        second_kernel,
        (ids, block, recv, recv_count, from_below, from_above, state, w, qw, flow, les_mat,
         ape_mat, place, place_edge, wr),
        [layered, one_layered, full, full, thin, thin],
        [grads, layered, full, (6 * NODES, LAYER), (6 * PLANE, LAYER)],
    )
    for step in (0.5 * time_step, time_step):
        from_below, from_above = exchange(up_planes, down_planes)

        def kernel(*refs, step=step):
            later_kernel(step, *refs)

        wr, acc, up_planes, down_planes = call(
            kernel,
            (ids, from_below, from_above, state, half, w, inv, flow, les_mat, ape_mat, wr, acc),
            [layered, full, thin, thin],
            [grads, layered, full],
        )
    from_below, from_above = exchange(up_planes, down_planes)
    (out,) = call(
        last_kernel,
        (ids, from_below, from_above, inv, wr, acc),
        [full],
        [layered],
    )
    return out.reshape(1, FIELDS, NODES, width)


def solution(mesh):
    placed = (
        P("grp", None, None, "elem"),
        P(None, None, "elem"),
        P("grp", None, "elem"),
        P("elem", None, None),
        P("elem", None, None),
        P("elem", None),
    )
    return jax.shard_map(
        on_device,
        mesh=mesh,
        in_specs=placed,
        out_specs=P("grp", None, None, "elem"),
        check_vma=False,
    )
```

time: 140 us -> 95.7 us (0.68)
  Pallas kernels: 61.6 us -> 18.5 us
  blocking collectives: 27.5 us -> 25.9 us
    pallas_call x5 -> x6, Pallas kernels: 61.6 us -> 18.5 us  [call(): pl.pallas_call(kernel, out_shape=[jax.ShapeDtypeStruct(s, f32) for s in o...]
    all_to_all x1, blocking collectives: 27.5 us -> 25.9 us  [on_device(): lax.all_to_all(block, 'elem', split_axis=0, concat_axis=0, tiled=True)]
    unnamed x22 -> x32, local copies, waits for them, and re-layouts: 5.61 us -> 7.07 us
where the time goes in v1:
time: 95.7 us; the launch traced here: 95.3 us
  starting transfers between devices  31.8 us (33%)
  blocking collectives  25.9 us (27%)
  Pallas kernels  18.5 us (19%)
  waiting for transfers between devices  12 us (13%)
  local copies, waits for them, and re-layouts  7.07 us (7%)
    ppermute x4, starting transfers between devices, exchange(): lax.ppermute(down_planes, 'elem', down_pairs)  29.5 us
    all_to_all x1, blocking collectives, on_device(): lax.all_to_all(block, 'elem', split_axis=0, concat_axis=0, tiled=True)  25.9 us
    pallas_call x6, Pallas kernels, call(): pl.pallas_call(kernel, out_shape=[jax.ShapeDtypeStruct(s, f32) for s in o...  18.5 us
    ppermute x4, waiting for transfers between devices, exchange(): lax.ppermute(up_planes, 'elem', up_pairs)  11.9 us
    unnamed x32, local copies, waits for them, and re-layouts  7.07 us
  transfers between devices with their start and end apart: 9, of which 4 were waited for; matrix products, arithmetic and copies ran while one was open for 0% of the time, Pallas kernels for 0%

profile of v1, /device:TPU:0, one launch (start us, length us, event | category | flops | bytes accessed | tf_op | source)
XLA Modules:
  0.0 95.3 jit_solution(8602544988909404790)
XLA Ops:
  0.0 1.6 %copy-done = f32[1,4,512,256]{3,2,1,0:T(8,128)S(1)} copy-done((f32[1,4,512,256]{3,2,1,0:T(8,128)S(1)}, f32[1,4,512,256]{3,2,1,0:T(8,128)}, u32[]{:S(2)}) %copy-start) | copy-done | bytes 2097176
  1.6 1.4 %copy-done.2 = f32[3,512,256]{2,1,0:T(8,128)S(1)} copy-done((f32[3,512,256]{2,1,0:T(8,128)S(1)}, f32[3,512,256]{2,1,0:T(8,128)}, u32[]{:S(2)}) %copy-start.2) | copy-done | bytes 1572888
  3.0 0.8 copy-done.4
  3.8 0.8 copy-done.6
  4.6 1.0 %copy-done.9 = f32[1,512,256]{2,1,0:T(8,128)S(1)} copy-done((f32[1,512,256]{2,1,0:T(8,128)S(1)}, f32[1,512,256]{2,1,0:T(8,128)}, u32[]{:S(2)}) %copy-start.9) | copy-done | bytes 524312
  5.7 0.7 copy-done.12
  6.4 0.7 copy-done.15
  7.0 3.3 %shard_map.109 = (f32[1536,256]{1,0:T(8,128)S(1)}, f32[4096,128]{1,0:T(8,128)S(1)}, f32[512,256]{1,0:T(8,128)S(1)}, f32[1024,128]{1,0:T(8,128)S(1)}, f32[328,128]{1,0:T(8,128)S(1)}, /*index=5*/f32[328,128]{1,0:T(8,128)S(1)}) custom-call(s32[1]{0:T(128)} %bitcast.ids.refs_0_, f32[2048,256]{1,0:T(8,128)S(1)} %bitcast.13, f32[512,256]{1,0:T(8,128)S(1)} %bitcast.22, ...), custom_call_target="tpu_custom_call" | custom-call | tf_op jit(solution)/shard_map/pallas_call | solution.py:489
  10.4 0.0 copy-start.1
  10.4 0.0 copy-start.5
  10.4 0.0 copy-start.7
  10.4 0.0 copy-start.10
  10.4 0.0 copy-start.11
  10.4 2.7 %shard_map.110 = f32[2048,128]{1,0:T(8,128)S(1)} custom-call(s32[1]{0:T(128)} %bitcast.ids.refs_0_, f32[1536,256]{1,0:T(8,128)S(1)} %get-tuple-element.25.lamb, bf16[2,296,512]{2,1,0:T(8,128)(2,1)S(1)} %copy-done.8, s32[4,64]{1,0:T(4,128)S(1)} %bitcast.25), custom_call_target="tpu_custom_call" | custom-call | tf_op jit(solution)/shard_map/pallas_call | solution.py:489
  13.1 25.9 %all_to_all.12 = f32[64,32,128]{2,1,0:T(8,128)S(1)} all-to-all(f32[64,32,128]{2,1,0:T(8,128)S(1)} %bitcast.21), channel_id=1, replica_groups=mesh['grp'=2,'elem'=64] {'elem'}, dimensions={0} | all-to-all | bytes 2097152 | tf_op jit(solution)/shard_map/all_to_all | solution.py:542
  39.0 1.3 %collective-permute-start = (f32[2048,128]{1,0:T(8,128)S(1)}, f32[2048,128]{1,0:T(8,128)S(1)}, u32[]{:S(2)}, u32[]{:S(2)}) collective-permute-start(f32[2048,128]{1,0:T(8,128)S(1)} %bitcast.26), channel_id=1, source_target_pairs={{0,64},{1,65},{2,66},{3,67},{4,68},{5,69},{6,70},{7,71},{8,72},{9,... | collective-permute-start | bytes 3145736 | tf_op jit(solution)/shard_map/ppermute | solution.py:543
  40.3 0.8 collective-permute-start.1
  41.1 6.8 %collective-permute-start.2 = (f32[328,128]{1,0:T(8,128)S(1)}, f32[328,128]{1,0:T(8,128)S(1)}, u32[]{:S(2)}, u32[]{:S(2)}) collective-permute-start(f32[328,128]{1,0:T(8,128)S(1)} %get-tuple-element.27), channel_id=1, source_target_pairs={{1,0},{2,1},{3,2},{4,3},{5,4},{6,5},{7,6},{8,7},{9,8},{10,9},{11,1... | collective-permute-start | bytes 503816 | tf_op jit(solution)/shard_map/ppermute | solution.py:526
  47.8 3.3 %collective-permute-done.1.from_below = f32[328,128]{1,0:T(8,128)S(1)} collective-permute-done((f32[328,128]{1,0:T(8,128)S(1)}, f32[328,128]{1,0:T(8,128)S(1)}, u32[]{:S(2)}, u32[]{:S(2)}) %collective-permute-start.1) | collective-permute-done | bytes 167968 | tf_op jit(solution)/shard_map/ppermute | solution.py:525
  51.2 3.8 %shard_map.111 = (f32[4096,128]{1,0:T(8,128)S(1)}, f32[1024,128]{1,0:T(8,128)S(1)}, f32[2048,256]{1,0:T(8,128)S(1)}, f32[2048,256]{1,0:T(8,128)S(1)}, f32[256,128]{1,0:T(8,128)S(1)}, /*index=5*/f32[256,128]{1,0:T(8,128)S(1)}) custom-call(s32[1]{0:T(128)} %bitcast.ids.refs_0_, f32[2048,128]{1,0:T(8,128)S(1)} %collective-permute-done.block, ...), custom_call_target="tpu_custom_call" | custom-call | tf_op jit(solution)/shard_map/pallas_call | solution.py:489
  55.1 0.1 collective-permute-start.3
  55.2 7.5 %collective-permute-start.4 = (f32[256,128]{1,0:T(8,128)S(1)}, f32[256,128]{1,0:T(8,128)S(1)}, u32[]{:S(2)}, u32[]{:S(2)}) collective-permute-start(f32[256,128]{1,0:T(8,128)S(1)} %get-tuple-element.32), channel_id=1, source_target_pairs={{1,0},{2,1},{3,2},{4,3},{5,4},{6,5},{7,6},{8,7},{9,8},{10,9},{11,1... | collective-permute-start | bytes 393224 | tf_op jit(solution)/shard_map/ppermute | solution.py:526
  62.7 2.9 %collective-permute-done.3.refs_1_ = f32[256,128]{1,0:T(8,128)S(1)} collective-permute-done((f32[256,128]{1,0:T(8,128)S(1)}, f32[256,128]{1,0:T(8,128)S(1)}, u32[]{:S(2)}, u32[]{:S(2)}) %collective-permute-start.3) | collective-permute-done | bytes 131104 | tf_op jit(solution)/shard_map/ppermute | solution.py:525
  65.5 3.4 %shard_map.112 = (f32[4096,128]{1,0:T(8,128)S(1)}, f32[2048,256]{1,0:T(8,128)S(1)}, f32[256,128]{1,0:T(8,128)S(1)}, f32[256,128]{1,0:T(8,128)S(1)}) custom-call(s32[1]{0:T(128)} %bitcast.ids.refs_0_, f32[256,128]{1,0:T(8,128)S(1)} %collective-permute-done.3.refs_1_, f32[256,128]{1,0:T(8,128)S(1)} %collective-permute-done.4.refs_2_, ...), custom_call_target="tpu_custom_call" | custom-call | tf_op jit(solution)/shard_map/pallas_call | solution.py:489
  68.9 0.1 collective-permute-start.5
  69.0 7.6 %collective-permute-start.6 = (f32[256,128]{1,0:T(8,128)S(1)}, f32[256,128]{1,0:T(8,128)S(1)}, u32[]{:S(2)}, u32[]{:S(2)}) collective-permute-start(f32[256,128]{1,0:T(8,128)S(1)} %get-tuple-element.38), channel_id=1, source_target_pairs={{1,0},{2,1},{3,2},{4,3},{5,4},{6,5},{7,6},{8,7},{9,8},{10,9},{11,1... | collective-permute-start | bytes 393224 | tf_op jit(solution)/shard_map/ppermute | solution.py:526
  76.6 2.9 %collective-permute-done.5.refs_1_ = f32[256,128]{1,0:T(8,128)S(1)} collective-permute-done((f32[256,128]{1,0:T(8,128)S(1)}, f32[256,128]{1,0:T(8,128)S(1)}, u32[]{:S(2)}, u32[]{:S(2)}) %collective-permute-start.5) | collective-permute-done | bytes 131104 | tf_op jit(solution)/shard_map/ppermute | solution.py:525
  79.4 3.6 %shard_map.113 = (f32[4096,128]{1,0:T(8,128)S(1)}, f32[2048,256]{1,0:T(8,128)S(1)}, f32[256,128]{1,0:T(8,128)S(1)}, f32[256,128]{1,0:T(8,128)S(1)}) custom-call(s32[1]{0:T(128)} %bitcast.ids.refs_0_, f32[256,128]{1,0:T(8,128)S(1)} %collective-permute-done.5.refs_1_, f32[256,128]{1,0:T(8,128)S(1)} %collective-permute-done.6.refs_2_, ...), custom_call_target="tpu_custom_call" | custom-call | tf_op jit(solution)/shard_map/pallas_call | solution.py:489
  83.1 0.1 collective-permute-start.7
  83.1 7.6 %collective-permute-start.8 = (f32[256,128]{1,0:T(8,128)S(1)}, f32[256,128]{1,0:T(8,128)S(1)}, u32[]{:S(2)}, u32[]{:S(2)}) collective-permute-start(f32[256,128]{1,0:T(8,128)S(1)} %get-tuple-element.42), channel_id=1, source_target_pairs={{1,0},{2,1},{3,2},{4,3},{5,4},{6,5},{7,6},{8,7},{9,8},{10,9},{11,1... | collective-permute-start | bytes 393224 | tf_op jit(solution)/shard_map/ppermute | solution.py:526
  90.7 2.9 %collective-permute-done.7.from_below = f32[256,128]{1,0:T(8,128)S(1)} collective-permute-done((f32[256,128]{1,0:T(8,128)S(1)}, f32[256,128]{1,0:T(8,128)S(1)}, u32[]{:S(2)}, u32[]{:S(2)}) %collective-permute-start.7) | collective-permute-done | bytes 131104 | tf_op jit(solution)/shard_map/ppermute | solution.py:525
  93.6 1.7 %shard_map.114 = f32[2048,256]{1,0:T(8,128)} custom-call(s32[1]{0:T(128)} %bitcast.ids.refs_0_, f32[256,128]{1,0:T(8,128)S(1)} %collective-permute-done.7.from_below, f32[256,128]{1,0:T(8,128)S(1)} %collective-permute-done.8.from_above, f32[1024,128]{1,0:T(8,128)S(1)} %get-tuple-element.34.refs_6_.inv, f32[4096,128]{1,0:T(8,128)S(1)} %get-tuple-element.43.wr_in, ...), custom_call_target="tpu_custom_call" | custom-call | tf_op jit(solution)/shard_map/pallas_call | solution.py:489
  (25 shorter events, 0.1 us)
Async XLA Ops:
  0.0 1.6 %copy-start = (f32[1,4,512,256]{3,2,1,0:T(8,128)S(1)}, f32[1,4,512,256]{3,2,1,0:T(8,128)}, u32[]{:S(2)}) copy-start(f32[1,4,512,256]{3,2,1,0:T(8,128)} %param.11) | copy-start | bytes 6291460
  1.6 1.4 %copy-start.2 = (f32[3,512,256]{2,1,0:T(8,128)S(1)}, f32[3,512,256]{2,1,0:T(8,128)}, u32[]{:S(2)}) copy-start(f32[3,512,256]{2,1,0:T(8,128)} %param.12) | copy-start | bytes 4718596
  3.0 0.8 copy-start.4
  3.8 0.8 copy-start.6
  4.6 1.0 %copy-start.9 = (f32[1,512,256]{2,1,0:T(8,128)S(1)}, f32[1,512,256]{2,1,0:T(8,128)}, u32[]{:S(2)}) copy-start(f32[1,512,256]{2,1,0:T(8,128)} %param.13) | copy-start | bytes 1572868
  5.7 0.7 copy-start.12
  6.4 0.7 copy-start.15
  7.0 3.3 %copy-start.8 = (bf16[2,296,512]{2,1,0:T(8,128)(2,1)S(1)}, bf16[2,296,512]{2,1,0:T(8,128)(2,1)}, u32[]{:S(2)}) copy-start(bf16[2,296,512]{2,1,0:T(8,128)(2,1)} %constant.18.clone.interp) | copy-start | bytes 1818628
  7.0 3.3 %copy-start.14 = (s32[1,64,4]{1,2,0:T(4,128)S(1)}, s32[1,64,4]{1,2,0:T(4,128)}, u32[]{:S(2)}) copy-start(s32[1,64,4]{1,2,0:T(4,128)} %param.14) | copy-start | bytes 3076
  10.4 40.8 %copy-start.1 = (f32[1,4,512,256]{3,2,1,0:T(8,128)S(1)}, f32[1,4,512,256]{3,2,1,0:T(8,128)}, u32[]{:S(2)}) copy-start(f32[1,4,512,256]{3,2,1,0:T(8,128)} %param.11) | copy-start | bytes 6291460
  10.4 40.8 %copy-start.3 = (f32[3,512,256]{2,1,0:T(8,128)S(1)}, f32[3,512,256]{2,1,0:T(8,128)}, u32[]{:S(2)}) copy-start(f32[3,512,256]{2,1,0:T(8,128)} %param.12) | copy-start | bytes 4718596
  10.4 40.8 %copy-start.5 = (bf16[128,192]{1,0:T(8,128)(2,1)S(1)}, bf16[128,192]{1,0:T(8,128)(2,1)}, u32[]{:S(2)}) copy-start(bf16[128,192]{1,0:T(8,128)(2,1)} %constant.16.clone.les_mat.refs_8_) | copy-start | bytes 147460
  10.4 40.8 %copy-start.7 = (bf16[96,144]{1,0:T(8,128)(2,1)S(1)}, bf16[96,144]{1,0:T(8,128)(2,1)}, u32[]{:S(2)}) copy-start(bf16[96,144]{1,0:T(8,128)(2,1)} %constant.17.clone.ape_mat.refs_9_) | copy-start | bytes 82948
  10.4 40.8 %copy-start.10 = (bf16[384,432]{1,0:T(8,128)(2,1)S(1)}, bf16[384,432]{1,0:T(8,128)(2,1)}, u32[]{:S(2)}) copy-start(bf16[384,432]{1,0:T(8,128)(2,1)} %constant.19.clone.place) | copy-start | bytes 995332
  10.4 40.8 %copy-start.11 = (bf16[64,80]{1,0:T(8,128)(2,1)S(1)}, bf16[64,80]{1,0:T(8,128)(2,1)}, u32[]{:S(2)}) copy-start(bf16[64,80]{1,0:T(8,128)(2,1)} %constant.20.clone.place_edge) | copy-start | bytes 30724
  10.4 40.8 %copy-start.13 = (s32[1,64,4]{1,2,0:T(4,128)S(1)}, s32[1,64,4]{1,2,0:T(4,128)}, u32[]{:S(2)}) copy-start(s32[1,64,4]{1,2,0:T(4,128)} %param.15) | copy-start | bytes 3076
  39.0 12.2 %collective-permute-start = (f32[2048,128]{1,0:T(8,128)S(1)}, f32[2048,128]{1,0:T(8,128)S(1)}, u32[]{:S(2)}, u32[]{:S(2)}) collective-permute-start(f32[2048,128]{1,0:T(8,128)S(1)} %bitcast.26), channel_id=1, source_target_pairs={{0,64},{1,65},{2,66},{3,67},{4,68},{5,69},{6,70},{7,71},{8,72},{9,... | collective-permute-start | bytes 3145736 | tf_op jit(solution)/shard_map/ppermute | solution.py:543
  40.3 10.9 %collective-permute-start.1 = (f32[328,128]{1,0:T(8,128)S(1)}, f32[328,128]{1,0:T(8,128)S(1)}, u32[]{:S(2)}, u32[]{:S(2)}) collective-permute-start(f32[328,128]{1,0:T(8,128)S(1)} %get-tuple-element.26), channel_id=1, source_target_pairs={{0,1},{1,2},{2,3},{3,4},{4,5},{5,6},{6,7},{7,8},{8,9},{9,10},{10,1... | collective-permute-start | bytes 503816 | tf_op jit(solution)/shard_map/ppermute | solution.py:525
  41.1 10.1 %collective-permute-start.2 = (f32[328,128]{1,0:T(8,128)S(1)}, f32[328,128]{1,0:T(8,128)S(1)}, u32[]{:S(2)}, u32[]{:S(2)}) collective-permute-start(f32[328,128]{1,0:T(8,128)S(1)} %get-tuple-element.27), channel_id=1, source_target_pairs={{1,0},{2,1},{3,2},{4,3},{5,4},{6,5},{7,6},{8,7},{9,8},{10,9},{11,1... | collective-permute-start | bytes 503816 | tf_op jit(solution)/shard_map/ppermute | solution.py:526
  55.1 10.5 %collective-permute-start.3 = (f32[256,128]{1,0:T(8,128)S(1)}, f32[256,128]{1,0:T(8,128)S(1)}, u32[]{:S(2)}, u32[]{:S(2)}) collective-permute-start(f32[256,128]{1,0:T(8,128)S(1)} %get-tuple-element.31), channel_id=1, source_target_pairs={{0,1},{1,2},{2,3},{3,4},{4,5},{5,6},{6,7},{7,8},{8,9},{9,10},{10,1... | collective-permute-start | bytes 393224 | tf_op jit(solution)/shard_map/ppermute | solution.py:525
  55.2 10.4 %collective-permute-start.4 = (f32[256,128]{1,0:T(8,128)S(1)}, f32[256,128]{1,0:T(8,128)S(1)}, u32[]{:S(2)}, u32[]{:S(2)}) collective-permute-start(f32[256,128]{1,0:T(8,128)S(1)} %get-tuple-element.32), channel_id=1, source_target_pairs={{1,0},{2,1},{3,2},{4,3},{5,4},{6,5},{7,6},{8,7},{9,8},{10,9},{11,1... | collective-permute-start | bytes 393224 | tf_op jit(solution)/shard_map/ppermute | solution.py:526
  68.9 10.5 %collective-permute-start.5 = (f32[256,128]{1,0:T(8,128)S(1)}, f32[256,128]{1,0:T(8,128)S(1)}, u32[]{:S(2)}, u32[]{:S(2)}) collective-permute-start(f32[256,128]{1,0:T(8,128)S(1)} %get-tuple-element.37), channel_id=1, source_target_pairs={{0,1},{1,2},{2,3},{3,4},{4,5},{5,6},{6,7},{7,8},{8,9},{9,10},{10,1... | collective-permute-start | bytes 393224 | tf_op jit(solution)/shard_map/ppermute | solution.py:525
  69.0 10.5 %collective-permute-start.6 = (f32[256,128]{1,0:T(8,128)S(1)}, f32[256,128]{1,0:T(8,128)S(1)}, u32[]{:S(2)}, u32[]{:S(2)}) collective-permute-start(f32[256,128]{1,0:T(8,128)S(1)} %get-tuple-element.38), channel_id=1, source_target_pairs={{1,0},{2,1},{3,2},{4,3},{5,4},{6,5},{7,6},{8,7},{9,8},{10,9},{11,1... | collective-permute-start | bytes 393224 | tf_op jit(solution)/shard_map/ppermute | solution.py:526
  83.1 10.5 %collective-permute-start.7 = (f32[256,128]{1,0:T(8,128)S(1)}, f32[256,128]{1,0:T(8,128)S(1)}, u32[]{:S(2)}, u32[]{:S(2)}) collective-permute-start(f32[256,128]{1,0:T(8,128)S(1)} %get-tuple-element.41), channel_id=1, source_target_pairs={{0,1},{1,2},{2,3},{3,4},{4,5},{5,6},{6,7},{7,8},{8,9},{9,10},{10,1... | collective-permute-start | bytes 393224 | tf_op jit(solution)/shard_map/ppermute | solution.py:525
  83.1 10.5 %collective-permute-start.8 = (f32[256,128]{1,0:T(8,128)S(1)}, f32[256,128]{1,0:T(8,128)S(1)}, u32[]{:S(2)}, u32[]{:S(2)}) collective-permute-start(f32[256,128]{1,0:T(8,128)S(1)} %get-tuple-element.42), channel_id=1, source_target_pairs={{1,0},{2,1},{3,2},{4,3},{5,4},{6,5},{7,6},{8,7},{9,8},{10,9},{11,1... | collective-permute-start | bytes 393224 | tf_op jit(solution)/shard_map/ppermute | solution.py:526

commit v2 on v1

--- a/solution.py
+++ b/solution.py
@@ -187,16 +187,16 @@
     )
 
 
-def z_derivative(d, k, points, v, f, j):
+def z_derivative(d, k, planes, v, f, j, lanes=slice(None)):
     total = None
-    for q in range(points):
+    for q in planes:
         if d[k, q] != 0.0:
-            part = float(d[k, q]) * v[span(f * NODES + q * PLANE + j * NP), :]
+            part = float(d[k, q]) * v[span(f * NODES + q * PLANE + j * NP), lanes]
             total = part if total is None else total + part
     return total
 
 
-def raw_stage(group, mat, v, w, flow, g, wr, lamb=None):
+def raw_stage(group, mat, v, w, flow, g, wr):
     points = POINTS[group]
     d = CONSTS["derivs"][group]
     size = points * NP
@@ -209,7 +209,7 @@
             at = base + j * NP
             gx = [g[k % 2, f, span(j * NP), :] for f in range(FIELDS)]
             gy = [g[k % 2, f, span(size + j * NP), :] for f in range(FIELDS)]
-            gz = [z_derivative(d, k, points, v, f, j) for f in range(FIELDS)]
+            gz = [z_derivative(d, k, range(points), v, f, j) for f in range(FIELDS)]
             u = [v[span(m * NODES + at), :] for m in range(3)]
             a = u if group == 0 else [flow[span(m * NODES + at), :] for m in range(3)]
             carried = [a[0] * gx[f] + a[1] * gy[f] + a[2] * gz[f] for f in range(FIELDS)]
@@ -219,95 +219,198 @@
                 put_layers(wr, FIELDS, m * NODES + at, weight * (carried[m] + press[m]))
             total = weight * (carried[3] + SPEEDS[group] * (gx[0] + gy[1] + gz[2]))
             put_layers(wr, FIELDS, 3 * NODES + at, total)
-            if lamb is not None:
-                vx = gy[2] - gz[1]
+
+
+def edge_lanes(ref, row, up, size=NP):
+    return jnp.concatenate(
+        [ref[span(row, size), :LAYER], ref[span(row + up * PLANE, size), LAYER:]], axis=1
+    )
+
+
+def get_edges(ref, row, size=NP):
+    return jnp.concatenate(
+        [ref[span(row, size), :], ref[span(FIELDS * PLANE + row, size), :]], axis=1
+    )
+
+
+def put_edges(ref, row, value):
+    size = value.shape[0]
+    ref[span(row, size), :] = value[:, :LAYER]
+    ref[span(FIELDS * PLANE + row, size), :] = value[:, LAYER:]
+
+
+def edge_stage(group, mat, v, vb, w, flow, g, up_out, down_out):
+    points = POINTS[group]
+    up = points - 1
+    d = CONSTS["derivs"][group]
+    size = points * NP
+    for f in range(FIELDS):
+        high, low = split(get_edges(vb, f * PLANE, size))
+        g[f, : 2 * size, :] = dot(mat[...], jnp.concatenate([high, low, high], axis=0))
+    for j in range(points):
+        u = [get_edges(vb, f * PLANE + j * NP) for f in range(FIELDS)]
+        gx = [g[f, span(j * NP), :] for f in range(FIELDS)]
+        gy = [g[f, span(size + j * NP), :] for f in range(FIELDS)]
+        gz = []
+        for f in range(FIELDS):
+            low = z_derivative(d, 0, range(1, points), v, f, j, slice(0, LAYER))
+            high = z_derivative(d, up, range(up), v, f, j, slice(LAYER, 2 * LAYER))
+            low = low + float(d[0, 0]) * u[f][:, :LAYER]
+            high = high + float(d[up, up]) * u[f][:, LAYER:]
+            gz.append(jnp.concatenate([low, high], axis=1))
+        a = u if group == 0 else [edge_lanes(flow, m * NODES + j * NP, up) for m in range(3)]
+        weight = -edge_lanes(w, j * NP, up)
+        carried = [a[0] * gx[f] + a[1] * gy[f] + a[2] * gz[f] for f in range(FIELDS)]
+        press = (gx[3], gy[3], gz[3])
+        values = [weight * (carried[m] + press[m]) for m in range(3)]
+        values.append(weight * (carried[3] + SPEEDS[group] * (gx[0] + gy[1] + gz[2])))
+        for f in range(FIELDS):
+            down_out[span(f * PLANE + j * NP), :] = values[f][:, :LAYER]
+            up_out[span(f * PLANE + j * NP), :] = values[f][:, LAYER:]
+    masks = lane_masks()
+    sum_in_plane(up_out, FIELDS, up, masks)
+    sum_in_plane(down_out, FIELDS, up, masks)
+
+
+def take_edges(group, ref, out):
+    for f in range(FIELDS):
+        put_edges(out, f * PLANE, edge_lanes(ref, f * NODES, POINTS[group] - 1, PLANE))
+
+
+def inner_stage(group, mat, v, w, flow, g, wr):
+    up = POINTS[group] - 1
+    raw_stage(group, mat, v, w, flow, g, wr)
+    sum_in_plane(wr, 2 * FIELDS * NP, up, lane_masks())
+    sum_inner(wr, FIELDS, up)
+
+
+def each_group(ids, body):
+    for group in range(2):
+        pl.when(ids[0] == group)(lambda group=group: body(group))
+
+
+def columns(row_table):
+    cap, peers = row_table.shape
+    tile = jnp.concatenate([row_table, jnp.zeros((cap, LAYER - peers), f32)], axis=1)
+    tile = jnp.concatenate([tile, jnp.zeros((NP - cap, LAYER), f32)], axis=0)
+    return jnp.transpose(tile)[:peers, :]
+
+
+def targets(recv, count):
+    slot = lax.broadcasted_iota(jnp.int32, recv.shape, 0)
+    return jnp.where(slot < count[...], recv[...], -1).astype(f32)
+
+
+def weights(group, jac, planes):
+    wts = np.ones(NP)
+    wts[: POINTS[group]] = CONSTS["weights"][group]
+    sub = lax.broadcasted_iota(jnp.int32, (NP, 2 * LAYER), 0)
+    wi = jnp.zeros((NP, 2 * LAYER), f32)
+    for i in range(NP):
+        wi = jnp.where(sub == i, float(wts[i]), wi)
+    for k in planes:
+        for j in range(NP):
+            at = k * PLANE + j * NP
+            yield k, j, at, (wi * float(wts[k] * wts[j])) * jac[span(at), :]
+
+
+def first_kernel(
+    ids, state, jac, flow, les_mat, ape_mat,
+    wr_out, w_out, qw_out, g,
+):
+    def body(group):
+        up = POINTS[group] - 1
+        for k, j, at, value in weights(group, jac, range(NP)):
+            w_out[span(at), :] = value
+            put_layers(qw_out, 1, at, value)
+        inner_stage(group, (les_mat, ape_mat)[group], state, w_out, flow, g, wr_out)
+        sum_in_plane(qw_out, 2 * NP, up, lane_masks())
+        sum_inner(qw_out, 1, up)
+
+    each_group(ids, body)
+
+
+def edge_kernel(
+    ids, state, jac_at, flow_at, les_at, ape_at, recv, count,
+    up_out, down_out,
+    v, jac, flow, les_mat, ape_mat, g, w, vb, sems,
+):
+    cap, peers = recv.shape
+    sources = (state, jac_at, (les_at, ape_at), flow_at)
+    places = (v, jac, (les_mat, ape_mat), flow)
+
+    def body(group):
+        copies = []
+        for n in range(4 if group == 1 else 3):
+            pick = (lambda x: x[group]) if n == 2 else (lambda x: x)
+            copies.append(pltpu.make_async_copy(pick(sources[n]), pick(places[n]), sems.at[n]))
+        for copy in copies:
+            copy.start()
+        at = span((FIELDS + 1) * PLANE, NP)
+        up_out[at, :] = jnp.zeros((NP, LAYER), f32)
+        down_out[at, :] = jnp.zeros((NP, LAYER), f32)
+        at = span((FIELDS + 1) * PLANE, cap)
+        target = targets(recv, count)
+        up_out[at, 0:peers] = target
+        down_out[at, 0:peers] = target
+        for copy in copies:
+            copy.wait()
+        up = POINTS[group] - 1
+        for k, j, at, value in weights(group, jac, (0, up)):
+            w[span(at), :] = value
+        take_edges(group, v, vb)
+        edge_stage(group, (les_mat, ape_mat)[group], v, vb, w, flow, g, up_out, down_out)
+        at = span(FIELDS * PLANE, PLANE)
+        up_out[at, :] = w[span(up * PLANE, PLANE), LAYER:]
+        down_out[at, :] = w[span(0, PLANE), :LAYER]
+
+    each_group(ids, body)
+
+
+def block_kernel(
+    ids, state, les_at, interp_at, send_at,
+    block_out,
+    v, les_mat, interp, send, g, lamb, comp, sems,
+):
+    cap, peers = send.shape
+
+    @pl.when(ids[0] == 0)
+    def _():
+        copies = [
+            pltpu.make_async_copy(les_at, les_mat, sems.at[0]),
+            pltpu.make_async_copy(state.at[0 : 3 * NODES, :], v, sems.at[1]),
+            pltpu.make_async_copy(send_at, send, sems.at[2]),
+            pltpu.make_async_copy(interp_at, interp, sems.at[3]),
+        ]
+        for copy in copies:
+            copy.start()
+        comp[3 * COMP : EDGE_LO, :] = jnp.zeros((EDGE_LO - 3 * COMP, 2 * LAYER), f32)
+        comp[EDGE_LO + 3 * EDGE : EDGE_HI, :] = jnp.zeros((8, 2 * LAYER), f32)
+        comp[EDGE_HI + 3 * EDGE : BLOCK, :] = jnp.zeros((8, 2 * LAYER), f32)
+        copies[0].wait()
+        copies[1].wait()
+        d = CONSTS["derivs"][0]
+        for k in range(NP):
+            base = k * PLANE
+            for f in range(3):
+                high, low = split(v[span(f * NODES + base, PLANE), :])
+                stack = jnp.concatenate([high, low, high], axis=0)
+                some = (slice(PLANE, 2 * PLANE), slice(0, PLANE), slice(0, 2 * PLANE))[f]
+                g[k % 2, f, some, :] = dot(les_mat[some, :], stack)
+            for j in range(NP):
+                at = base + j * NP
+                gx = [None] + [g[k % 2, f, span(j * NP), :] for f in (1, 2)]
+                gy = [g[k % 2, f, span(PLANE + j * NP), :] for f in (0, 2)]
+                gz = [z_derivative(d, k, range(NP), v, f, j) for f in (0, 1)]
+                u = [v[span(m * NODES + at), :] for m in range(3)]
+                vx = gy[1] - gz[1]
                 vy = gz[0] - gx[2]
                 vz = gx[1] - gy[0]
                 lamb[span(at), :] = vy * u[2] - vz * u[1]
                 lamb[span(NODES + at), :] = vz * u[0] - vx * u[2]
                 lamb[span(2 * NODES + at), :] = vx * u[1] - vy * u[0]
-
-
-def put_planes(wr, up, up_out, down_out, fields):
-    for f in range(fields):
-        at = span(f * PLANE, PLANE)
-        up_out[at, :] = wr[span((fields + f) * NODES + up * PLANE, PLANE), :]
-        down_out[at, :] = wr[span(f * NODES, PLANE), :]
-
-
-def finish_stage(group, mat, v, w, flow, g, wr, up_out, down_out, lamb=None):
-    up = POINTS[group] - 1
-    raw_stage(group, mat, v, w, flow, g, wr, lamb)
-    sum_in_plane(wr, 2 * FIELDS * NP, up, lane_masks())
-    put_planes(wr, up, up_out, down_out, FIELDS)
-    sum_inner(wr, FIELDS, up)
-
-
-def each_group(ids, body):
-    for group in range(2):
-        pl.when(ids[0] == group)(lambda group=group: body(group))
-
-
-def columns(row_table):
-    cap, peers = row_table.shape
-    tile = jnp.concatenate([row_table, jnp.zeros((cap, LAYER - peers), f32)], axis=1)
-    tile = jnp.concatenate([tile, jnp.zeros((NP - cap, LAYER), f32)], axis=0)
-    return jnp.transpose(tile)[:peers, :]
-
-
-def targets(recv, count):
-    slot = lax.broadcasted_iota(jnp.int32, recv.shape, 0)
-    return jnp.where(slot < count[...], recv[...], -1).astype(f32)
-
-
-def first_kernel(
-    ids, state, jac, flow, les_mat, ape_mat, recv, count,
-    lamb_out, wr_out, w_out, qw_out, up_out, down_out, g,
-):
-    def body(group):
-        up = POINTS[group] - 1
-        points = POINTS[group]
-        wts = np.ones(NP)
-        wts[:points] = CONSTS["weights"][group]
-        sub = lax.broadcasted_iota(jnp.int32, (NP, 2 * LAYER), 0)
-        wi = jnp.zeros((NP, 2 * LAYER), f32)
-        for i in range(NP):
-            wi = jnp.where(sub == i, float(wts[i]), wi)
-        for k in range(NP):
-            for j in range(NP):
-                at = k * PLANE + j * NP
-                value = (wi * float(wts[k] * wts[j])) * jac[span(at), :]
-                w_out[span(at), :] = value
-                put_layers(qw_out, 1, at, value)
-        finish_stage(
-            group, (les_mat, ape_mat)[group], state, w_out, flow, g, wr_out, up_out, down_out,
-            lamb_out if group == 0 else None,
-        )
-        at = span(FIELDS * PLANE, PLANE)
-        up_out[at, :] = w_out[span(up * PLANE, PLANE), LAYER : 2 * LAYER]
-        down_out[at, :] = w_out[0:PLANE, 0:LAYER]
-        sum_in_plane(qw_out, 2 * NP, up, lane_masks())
-        sum_inner(qw_out, 1, up)
-
-    each_group(ids, body)
-    cap, peers = recv.shape
-    at = span((FIELDS + 1) * PLANE, NP)
-    up_out[at, :] = jnp.zeros((NP, LAYER), f32)
-    down_out[at, :] = jnp.zeros((NP, LAYER), f32)
-    at = span((FIELDS + 1) * PLANE, cap)
-    target = targets(recv, count)
-    up_out[at, 0:peers] = target
-    down_out[at, 0:peers] = target
-
-
-def block_kernel(ids, lamb, interp, send, block_out, comp):
-    cap, peers = send.shape
-
-    @pl.when(ids[0] == 0)
-    def _():
-        comp[3 * COMP : EDGE_LO, :] = jnp.zeros((EDGE_LO - 3 * COMP, 2 * LAYER), f32)
-        comp[EDGE_LO + 3 * EDGE : EDGE_HI, :] = jnp.zeros((8, 2 * LAYER), f32)
-        comp[EDGE_HI + 3 * EDGE : BLOCK, :] = jnp.zeros((8, 2 * LAYER), f32)
+        copies[2].wait()
+        copies[3].wait()
         for m in range(3):
             high, low = split(lamb[m * NODES : (m + 1) * NODES, :])
             got = dot(interp[0], high) + dot(interp[0], low) + dot(interp[1], high)
@@ -317,11 +420,12 @@
         elem = lax.broadcasted_iota(jnp.int32, (peers, 2 * LAYER), 1)
         high, low = split(comp[...])
         table = columns(send[...].astype(f32)).astype(jnp.int32)
+        pick = [(table[:, c : c + 1] == elem).astype(f32).astype(bf16) for c in range(cap)]
+        pick = jnp.concatenate(pick, axis=0)
+        got = dot_nt(pick, high) + dot_nt(pick, low)
         for c in range(cap):
-            pick = (table[:, c : c + 1] == elem).astype(f32).astype(bf16)
-            got = dot_nt(pick, high) + dot_nt(pick, low)
             for t in range(TILES):
-                value = got[:, t * LAYER : (t + 1) * LAYER]
+                value = got[span(c * peers, peers), t * LAYER : (t + 1) * LAYER]
                 if t >= TILES - 2:
                     value = pltpu.roll(value, peers - 1 if t == TILES - 2 else 1, 0)
                 block_out[pl.ds(t * cap + c, peers, stride=TILES * cap), :] = value
@@ -344,31 +448,39 @@
     return dot(high, pick) + dot(low, pick)
 
 
-def update(group, half, state, wr, inv, v, step, acc_in, acc_out, share):
+def summed(group, wr, f, k, size, from_below, from_above):
+    at = f * NODES + k * PLANE
+    low = wr[span(at, size), :]
+    high = wr[span(FIELDS * NODES + at, size), :]
+    if from_below is not None and k == 0:
+        low = low + from_below[span(f * PLANE, size), :]
+    if from_above is not None and k == POINTS[group] - 1:
+        high = high + from_above[span(f * PLANE, size), :]
+    return jnp.concatenate([low, high], axis=1)
+
+
+def update(group, half, state, wr, inv, v, step, acc_in, acc_out, share, from_below, from_above):
     points = POINTS[group]
     size = points * NP
     for k in range(points):
         scale = get_layers(inv, 1, k * PLANE, size)
         for f in range(FIELDS):
             at = f * NODES + k * PLANE
-            rate = get_layers(wr, FIELDS, at, size) * scale
+            rate = summed(group, wr, f, k, size, from_below, from_above) * scale
             base = half[span(at, size), :]
-            if state is not None:
-                start = state[span(at, size), :]
+            if acc_in is None or step == time_step:
+                full = base + (base - state[span(at, size), :])
             if step == time_step:
-                base = base + (base - start)
+                base = full
             v[span(at, size), :] = base + step * rate
-            if acc_in is None:
-                before = base + (base - start)
-            else:
-                before = acc_in[span(at, size), :]
+            before = full if acc_in is None else acc_in[span(at, size), :]
             acc_out[span(at, size), :] = before + share * rate
 
 
 def second_kernel(
     ids, block, recv, count, from_below, from_above, state, w, qw, flow, les_mat, ape_mat, place,
     place_edge, wr_in,
-    wr_out, inv_out, acc_out, half_out, up_out, down_out, g, wr, v, src, edge,
+    v, inv_out, acc_out, half_out, acc_edges, up_out, down_out, g, vb, src, edge,
 ):
     cap, peers = recv.shape
     weights_at = span(FIELDS * PLANE, PLANE)
@@ -418,65 +530,130 @@
 
     def body(group):
         up = POINTS[group] - 1
-        wr[...] = wr_in[...]
         inv_out[...] = qw[...]
         edge[0:PLANE, :] = from_below[weights_at, :]
         edge[PLANE : 2 * PLANE, :] = from_above[weights_at, :]
         sum_in_plane(edge, 2, up, lane_masks())
         add_planes(inv_out, up, edge.at[0:PLANE], edge.at[PLANE : 2 * PLANE], 1)
         inv_out[...] = 1.0 / inv_out[...]
-        add_planes(wr, up, from_below, from_above, FIELDS)
         if group == 1:
             source()
         else:
             half_out[...] = state[...]
-        update(group, half_out, state, wr, inv_out, v, 0.5 * time_step, None, acc_out,
-               time_step / 6.0)
-        finish_stage(
-            group, (les_mat, ape_mat)[group], v, w, flow, g, wr_out, up_out, down_out
-        )
+        update(group, half_out, state, wr_in, inv_out, v, 0.5 * time_step, None, acc_out,
+               time_step / 6.0, from_below, from_above)
+        take_edges(group, v, vb)
+        take_edges(group, acc_out, acc_edges)
+        edge_stage(group, (les_mat, ape_mat)[group], v, vb, w, flow, g, up_out, down_out)
 
     each_group(ids, body)
 
 
-def later_kernel(
-    step, ids, from_below, from_above, state, half, w, inv, flow, les_mat, ape_mat, wr_in, acc_in,
-    wr_out, acc_out, up_out, down_out, g, wr, v,
+def edge_rate(group, f, from_below, from_above, down, up_planes, inv):
+    size = POINTS[group] * NP
+    at = span(f * PLANE, size)
+    low = down[at, :] + from_below[at, :]
+    high = up_planes[at, :] + from_above[at, :]
+    low = low * inv[span(0, size), :]
+    high = high * inv[span(NODES + (POINTS[group] - 1) * PLANE, size), :]
+    return jnp.concatenate([low, high], axis=1)
+
+
+def edge_step_kernel(
+    step, ids, from_below, from_above, down, up_planes, v, half, state, w, inv, flow, les_mat,
+    ape_mat, acc_in,
+    vb, acc_edges, up_out, down_out, g,
 ):
     def body(group):
-        wr[...] = wr_in[...]
-        add_planes(wr, POINTS[group] - 1, from_below, from_above, FIELDS)
-        update(group, half, state, wr, inv, v, step, acc_in, acc_out, time_step / 3.0)
-        finish_stage(
-            group, (les_mat, ape_mat)[group], v, w, flow, g, wr_out, up_out, down_out
-        )
+        up = POINTS[group] - 1
+        size = POINTS[group] * NP
+        for f in range(FIELDS):
+            rate = edge_rate(group, f, from_below, from_above, down, up_planes, inv)
+            base = edge_lanes(half, f * NODES, up, size)
+            if step == time_step:
+                base = base + (base - edge_lanes(state, f * NODES, up, size))
+            put_edges(vb, f * PLANE, base + step * rate)
+            before = get_edges(acc_in, f * PLANE, size)
+            put_edges(acc_edges, f * PLANE, before + (time_step / 3.0) * rate)
+        edge_stage(group, (les_mat, ape_mat)[group], v, vb, w, flow, g, up_out, down_out)
 
     each_group(ids, body)
 
 
-def last_kernel(ids, from_below, from_above, inv, wr_in, acc_in, out, wr):
+def inner_kernel(step, ids, v_in, *refs):
+    if step == 0.5 * time_step:
+        half, state, w, inv, flow, les_mat, ape_mat, acc_in, v_out, acc_out, g, wr = refs
+        v = v_in
+    else:
+        vb, half, state, w, inv, flow, les_mat, ape_mat, acc_in = refs[:9]
+        g, wr, v = refs[-3:]
+        v_out, acc_out = (refs[9], refs[10]) if step is not None else (None, refs[9])
+
+    def body(group):
+        if v is not v_in:
+            v[...] = v_in[...]
+            for f in range(FIELDS):
+                size = POINTS[group] * NP
+                up = POINTS[group] - 1
+                value = get_edges(vb, f * PLANE, size)
+                v[span(f * NODES, size), :LAYER] = value[:, :LAYER]
+                v[span(f * NODES + up * PLANE, size), LAYER:] = value[:, LAYER:]
+        inner_stage(group, (les_mat, ape_mat)[group], v, w, flow, g, wr)
+        if step is None:
+            finish(group, wr, inv, acc_in, acc_out)
+        else:
+            update(group, half, state, wr, inv, v_out, step, acc_in, acc_out, time_step / 3.0,
+                   None, None)
+
+    each_group(ids, body)
+
+
+def finish(group, wr, inv, acc_in, out):
+    points = POINTS[group]
+    size = points * NP
+    keep = lax.broadcasted_iota(jnp.int32, (size, 2 * LAYER), 0) % NP < points
+    for k in range(NP):
+        for f in range(FIELDS):
+            at = f * NODES + k * PLANE
+            done = 0
+            if k < points:
+                scale = get_layers(inv, 1, k * PLANE, size) * (time_step / 6.0)
+                rate = summed(group, wr, f, k, size, None, None) * scale
+                value = acc_in[span(at, size), :] + rate
+                if points < NP:
+                    value = jnp.where(keep, value, 0.0)
+                out[span(at, size), :] = value
+                done = size
+            if done < PLANE:
+                out[span(at + done, PLANE - done), :] = jnp.zeros((PLANE - done, 2 * LAYER), f32)
+
+
+def last_kernel(
+    ids, from_below, from_above, down, up_planes, inv, acc_edges, inner, out, planes, sems
+):
     def body(group):
         points = POINTS[group]
         size = points * NP
-        wr[...] = wr_in[...]
-        add_planes(wr, points - 1, from_below, from_above, FIELDS)
         keep = lax.broadcasted_iota(jnp.int32, (size, 2 * LAYER), 0) % NP < points
-        for k in range(NP):
-            for f in range(FIELDS):
-                at = f * NODES + k * PLANE
-                done = 0
-                if k < points:
-                    scale = get_layers(inv, 1, k * PLANE, size) * (time_step / 6.0)
-                    rate = get_layers(wr, FIELDS, at, size) * scale
-                    value = acc_in[span(at, size), :] + rate
-                    if points < NP:
-                        value = jnp.where(keep, value, 0.0)
-                    out[span(at, size), :] = value
-                    done = size
-                if done < PLANE:
-                    out[span(at + done, PLANE - done), :] = jnp.zeros(
-                        (PLANE - done, 2 * LAYER), f32
+        copies = []
+        for f in range(FIELDS):
+            rate = edge_rate(group, f, from_below, from_above, down, up_planes, inv)
+            value = get_edges(acc_edges, f * PLANE, size) + (time_step / 6.0) * rate
+            if points < NP:
+                value = jnp.where(keep, value, 0.0)
+            put_edges(planes, f * PLANE, value)
+            for side in range(2):
+                row = f * NODES + side * (points - 1) * PLANE
+                copies.append(
+                    pltpu.make_async_copy(
+                        planes.at[span((side * FIELDS + f) * PLANE, size), :],
+                        out.at[span(row, size), side * LAYER : (side + 1) * LAYER],
+                        sems.at[side * FIELDS + f],
                     )
+                )
+                copies[-1].start()
+        for copy in copies:
+            copy.wait()
 
     each_group(ids, body)
 
@@ -485,7 +662,7 @@
 VMEM = pl.BlockSpec(memory_space=pltpu.VMEM)
 
 
-def call(kernel, args, outs, scratch, megabytes=24):
+def call(kernel, args, outs, scratch, megabytes):
     return pl.pallas_call(
         kernel,
         out_shape=[jax.ShapeDtypeStruct(s, f32) for s in outs],
@@ -514,6 +691,7 @@
     layered = (2 * FIELDS * NODES, LAYER)
     one_layered = (2 * NODES, LAYER)
     thin = (FIELDS * PLANE, LAYER)
+    edges = (2 * FIELDS * PLANE, LAYER)
     thick = ((FIELDS + 1) * PLANE + NP, LAYER)
     grads = (2, FIELDS, 2 * PLANE, width)
     size = lax.axis_size("elem")
@@ -526,47 +704,98 @@
             lax.ppermute(down_planes, "elem", down_pairs),
         )
 
-    lamb, wr, w, qw, up_planes, down_planes = call(
+    hbm = pl.BlockSpec(memory_space=pltpu.HBM)
+    (block,) = pl.pallas_call(
+        block_kernel,
+        out_shape=[jax.ShapeDtypeStruct((TILES * cap * peers, LAYER), f32)],
+        in_specs=[SMEM] + [hbm] * 4,
+        out_specs=[VMEM],
+        scratch_shapes=[
+            pltpu.VMEM((3 * NODES, width), f32),
+            pltpu.VMEM(les_mat.shape, bf16),
+            pltpu.VMEM(interp.shape, bf16),
+            pltpu.VMEM((cap, peers), jnp.int32),
+            pltpu.VMEM(grads, f32),
+            pltpu.VMEM((3 * NODES, width), f32),
+            pltpu.VMEM((BLOCK, width), f32),
+            pltpu.SemaphoreType.DMA((4,)),
+        ],
+        compiler_params=pltpu.CompilerParams(vmem_limit_bytes=62 * 1024 * 1024),
+    )(ids, state, les_mat, interp, send)
+    up_planes, down_planes = pl.pallas_call(
+        edge_kernel,
+        out_shape=[jax.ShapeDtypeStruct(thick, f32)] * 2,
+        in_specs=[SMEM] + [hbm] * 5 + [VMEM] * 2,
+        out_specs=[VMEM] * 2,
+        scratch_shapes=[
+            pltpu.VMEM(full, f32),
+            pltpu.VMEM(one, f32),
+            pltpu.VMEM((3 * NODES, width), f32),
+            pltpu.VMEM(les_mat.shape, bf16),
+            pltpu.VMEM(ape_mat.shape, bf16),
+            pltpu.VMEM(grads[1:], f32),
+            pltpu.VMEM(one, f32),
+            pltpu.VMEM(edges, f32),
+            pltpu.SemaphoreType.DMA((4,)),
+        ],
+        compiler_params=pltpu.CompilerParams(vmem_limit_bytes=62 * 1024 * 1024),
+    )(ids, state, jac, flow, les_mat, ape_mat, recv, recv_count)
+    from_below, from_above = exchange(up_planes, down_planes)
+    block = lax.all_to_all(block, "elem", split_axis=0, concat_axis=0, tiled=True)
+    block, from_below, from_above, late_state, late_jac, late_flow = lax.optimization_barrier(
+        (block, from_below, from_above, state, jac, flow)
+    )
+    wr, w, qw = call(
         first_kernel,
-        (ids, state, jac, flow, les_mat, ape_mat, recv, recv_count),
-        [(3 * NODES, width), layered, one, one_layered, thick, thick],
+        (ids, late_state, late_jac, late_flow, les_mat, ape_mat),
+        [layered, one, one_layered],
         [grads],
-    )
-    from_below, from_above = exchange(up_planes, down_planes)
-    (block,) = call(
-        block_kernel,
-        (ids, lamb, interp, send),
-        [(TILES * cap * peers, LAYER)],
-        [(BLOCK, width)],
-    )
-    block = lax.all_to_all(block, "elem", split_axis=0, concat_axis=0, tiled=True)
+        10,
+    )
     block = lax.ppermute(block, "grp", [(0, 1)])
-    wr, inv, acc, half, up_planes, down_planes = call(
+    v, inv, acc, half, acc_edges, up_planes, down_planes = call(
         second_kernel,
         (ids, block, recv, recv_count, from_below, from_above, state, w, qw, flow, les_mat,
          ape_mat, place, place_edge, wr),
-        [layered, one_layered, full, full, thin, thin],
-        [grads, layered, full, (6 * NODES, LAYER), (6 * PLANE, LAYER)],
-    )
-    for step in (0.5 * time_step, time_step):
+        [full, one_layered, full, full, edges, thin, thin],
+        [grads[1:], edges, (6 * NODES, LAYER), (6 * PLANE, LAYER)],
+        20,
+    )
+    vb = None
+    for step in (0.5 * time_step, time_step, None):
         from_below, from_above = exchange(up_planes, down_planes)
 
-        def kernel(*refs, step=step):
-            later_kernel(step, *refs)
-
-        wr, acc, up_planes, down_planes = call(
-            kernel,
-            (ids, from_below, from_above, state, half, w, inv, flow, les_mat, ape_mat, wr, acc),
-            [layered, full, thin, thin],
-            [grads, layered, full],
+        def inner(*refs, step=step):
+            inner_kernel(step, *refs)
+
+        def edge_step(*refs, step=step):
+            edge_step_kernel(step, *refs)
+
+        rest = (half, state, w, inv, flow, les_mat, ape_mat, acc)
+        if vb is None:
+            v, acc = call(inner, (ids, v) + rest, [full, full], [grads, layered], 22)
+        elif step is not None:
+            v, acc = call(inner, (ids, v, vb) + rest, [full, full], [grads, layered, full], 22)
+        else:
+            (out,) = call(inner, (ids, v, vb) + rest, [full], [grads, layered, full], 22)
+            break
+        vb, acc_edges, up_planes, down_planes = call(
+            edge_step,
+            (ids, from_below, from_above, down_planes, up_planes, v, half, state, w, inv, flow,
+             les_mat, ape_mat, acc_edges),
+            [edges, edges, thin, thin],
+            [grads[1:]],
+            14,
         )
-    from_below, from_above = exchange(up_planes, down_planes)
-    (out,) = call(
+    out = pl.pallas_call(
         last_kernel,
-        (ids, from_below, from_above, inv, wr, acc),
-        [full],
-        [layered],
-    )
+        out_shape=jax.ShapeDtypeStruct(full, f32),
+        in_specs=[SMEM] + [VMEM] * 6 + [hbm],
+        out_specs=hbm,
+        scratch_shapes=[pltpu.VMEM(edges, f32), pltpu.SemaphoreType.DMA((2 * FIELDS,))],
+        input_output_aliases={7: 0},
+        compiler_params=pltpu.CompilerParams(vmem_limit_bytes=6 * 1024 * 1024),
+    )(ids, from_below, from_above, down_planes, up_planes, inv, acc_edges, out)
     return out.reshape(1, FIELDS, NODES, width)
 
 

time: 95.7 us -> 78.7 us (0.82)
  blocking collectives: 25.9 us -> 0 us
  starting transfers between devices: 31.8 us -> 43.2 us
  Pallas kernels: 18.5 us -> 26.2 us
  waiting for transfers between devices: 12 us -> 5.82 us
  local copies, waits for them, and re-layouts: 7.07 us -> 2.67 us
    all_to_all x1 -> x0, blocking collectives: 25.9 us -> none  [on_device(): lax.all_to_all(block, 'elem', split_axis=0, concat_axis=0, tiled=True)]
    all_to_all x0 -> x1, starting transfers between devices: none -> 11.8 us  [on_device(): lax.all_to_all(block, 'elem', split_axis=0, concat_axis=0, tiled=True)]
    pallas_call x0 -> x3, Pallas kernels: none -> 10.3 us  [the longest x1 5.74 us: on_device(): pl.pallas_call(block_kernel, out_shape=[jax.ShapeDtypeStruct((TILES * cap...]
    ppermute x4, waiting for transfers between devices: 11.9 us -> 5.81 us  [exchange(): lax.ppermute(up_planes, 'elem', up_pairs)]
    unnamed x32 -> x20, local copies, waits for them, and re-layouts: 7.07 us -> 2.67 us
    pallas_call x6 -> x7, Pallas kernels: 18.5 us -> 15.9 us  [call(): pl.pallas_call(kernel, out_shape=[jax.ShapeDtypeStruct(s, f32) for s in o...]
    ppermute x4, starting transfers between devices: 29.5 us -> 28.3 us  [exchange(): lax.ppermute(down_planes, 'elem', down_pairs)]
  transfers between devices with their start and end apart: 9 -> 10, of which waited for: 4 -> 1; matrix products, arithmetic and copies ran while one was open for 0% -> 0% of each run, Pallas kernels for 0% -> 22%
where the time goes in v2:
time: 78.7 us; the launch traced here: 78.3 us
  starting transfers between devices  43.2 us (55%)
  Pallas kernels  26.2 us (33%)
  waiting for transfers between devices  5.82 us (7%)
  local copies, waits for them, and re-layouts  2.67 us (3%)
    ppermute x4, starting transfers between devices, exchange(): lax.ppermute(down_planes, 'elem', down_pairs)  28.3 us
    pallas_call x7, Pallas kernels, call(): pl.pallas_call(kernel, out_shape=[jax.ShapeDtypeStruct(s, f32) for s in o...  15.9 us
    all_to_all x1, starting transfers between devices, on_device(): lax.all_to_all(block, 'elem', split_axis=0, concat_axis=0, tiled=True)  11.8 us
    ppermute x4, waiting for transfers between devices, exchange(): lax.ppermute(up_planes, 'elem', up_pairs)  5.81 us
    pallas_call x1, Pallas kernels, on_device(): pl.pallas_call(block_kernel, out_shape=[jax.ShapeDtypeStruct((TILES * cap...  5.74 us
    pallas_call x1, Pallas kernels, on_device(): pl.pallas_call(edge_kernel, out_shape=[jax.ShapeDtypeStruct(thick, f32)]...  3.75 us
    unnamed x20, local copies, waits for them, and re-layouts  2.67 us
    ppermute x4, starting transfers between devices, exchange(): lax.ppermute(up_planes, 'elem', up_pairs)  1.79 us
  transfers between devices with their start and end apart: 10, of which 1 were waited for; matrix products, arithmetic and copies ran while one was open for 0% of the time, Pallas kernels for 22%

profile of v2, /device:TPU:0, one launch (start us, length us, event | category | flops | bytes accessed | tf_op | source)
XLA Modules:
  0.0 78.3 jit_solution(12753182186809815113)
XLA Ops:
  0.0 5.7 %shard_map.109 = f32[2048,128]{1,0:T(8,128)} custom-call(s32[1]{0:T(128)} %bitcast.ids.refs_0_, f32[2048,256]{1,0:T(8,128)} %bitcast.13, bf16[128,192]{1,0:T(8,128)(2,1)} %constant.16.clone.les_at.les_mat.refs_7_.refs_11_.refs_8_, bf16[2,296,512]{2,1,0:T(8,128)(2,1)} %constant.18.clone.interp_at, s32[4,64]{1,0:T(4,128)} %bitcast.35), custom_call_target="tpu_custom_call" | custom-call | tf_op jit(solution)/shard_map/pallas_call | solution.py:708
  5.7 11.8 %all-to-all-start = ((f32[64,32,128]{2,1,0:T(8,128)}), f32[64,32,128]{2,1,0:T(8,128)}, u32[]{:S(2)}, u32[]{:S(2)}) async-start(f32[64,32,128]{2,1,0:T(8,128)} %bitcast.34), calls=%async_computation | async-start | bytes 2097152 | tf_op jit(solution)/shard_map/all_to_all | solution.py:744
  17.5 0.0 copy-start.2
  17.5 0.0 copy-start.3
  17.6 0.0 copy-start.4
  17.6 3.7 %shard_map.110 = (f32[328,128]{1,0:T(8,128)}, f32[328,128]{1,0:T(8,128)}) custom-call(s32[1]{0:T(128)} %bitcast.ids.refs_0_, f32[2048,256]{1,0:T(8,128)} %bitcast.14, f32[512,256]{1,0:T(8,128)} %bitcast.30, f32[1536,256]{1,0:T(8,128)} %bitcast.22, bf16[128,192]{1,0:T(8,128)(2,1)} %constant.16.clone.les_at.les_mat.refs_7_.refs_11_.refs_8_, ...), custom_call_target="tpu_custom_call" | custom-call | tf_op jit(solution)/shard_map/pallas_call | solution.py:725
  21.3 1.6 %collective-permute-start = (f32[328,128]{1,0:T(8,128)}, f32[328,128]{1,0:T(8,128)S(1)}, u32[]{:S(2)}, u32[]{:S(2)}) collective-permute-start(f32[328,128]{1,0:T(8,128)} %get-tuple-element.35), channel_id=1, source_target_pairs={{0,1},{1,2},{2,3},{3,4},{4,5},{5,6},{6,7},{7,8},{8,9},{9,10},{10,1... | collective-permute-start | bytes 503816 | tf_op jit(solution)/shard_map/ppermute | solution.py:703
  22.9 6.0 %collective-permute-start.1 = (f32[328,128]{1,0:T(8,128)}, f32[328,128]{1,0:T(8,128)S(1)}, u32[]{:S(2)}, u32[]{:S(2)}) collective-permute-start(f32[328,128]{1,0:T(8,128)} %get-tuple-element.36), channel_id=1, source_target_pairs={{1,0},{2,1},{3,2},{4,3},{5,4},{6,5},{7,6},{8,7},{9,8},{10,9},{11,1... | collective-permute-start | bytes 503816 | tf_op jit(solution)/shard_map/ppermute | solution.py:704
  28.9 5.8 %collective-permute-done.from_below = f32[328,128]{1,0:T(8,128)S(1)} collective-permute-done((f32[328,128]{1,0:T(8,128)}, f32[328,128]{1,0:T(8,128)S(1)}, u32[]{:S(2)}, u32[]{:S(2)}) %collective-permute-start) | collective-permute-done | bytes 167968 | tf_op jit(solution)/shard_map/ppermute | solution.py:703
  34.7 0.0 collective-permute-done.1.from_above
  34.7 1.3 %collective-permute-start.2 = (f32[2048,128]{1,0:T(8,128)}, f32[2048,128]{1,0:T(8,128)S(1)}, u32[]{:S(2)}, u32[]{:S(2)}) collective-permute-start(f32[2048,128]{1,0:T(8,128)} %bitcast.5), channel_id=1, source_target_pairs={{0,64},{1,65},{2,66},{3,67},{4,68},{5,69},{6,70},{7,71},{8,72},{9,... | collective-permute-start | bytes 3145736 | tf_op jit(solution)/shard_map/ppermute | solution.py:755
  36.0 0.0 copy-start
  36.1 1.6 %copy-done = f32[1,4,512,256]{3,2,1,0:T(8,128)S(1)} copy-done((f32[1,4,512,256]{3,2,1,0:T(8,128)S(1)}, f32[1,4,512,256]{3,2,1,0:T(8,128)}, u32[]{:S(2)}) %copy-start) | copy-done | bytes 2097176
  37.6 1.0 %copy-done.5 = f32[1,512,256]{2,1,0:T(8,128)S(1)} copy-done((f32[1,512,256]{2,1,0:T(8,128)S(1)}, f32[1,512,256]{2,1,0:T(8,128)}, u32[]{:S(2)}) %copy-start.5) | copy-done | bytes 524312
  38.7 0.0 copy-start.9
  38.7 2.8 %shard_map.111 = (f32[4096,128]{1,0:T(8,128)S(1)}, f32[512,256]{1,0:T(8,128)S(1)}, f32[1024,128]{1,0:T(8,128)S(1)}) custom-call(s32[1]{0:T(128)} %bitcast.ids.refs_0_, f32[2048,256]{1,0:T(8,128)S(1)} %bitcast.15, f32[512,256]{1,0:T(8,128)S(1)} %bitcast.31, f32[1536,256]{1,0:T(8,128)S(1)} %bitcast.23, bf16[128,192]{1,0:T(8,128)(2,1)S(1)} %copy-done.3, ...), custom_call_target="tpu_custom_call" | custom-call | tf_op jit(solution)/shard_map/pallas_call | solution.py:666
  41.5 0.0 collective-permute-done.2.block
  41.6 1.5 %shard_map.112 = (f32[2048,256]{1,0:T(8,128)S(1)}, f32[1024,128]{1,0:T(8,128)S(1)}, f32[2048,256]{1,0:T(8,128)S(1)}, f32[2048,256]{1,0:T(8,128)S(1)}, f32[512,12...) custom-call(s32[1]{0:T(128)} %bitcast.ids.refs_0_, f32[2048,128]{1,0:T(8,128)S(1)} %collective-permute-done.2.block, ...), custom_call_target="tpu_custom_call" | custom-call | tf_op jit(solution)/shard_map/pallas_call | solution.py:666
  43.1 0.1 collective-permute-start.3
  43.2 7.4 %collective-permute-start.4 = (f32[256,128]{1,0:T(8,128)S(1)}, f32[256,128]{1,0:T(8,128)S(1)}, u32[]{:S(2)}, u32[]{:S(2)}) collective-permute-start(f32[256,128]{1,0:T(8,128)S(1)} %get-tuple-element.47.refs_3_), channel_id=1, source_target_pairs={{1,0},{2,1},{3,2},{4,3},{5,4},{6,5},{7,6},{8,7},{9,8},{10,9},{11,1... | collective-permute-start | bytes 393224 | tf_op jit(solution)/shard_map/ppermute | solution.py:704
  50.6 3.0 %shard_map.113 = (f32[2048,256]{1,0:T(8,128)S(1)}, f32[2048,256]{1,0:T(8,128)S(1)}) custom-call(s32[1]{0:T(128)} %bitcast.ids.refs_0_, f32[2048,256]{1,0:T(8,128)S(1)} %get-tuple-element.48.refs_1_, f32[2048,256]{1,0:T(8,128)S(1)} %get-tuple-element.49.refs_2_.refs_6_.refs_3_, f32[2048,256]{1,0:T(8,128)S(1)} %bitcast.17, ...), custom_call_target="tpu_custom_call" | custom-call | tf_op jit(solution)/shard_map/pallas_call | solution.py:666
  53.7 0.0 collective-permute-done.4.refs_2_
  53.7 0.5 shard_map.114
  54.2 0.1 collective-permute-start.5
  54.3 7.4 %collective-permute-start.6 = (f32[256,128]{1,0:T(8,128)S(1)}, f32[256,128]{1,0:T(8,128)S(1)}, u32[]{:S(2)}, u32[]{:S(2)}) collective-permute-start(f32[256,128]{1,0:T(8,128)S(1)} %get-tuple-element.55.refs_3_), channel_id=1, source_target_pairs={{1,0},{2,1},{3,2},{4,3},{5,4},{6,5},{7,6},{8,7},{9,8},{10,9},{11,1... | collective-permute-start | bytes 393224 | tf_op jit(solution)/shard_map/ppermute | solution.py:704
  61.7 3.2 %shard_map.115 = (f32[2048,256]{1,0:T(8,128)S(1)}, f32[2048,256]{1,0:T(8,128)S(1)}) custom-call(s32[1]{0:T(128)} %bitcast.ids.refs_0_, f32[2048,256]{1,0:T(8,128)S(1)} %get-tuple-element.52.refs_5_.refs_1_, f32[512,128]{1,0:T(8,128)S(1)} %get-tuple-element.56.refs_2_, f32[2048,256]{1,0:T(8,128)S(1)} %get-tuple-element.49.refs_2_.refs_6_.refs_3_, ...), custom_call_target="tpu_custom_call" | custom-call | tf_op jit(solution)/shard_map/pallas_call | solution.py:666
  65.0 0.0 collective-permute-done.6.refs_2_
  65.0 0.6 shard_map.116
  65.6 0.1 collective-permute-start.7
  65.7 7.4 %collective-permute-start.8 = (f32[256,128]{1,0:T(8,128)S(1)}, f32[256,128]{1,0:T(8,128)S(1)}, u32[]{:S(2)}, u32[]{:S(2)}) collective-permute-start(f32[256,128]{1,0:T(8,128)S(1)} %get-tuple-element.61.down), channel_id=1, source_target_pairs={{1,0},{2,1},{3,2},{4,3},{5,4},{6,5},{7,6},{8,7},{9,8},{10,9},{11,1... | collective-permute-start | bytes 393224 | tf_op jit(solution)/shard_map/ppermute | solution.py:704
  73.1 4.3 %shard_map.117.inner = f32[2048,256]{1,0:T(8,128)} custom-call(s32[1]{0:T(128)} %bitcast.ids.refs_0_, f32[2048,256]{1,0:T(8,128)S(1)} %get-tuple-element.58.refs_5_.refs_1_, f32[512,128]{1,0:T(8,128)S(1)} %get-tuple-element.63.refs_2_, f32[2048,256]{1,0:T(8,128)S(1)} %get-tuple-element.49.refs_2_.refs_6_.refs_3_, f32[2048,256]{1,0:T(8,128)S(1)} %bitcast.21, ...), custom_call_target="tpu_custom_call" | custom-call | tf_op jit(solution)/shard_map/pallas_call | solution.py:666
  77.4 0.8 shard_map.118
  (18 shorter events, 0.0 us)
Async XLA Ops:
  5.7 28.9 %all-to-all-start = ((f32[64,32,128]{2,1,0:T(8,128)}), f32[64,32,128]{2,1,0:T(8,128)}, u32[]{:S(2)}, u32[]{:S(2)}) async-start(f32[64,32,128]{2,1,0:T(8,128)} %bitcast.34), calls=%async_computation | async-start | bytes 2097152 | tf_op jit(solution)/shard_map/all_to_all | solution.py:744
  17.5 18.5 %copy-start.2 = (f32[3,512,256]{2,1,0:T(8,128)S(1)}, f32[3,512,256]{2,1,0:T(8,128)}, u32[]{:S(2)}) copy-start(f32[3,512,256]{2,1,0:T(8,128)} %param.12) | copy-start | bytes 4718596
  17.5 18.5 %copy-start.3 = (bf16[128,192]{1,0:T(8,128)(2,1)S(1)}, bf16[128,192]{1,0:T(8,128)(2,1)}, u32[]{:S(2)}) copy-start(bf16[128,192]{1,0:T(8,128)(2,1)} %constant.16.clone.les_at.les_mat.refs_7_.refs_11_.refs_8_) | copy-start | bytes 147460
  17.6 18.5 %copy-start.4 = (bf16[96,144]{1,0:T(8,128)(2,1)S(1)}, bf16[96,144]{1,0:T(8,128)(2,1)}, u32[]{:S(2)}) copy-start(bf16[96,144]{1,0:T(8,128)(2,1)} %constant.17.clone.ape_at.ape_mat.refs_8_.refs_12_.refs_9_) | copy-start | bytes 82948
  21.3 13.3 %collective-permute-start = (f32[328,128]{1,0:T(8,128)}, f32[328,128]{1,0:T(8,128)S(1)}, u32[]{:S(2)}, u32[]{:S(2)}) collective-permute-start(f32[328,128]{1,0:T(8,128)} %get-tuple-element.35), channel_id=1, source_target_pairs={{0,1},{1,2},{2,3},{3,4},{4,5},{5,6},{6,7},{7,8},{8,9},{9,10},{10,1... | collective-permute-start | bytes 503816 | tf_op jit(solution)/shard_map/ppermute | solution.py:703
  22.9 11.8 %collective-permute-start.1 = (f32[328,128]{1,0:T(8,128)}, f32[328,128]{1,0:T(8,128)S(1)}, u32[]{:S(2)}, u32[]{:S(2)}) collective-permute-start(f32[328,128]{1,0:T(8,128)} %get-tuple-element.36), channel_id=1, source_target_pairs={{1,0},{2,1},{3,2},{4,3},{5,4},{6,5},{7,6},{8,7},{9,8},{10,9},{11,1... | collective-permute-start | bytes 503816 | tf_op jit(solution)/shard_map/ppermute | solution.py:704
  34.7 6.8 %collective-permute-start.2 = (f32[2048,128]{1,0:T(8,128)}, f32[2048,128]{1,0:T(8,128)S(1)}, u32[]{:S(2)}, u32[]{:S(2)}) collective-permute-start(f32[2048,128]{1,0:T(8,128)} %bitcast.5), channel_id=1, source_target_pairs={{0,64},{1,65},{2,66},{3,67},{4,68},{5,69},{6,70},{7,71},{8,72},{9,... | collective-permute-start | bytes 3145736 | tf_op jit(solution)/shard_map/ppermute | solution.py:755
  36.0 1.6 %copy-start = (f32[1,4,512,256]{3,2,1,0:T(8,128)S(1)}, f32[1,4,512,256]{3,2,1,0:T(8,128)}, u32[]{:S(2)}) copy-start(f32[1,4,512,256]{3,2,1,0:T(8,128)} %param.11) | copy-start | bytes 6291460
  37.6 1.0 %copy-start.5 = (f32[1,512,256]{2,1,0:T(8,128)S(1)}, f32[1,512,256]{2,1,0:T(8,128)}, u32[]{:S(2)}) copy-start(f32[1,512,256]{2,1,0:T(8,128)} %param.13) | copy-start | bytes 1572868
  38.7 2.8 %copy-start.1 = (f32[1,4,512,256]{3,2,1,0:T(8,128)S(1)}, f32[1,4,512,256]{3,2,1,0:T(8,128)}, u32[]{:S(2)}) copy-start(f32[1,4,512,256]{3,2,1,0:T(8,128)} %param.11) | copy-start | bytes 6291460
  38.7 2.8 %copy-start.6 = (bf16[384,432]{1,0:T(8,128)(2,1)S(1)}, bf16[384,432]{1,0:T(8,128)(2,1)}, u32[]{:S(2)}) copy-start(bf16[384,432]{1,0:T(8,128)(2,1)} %constant.19.clone.place) | copy-start | bytes 995332
  38.7 2.8 %copy-start.7 = (bf16[64,80]{1,0:T(8,128)(2,1)S(1)}, bf16[64,80]{1,0:T(8,128)(2,1)}, u32[]{:S(2)}) copy-start(bf16[64,80]{1,0:T(8,128)(2,1)} %constant.20.clone.place_edge) | copy-start | bytes 30724
  38.7 2.9 %copy-start.8 = (s32[1,64,4]{1,2,0:T(4,128)S(1)}, s32[1,64,4]{1,2,0:T(4,128)}, u32[]{:S(2)}) copy-start(s32[1,64,4]{1,2,0:T(4,128)} %param.15) | copy-start | bytes 3076
  38.7 2.9 %copy-start.9 = (s32[1,64]{1,0:T(1,128)S(1)}, s32[1,64]{1,0:T(1,128)}, u32[]{:S(2)}) copy-start(s32[1,64]{1,0:T(1,128)} %count.3) | copy-start | bytes 772
  43.1 10.6 %collective-permute-start.3 = (f32[256,128]{1,0:T(8,128)S(1)}, f32[256,128]{1,0:T(8,128)S(1)}, u32[]{:S(2)}, u32[]{:S(2)}) collective-permute-start(f32[256,128]{1,0:T(8,128)S(1)} %get-tuple-element.46.refs_4_), channel_id=1, source_target_pairs={{0,1},{1,2},{2,3},{3,4},{4,5},{5,6},{6,7},{7,8},{8,9},{9,10},{10,1... | collective-permute-start | bytes 393224 | tf_op jit(solution)/shard_map/ppermute | solution.py:703
  43.2 10.5 %collective-permute-start.4 = (f32[256,128]{1,0:T(8,128)S(1)}, f32[256,128]{1,0:T(8,128)S(1)}, u32[]{:S(2)}, u32[]{:S(2)}) collective-permute-start(f32[256,128]{1,0:T(8,128)S(1)} %get-tuple-element.47.refs_3_), channel_id=1, source_target_pairs={{1,0},{2,1},{3,2},{4,3},{5,4},{6,5},{7,6},{8,7},{9,8},{10,9},{11,1... | collective-permute-start | bytes 393224 | tf_op jit(solution)/shard_map/ppermute | solution.py:704
  54.2 10.8 %collective-permute-start.5 = (f32[256,128]{1,0:T(8,128)S(1)}, f32[256,128]{1,0:T(8,128)S(1)}, u32[]{:S(2)}, u32[]{:S(2)}) collective-permute-start(f32[256,128]{1,0:T(8,128)S(1)} %get-tuple-element.54.refs_4_), channel_id=1, source_target_pairs={{0,1},{1,2},{2,3},{3,4},{4,5},{5,6},{6,7},{7,8},{8,9},{9,10},{10,1... | collective-permute-start | bytes 393224 | tf_op jit(solution)/shard_map/ppermute | solution.py:703
  54.3 10.7 %collective-permute-start.6 = (f32[256,128]{1,0:T(8,128)S(1)}, f32[256,128]{1,0:T(8,128)S(1)}, u32[]{:S(2)}, u32[]{:S(2)}) collective-permute-start(f32[256,128]{1,0:T(8,128)S(1)} %get-tuple-element.55.refs_3_), channel_id=1, source_target_pairs={{1,0},{2,1},{3,2},{4,3},{5,4},{6,5},{7,6},{8,7},{9,8},{10,9},{11,1... | collective-permute-start | bytes 393224 | tf_op jit(solution)/shard_map/ppermute | solution.py:704
  65.6 11.8 %collective-permute-start.7 = (f32[256,128]{1,0:T(8,128)S(1)}, f32[256,128]{1,0:T(8,128)S(1)}, u32[]{:S(2)}, u32[]{:S(2)}) collective-permute-start(f32[256,128]{1,0:T(8,128)S(1)} %get-tuple-element.60.up_planes), channel_id=1, source_target_pairs={{0,1},{1,2},{2,3},{3,4},{4,5},{5,6},{6,7},{7,8},{8,9},{9,10},{10,1... | collective-permute-start | bytes 393224 | tf_op jit(solution)/shard_map/ppermute | solution.py:703
  65.7 11.7 %collective-permute-start.8 = (f32[256,128]{1,0:T(8,128)S(1)}, f32[256,128]{1,0:T(8,128)S(1)}, u32[]{:S(2)}, u32[]{:S(2)}) collective-permute-start(f32[256,128]{1,0:T(8,128)S(1)} %get-tuple-element.61.down), channel_id=1, source_target_pairs={{1,0},{2,1},{3,2},{4,3},{5,4},{6,5},{7,6},{8,7},{9,8},{10,9},{11,1... | collective-permute-start | bytes 393224 | tf_op jit(solution)/shard_map/ppermute | solution.py:704

commit v3 on v2

--- a/solution.py
+++ b/solution.py
@@ -145,21 +145,23 @@
     )
 
 
+def sum_one_plane(ref, row, up, masks):
+    px, nx, py, ny = masks
+    lo_at = pl.ds(row, NP, stride=NP)
+    hi_at = pl.ds(row + up, NP, stride=NP)
+    lo, hi = pair_sum(ref[lo_at, :], ref[hi_at, :], 1, px, nx)
+    ref[lo_at, :] = lo
+    ref[hi_at, :] = hi
+    lo_rows = span(row)
+    hi_rows = span(row + up * NP)
+    lo, hi = pair_sum(ref[lo_rows, :], ref[hi_rows, :], EX, py, ny)
+    ref[lo_rows, :] = lo
+    ref[hi_rows, :] = hi
+
+
 def sum_in_plane(ref, blocks, up, masks):
-    px, nx, py, ny = masks
-    for group in range(0, blocks, NP):
-        count = min(NP, blocks - group)
-        lo_at = pl.ds(group * PLANE, count * NP, stride=NP)
-        hi_at = pl.ds(group * PLANE + up, count * NP, stride=NP)
-        lo, hi = pair_sum(ref[lo_at, :], ref[hi_at, :], 1, px, nx)
-        ref[lo_at, :] = lo
-        ref[hi_at, :] = hi
-        for k in range(group, group + count):
-            lo_rows = slice(k * PLANE, k * PLANE + NP)
-            hi_rows = slice(k * PLANE + up * NP, k * PLANE + (up + 1) * NP)
-            lo, hi = pair_sum(ref[lo_rows, :], ref[hi_rows, :], EX, py, ny)
-            ref[lo_rows, :] = lo
-            ref[hi_rows, :] = hi
+    for block in range(blocks):
+        sum_one_plane(ref, block * PLANE, up, masks)
 
 
 def sum_inner(ref, fields, up):
@@ -196,20 +198,42 @@
     return total
 
 
-def raw_stage(group, mat, v, w, flow, g, wr):
+def z_derivatives(d, points, v, gz):
+    for f in range(FIELDS):
+        for j in range(points):
+            at = [f * NODES + q * PLANE + j * NP for q in range(points)]
+            u = [v[span(a), :] for a in at]
+            half = points // 2
+            even = [u[q] + u[points - 1 - q] for q in range(half)]
+            odd = [u[q] - u[points - 1 - q] for q in range(half)]
+            for k in range(half):
+                first = second = None
+                for q in range(half):
+                    x = float(0.5 * (d[k, q] + d[k, points - 1 - q])) * even[q]
+                    y = float(0.5 * (d[k, q] - d[k, points - 1 - q])) * odd[q]
+                    first = x if first is None else first + x
+                    second = y if second is None else second + y
+                gz[span(at[k]), :] = second + first
+                gz[span(at[points - 1 - k]), :] = second - first
+
+
+def inner_stage(group, mat, v, w, flow, g, gz_at, wr, after=None):
     points = POINTS[group]
+    up = points - 1
     d = CONSTS["derivs"][group]
     size = points * NP
-    for k in range(points):
+    masks = lane_masks()
+    z_derivatives(d, points, v, gz_at)
+    for turn, k in enumerate([0, up] + list(range(1, up))):
         base = k * PLANE
         for f in range(FIELDS):
             high, low = split(v[span(f * NODES + base, size), :])
-            g[k % 2, f, : 2 * size, :] = dot(mat[...], jnp.concatenate([high, low, high], axis=0))
+            g[turn % 2, f, : 2 * size, :] = dot(mat[...], jnp.concatenate([high, low, high], axis=0))
         for j in range(points):
             at = base + j * NP
-            gx = [g[k % 2, f, span(j * NP), :] for f in range(FIELDS)]
-            gy = [g[k % 2, f, span(size + j * NP), :] for f in range(FIELDS)]
-            gz = [z_derivative(d, k, range(points), v, f, j) for f in range(FIELDS)]
+            gx = [g[turn % 2, f, span(j * NP), :] for f in range(FIELDS)]
+            gy = [g[turn % 2, f, span(size + j * NP), :] for f in range(FIELDS)]
+            gz = [gz_at[span(f * NODES + at), :] for f in range(FIELDS)]
             u = [v[span(m * NODES + at), :] for m in range(3)]
             a = u if group == 0 else [flow[span(m * NODES + at), :] for m in range(3)]
             carried = [a[0] * gx[f] + a[1] * gy[f] + a[2] * gz[f] for f in range(FIELDS)]
@@ -219,6 +243,13 @@
                 put_layers(wr, FIELDS, m * NODES + at, weight * (carried[m] + press[m]))
             total = weight * (carried[3] + SPEEDS[group] * (gx[0] + gy[1] + gz[2]))
             put_layers(wr, FIELDS, 3 * NODES + at, total)
+        for block in range(2 * FIELDS):
+            sum_one_plane(wr, block * NODES + base, up, masks)
+        if turn == 1:
+            sum_inner(wr, FIELDS, up)
+        if after is not None and turn >= 1:
+            for ready in (0, up) if turn == 1 else (k,):
+                after(ready)
 
 
 def edge_lanes(ref, row, up, size=NP):
@@ -277,13 +308,6 @@
         put_edges(out, f * PLANE, edge_lanes(ref, f * NODES, POINTS[group] - 1, PLANE))
 
 
-def inner_stage(group, mat, v, w, flow, g, wr):
-    up = POINTS[group] - 1
-    raw_stage(group, mat, v, w, flow, g, wr)
-    sum_in_plane(wr, 2 * FIELDS * NP, up, lane_masks())
-    sum_inner(wr, FIELDS, up)
-
-
 def each_group(ids, body):
     for group in range(2):
         pl.when(ids[0] == group)(lambda group=group: body(group))
@@ -316,34 +340,44 @@
 
 def first_kernel(
     ids, state, jac, flow, les_mat, ape_mat,
-    wr_out, w_out, qw_out, g,
+    wr_out, w_out, qw_out, g, gz,
 ):
     def body(group):
         up = POINTS[group] - 1
         for k, j, at, value in weights(group, jac, range(NP)):
             w_out[span(at), :] = value
             put_layers(qw_out, 1, at, value)
-        inner_stage(group, (les_mat, ape_mat)[group], state, w_out, flow, g, wr_out)
         sum_in_plane(qw_out, 2 * NP, up, lane_masks())
         sum_inner(qw_out, 1, up)
+        inner_stage(group, (les_mat, ape_mat)[group], state, w_out, flow, g, gz, wr_out)
 
     each_group(ids, body)
 
 
+def flow_copies(flow_at, flow, up, sems):
+    copies = []
+    for m in range(3):
+        for side in range(2):
+            where = (
+                span(m * NODES + side * up * PLANE, PLANE),
+                slice(side * LAYER, (side + 1) * LAYER),
+            )
+            copies.append(
+                pltpu.make_async_copy(flow_at.at[where], flow.at[where], sems.at[2 * m + side])
+            )
+    return copies
+
+
 def edge_kernel(
-    ids, state, jac_at, flow_at, les_at, ape_at, recv, count,
+    ids, state, jac, flow_at, les_mat, ape_mat, recv, count,
     up_out, down_out,
-    v, jac, flow, les_mat, ape_mat, g, w, vb, sems,
+    flow, g, w, vb, sems,
 ):
     cap, peers = recv.shape
-    sources = (state, jac_at, (les_at, ape_at), flow_at)
-    places = (v, jac, (les_mat, ape_mat), flow)
 
     def body(group):
-        copies = []
-        for n in range(4 if group == 1 else 3):
-            pick = (lambda x: x[group]) if n == 2 else (lambda x: x)
-            copies.append(pltpu.make_async_copy(pick(sources[n]), pick(places[n]), sems.at[n]))
+        up = POINTS[group] - 1
+        copies = flow_copies(flow_at, flow, up, sems) if group == 1 else []
         for copy in copies:
             copy.start()
         at = span((FIELDS + 1) * PLANE, NP)
@@ -353,16 +387,15 @@
         target = targets(recv, count)
         up_out[at, 0:peers] = target
         down_out[at, 0:peers] = target
-        for copy in copies:
-            copy.wait()
-        up = POINTS[group] - 1
         for k, j, at, value in weights(group, jac, (0, up)):
             w[span(at), :] = value
-        take_edges(group, v, vb)
-        edge_stage(group, (les_mat, ape_mat)[group], v, vb, w, flow, g, up_out, down_out)
+        take_edges(group, state, vb)
         at = span(FIELDS * PLANE, PLANE)
         up_out[at, :] = w[span(up * PLANE, PLANE), LAYER:]
         down_out[at, :] = w[span(0, PLANE), :LAYER]
+        for copy in copies:
+            copy.wait()
+        edge_stage(group, (les_mat, ape_mat)[group], state, vb, w, flow, g, up_out, down_out)
 
     each_group(ids, body)
 
@@ -378,17 +411,25 @@
     def _():
         copies = [
             pltpu.make_async_copy(les_at, les_mat, sems.at[0]),
-            pltpu.make_async_copy(state.at[0 : 3 * NODES, :], v, sems.at[1]),
-            pltpu.make_async_copy(send_at, send, sems.at[2]),
-            pltpu.make_async_copy(interp_at, interp, sems.at[3]),
+            pltpu.make_async_copy(send_at, send, sems.at[1]),
+            pltpu.make_async_copy(interp_at, interp, sems.at[2]),
         ]
-        for copy in copies:
+        fields = [
+            pltpu.make_async_copy(
+                state.at[span(half * NODES // 2, NODES // 2), :],
+                v.at[span(half * NODES // 2, NODES // 2), :],
+                sems.at[3 + half],
+            )
+            for half in range(6)
+        ]
+        for copy in fields + copies:
             copy.start()
         comp[3 * COMP : EDGE_LO, :] = jnp.zeros((EDGE_LO - 3 * COMP, 2 * LAYER), f32)
         comp[EDGE_LO + 3 * EDGE : EDGE_HI, :] = jnp.zeros((8, 2 * LAYER), f32)
         comp[EDGE_HI + 3 * EDGE : BLOCK, :] = jnp.zeros((8, 2 * LAYER), f32)
         copies[0].wait()
-        copies[1].wait()
+        for copy in fields:
+            copy.wait()
         d = CONSTS["derivs"][0]
         for k in range(NP):
             base = k * PLANE
@@ -409,8 +450,8 @@
                 lamb[span(at), :] = vy * u[2] - vz * u[1]
                 lamb[span(NODES + at), :] = vz * u[0] - vx * u[2]
                 lamb[span(2 * NODES + at), :] = vx * u[1] - vy * u[0]
+        copies[1].wait()
         copies[2].wait()
-        copies[3].wait()
         for m in range(3):
             high, low = split(lamb[m * NODES : (m + 1) * NODES, :])
             got = dot(interp[0], high) + dot(interp[0], low) + dot(interp[1], high)
@@ -459,10 +500,11 @@
     return jnp.concatenate([low, high], axis=1)
 
 
-def update(group, half, state, wr, inv, v, step, acc_in, acc_out, share, from_below, from_above):
-    points = POINTS[group]
-    size = points * NP
-    for k in range(points):
+def update(
+    group, half, state, wr, inv, v, step, acc_in, acc_out, share, from_below, from_above, planes=None
+):
+    for k in range(POINTS[group]) if planes is None else planes:
+        size = POINTS[group] * NP
         scale = get_layers(inv, 1, k * PLANE, size)
         for f in range(FIELDS):
             at = f * NODES + k * PLANE
@@ -478,9 +520,9 @@
 
 
 def second_kernel(
-    ids, block, recv, count, from_below, from_above, state, w, qw, flow, les_mat, ape_mat, place,
+    ids, block, recv, count, from_below, from_above, state, w, qw, flow_at, les_mat, ape_mat, place,
     place_edge, wr_in,
-    v, inv_out, acc_out, half_out, acc_edges, up_out, down_out, g, vb, src, edge,
+    v, inv_out, acc_out, half_out, acc_edges, up_out, down_out, g, vb, src, edge, flow, sems,
 ):
     cap, peers = recv.shape
     weights_at = span(FIELDS * PLANE, PLANE)
@@ -530,6 +572,9 @@
 
     def body(group):
         up = POINTS[group] - 1
+        copies = flow_copies(flow_at, flow, up, sems) if group == 1 else []
+        for copy in copies:
+            copy.start()
         inv_out[...] = qw[...]
         edge[0:PLANE, :] = from_below[weights_at, :]
         edge[PLANE : 2 * PLANE, :] = from_above[weights_at, :]
@@ -544,6 +589,8 @@
                time_step / 6.0, from_below, from_above)
         take_edges(group, v, vb)
         take_edges(group, acc_out, acc_edges)
+        for copy in copies:
+            copy.wait()
         edge_stage(group, (les_mat, ape_mat)[group], v, vb, w, flow, g, up_out, down_out)
 
     each_group(ids, body)
@@ -582,12 +629,14 @@
 
 def inner_kernel(step, ids, v_in, *refs):
     if step == 0.5 * time_step:
-        half, state, w, inv, flow, les_mat, ape_mat, acc_in, v_out, acc_out, g, wr = refs
+        half, state, w, inv, flow, les_mat, ape_mat, acc_in, v_out, acc_out, g, gz, wr = refs
         v = v_in
     else:
         vb, half, state, w, inv, flow, les_mat, ape_mat, acc_in = refs[:9]
-        g, wr, v = refs[-3:]
-        v_out, acc_out = (refs[9], refs[10]) if step is not None else (None, refs[9])
+        if step is None:
+            acc_out, g, gz, wr, v, result, sems = refs[9:]
+        else:
+            v_out, acc_out, g, gz, wr, v = refs[9:]
 
     def body(group):
         if v is not v_in:
@@ -598,34 +647,53 @@
                 value = get_edges(vb, f * PLANE, size)
                 v[span(f * NODES, size), :LAYER] = value[:, :LAYER]
                 v[span(f * NODES + up * PLANE, size), LAYER:] = value[:, LAYER:]
-        inner_stage(group, (les_mat, ape_mat)[group], v, w, flow, g, wr)
+        copies = []
+
+        def after(k):
+            if step is None:
+                finish(group, wr, inv, acc_in, result, k)
+                send_out(k)
+            else:
+                update(group, half, state, wr, inv, v_out, step, acc_in, acc_out, time_step / 3.0,
+                       None, None, (k,))
+
+        def send_out(k):
+            for f in range(FIELDS):
+                at = span(f * NODES + k * PLANE, PLANE)
+                copy = pltpu.make_async_copy(
+                    result.at[at, :], acc_out.at[at, :], sems.at[k * FIELDS + f]
+                )
+                copy.start()
+                copies.append(copy)
+
         if step is None:
-            finish(group, wr, inv, acc_in, acc_out)
-        else:
-            update(group, half, state, wr, inv, v_out, step, acc_in, acc_out, time_step / 3.0,
-                   None, None)
+            for k in range(POINTS[group], NP):
+                finish(group, wr, inv, acc_in, result, k)
+                send_out(k)
+        inner_stage(group, (les_mat, ape_mat)[group], v, w, flow, g, gz, wr, after)
+        for copy in copies:
+            copy.wait()
 
     each_group(ids, body)
 
 
-def finish(group, wr, inv, acc_in, out):
+def finish(group, wr, inv, acc_in, out, k):
     points = POINTS[group]
     size = points * NP
     keep = lax.broadcasted_iota(jnp.int32, (size, 2 * LAYER), 0) % NP < points
-    for k in range(NP):
-        for f in range(FIELDS):
-            at = f * NODES + k * PLANE
-            done = 0
-            if k < points:
-                scale = get_layers(inv, 1, k * PLANE, size) * (time_step / 6.0)
-                rate = summed(group, wr, f, k, size, None, None) * scale
-                value = acc_in[span(at, size), :] + rate
-                if points < NP:
-                    value = jnp.where(keep, value, 0.0)
-                out[span(at, size), :] = value
-                done = size
-            if done < PLANE:
-                out[span(at + done, PLANE - done), :] = jnp.zeros((PLANE - done, 2 * LAYER), f32)
+    for f in range(FIELDS):
+        at = f * NODES + k * PLANE
+        done = 0
+        if k < points:
+            scale = get_layers(inv, 1, k * PLANE, size) * (time_step / 6.0)
+            rate = summed(group, wr, f, k, size, None, None) * scale
+            value = acc_in[span(at, size), :] + rate
+            if points < NP:
+                value = jnp.where(keep, value, 0.0)
+            out[span(at, size), :] = value
+            done = size
+        if done < PLANE:
+            out[span(at + done, PLANE - done), :] = jnp.zeros((PLANE - done, 2 * LAYER), f32)
 
 
 def last_kernel(
@@ -718,48 +786,54 @@
             pltpu.VMEM(grads, f32),
             pltpu.VMEM((3 * NODES, width), f32),
             pltpu.VMEM((BLOCK, width), f32),
-            pltpu.SemaphoreType.DMA((4,)),
+            pltpu.SemaphoreType.DMA((9,)),
         ],
         compiler_params=pltpu.CompilerParams(vmem_limit_bytes=62 * 1024 * 1024),
     )(ids, state, les_mat, interp, send)
     up_planes, down_planes = pl.pallas_call(
         edge_kernel,
         out_shape=[jax.ShapeDtypeStruct(thick, f32)] * 2,
-        in_specs=[SMEM] + [hbm] * 5 + [VMEM] * 2,
+        in_specs=[SMEM] + [VMEM] * 2 + [hbm] + [VMEM] * 4,
         out_specs=[VMEM] * 2,
         scratch_shapes=[
-            pltpu.VMEM(full, f32),
-            pltpu.VMEM(one, f32),
             pltpu.VMEM((3 * NODES, width), f32),
-            pltpu.VMEM(les_mat.shape, bf16),
-            pltpu.VMEM(ape_mat.shape, bf16),
             pltpu.VMEM(grads[1:], f32),
             pltpu.VMEM(one, f32),
             pltpu.VMEM(edges, f32),
-            pltpu.SemaphoreType.DMA((4,)),
+            pltpu.SemaphoreType.DMA((6,)),
         ],
-        compiler_params=pltpu.CompilerParams(vmem_limit_bytes=62 * 1024 * 1024),
+        compiler_params=pltpu.CompilerParams(vmem_limit_bytes=8 * 1024 * 1024),
     )(ids, state, jac, flow, les_mat, ape_mat, recv, recv_count)
     from_below, from_above = exchange(up_planes, down_planes)
     block = lax.all_to_all(block, "elem", split_axis=0, concat_axis=0, tiled=True)
-    block, from_below, from_above, late_state, late_jac, late_flow = lax.optimization_barrier(
-        (block, from_below, from_above, state, jac, flow)
+    block, from_below, from_above, late_ids = lax.optimization_barrier(
+        (block, from_below, from_above, ids)
     )
     wr, w, qw = call(
         first_kernel,
-        (ids, late_state, late_jac, late_flow, les_mat, ape_mat),
+        (late_ids, state, jac, flow, les_mat, ape_mat),
         [layered, one, one_layered],
-        [grads],
-        10,
+        [grads, full],
+        12,
     )
     block = lax.ppermute(block, "grp", [(0, 1)])
-    v, inv, acc, half, acc_edges, up_planes, down_planes = call(
+    v, inv, acc, half, acc_edges, up_planes, down_planes = pl.pallas_call(
         second_kernel,
-        (ids, block, recv, recv_count, from_below, from_above, state, w, qw, flow, les_mat,
-         ape_mat, place, place_edge, wr),
-        [full, one_layered, full, full, edges, thin, thin],
-        [grads[1:], edges, (6 * NODES, LAYER), (6 * PLANE, LAYER)],
-        20,
+        out_shape=[
+            jax.ShapeDtypeStruct(s, f32)
+            for s in (full, one_layered, full, full, edges, thin, thin)
+        ],
+        in_specs=[SMEM] + [VMEM] * 8 + [hbm] + [VMEM] * 5,
+        out_specs=[VMEM] * 7,
+        scratch_shapes=[
+            pltpu.VMEM(s, f32)
+            for s in (grads[1:], edges, (6 * NODES, LAYER), (6 * PLANE, LAYER), (3 * NODES, width))
+        ]
+        + [pltpu.SemaphoreType.DMA((6,))],
+        compiler_params=pltpu.CompilerParams(vmem_limit_bytes=24 * 1024 * 1024),
+    )(
+        ids, block, recv, recv_count, from_below, from_above, state, w, qw, flow, les_mat,
+        ape_mat, place, place_edge, wr,
     )
     vb = None
     for step in (0.5 * time_step, time_step, None):
@@ -773,11 +847,19 @@
 
         rest = (half, state, w, inv, flow, les_mat, ape_mat, acc)
         if vb is None:
-            v, acc = call(inner, (ids, v) + rest, [full, full], [grads, layered], 22)
+            v, acc = call(inner, (ids, v) + rest, [full, full], [grads, full, layered], 24)
         elif step is not None:
-            v, acc = call(inner, (ids, v, vb) + rest, [full, full], [grads, layered, full], 22)
+            v, acc = call(inner, (ids, v, vb) + rest, [full, full], [grads, full, layered, full], 24)
         else:
-            (out,) = call(inner, (ids, v, vb) + rest, [full], [grads, layered, full], 22)
+            out = pl.pallas_call(
+                inner,
+                out_shape=jax.ShapeDtypeStruct(full, f32),
+                in_specs=[SMEM] + [VMEM] * 10,
+                out_specs=hbm,
+                scratch_shapes=[pltpu.VMEM(s, f32) for s in (grads, full, layered, full, full)]
+                + [pltpu.SemaphoreType.DMA((FIELDS * NP,))],
+                compiler_params=pltpu.CompilerParams(vmem_limit_bytes=24 * 1024 * 1024),
+            )(ids, v, vb, *rest)
             break
         vb, acc_edges, up_planes, down_planes = call(
             edge_step,

time: 78.7 us -> 77.9 us (0.990)
  Pallas kernels: 26.2 us -> 22.7 us
  waiting for transfers between devices: 5.82 us -> 8.32 us
    pallas_call x7 -> x5, Pallas kernels: 15.9 us -> 10 us  [call(): pl.pallas_call(kernel, out_shape=[jax.ShapeDtypeStruct(s, f32) for s in o...]
    pallas_call x0 -> x2, Pallas kernels: none -> 5.46 us  [the longest x1 3.94 us: on_device(): pl.pallas_call(inner, out_shape=jax.ShapeDtypeStruct(full, f32), in_specs...]
    pallas_call x1, Pallas kernels: 3.75 us -> 0.56 us  [on_device(): pl.pallas_call(edge_kernel, out_shape=[jax.ShapeDtypeStruct(thick, f32)]...]
    ppermute x4, waiting for transfers between devices: 5.81 us -> 8.31 us  [exchange(): lax.ppermute(up_planes, 'elem', up_pairs)]
    unnamed x20 -> x22, local copies, waits for them, and re-layouts: 2.67 us -> 2.84 us
  transfers between devices with their start and end apart: 10 -> 10, of which waited for: 1 -> 2; matrix products, arithmetic and copies ran while one was open for 0% -> 0% of each run, Pallas kernels for 22% -> 17%
where the time goes in v3:
time: 77.9 us; the launch traced here: 77.6 us
  starting transfers between devices  43.3 us (56%)
  Pallas kernels  22.7 us (29%)
  waiting for transfers between devices  8.32 us (11%)
  local copies, waits for them, and re-layouts  2.84 us (4%)
    ppermute x4, starting transfers between devices, exchange(): lax.ppermute(down_planes, 'elem', down_pairs)  28.3 us
    all_to_all x1, starting transfers between devices, on_device(): lax.all_to_all(block, 'elem', split_axis=0, concat_axis=0, tiled=True)  11.9 us
    pallas_call x5, Pallas kernels, call(): pl.pallas_call(kernel, out_shape=[jax.ShapeDtypeStruct(s, f32) for s in o...  10 us
    ppermute x4, waiting for transfers between devices, exchange(): lax.ppermute(up_planes, 'elem', up_pairs)  8.31 us
    pallas_call x1, Pallas kernels, on_device(): pl.pallas_call(block_kernel, out_shape=[jax.ShapeDtypeStruct((TILES * cap...  5.86 us
    pallas_call x1, Pallas kernels, on_device(): pl.pallas_call(inner, out_shape=jax.ShapeDtypeStruct(full, f32), in_specs...  3.94 us
    unnamed x22, local copies, waits for them, and re-layouts  2.84 us
    ppermute x4, starting transfers between devices, exchange(): lax.ppermute(up_planes, 'elem', up_pairs)  1.79 us
  transfers between devices with their start and end apart: 10, of which 2 were waited for; matrix products, arithmetic and copies ran while one was open for 0% of the time, Pallas kernels for 17%

profile of v3, /device:TPU:0, one launch (start us, length us, event | category | flops | bytes accessed | tf_op | source)
XLA Modules:
  0.0 77.6 jit_solution(2907906329670718799)
XLA Ops:
  0.0 5.9 %shard_map.109 = f32[2048,128]{1,0:T(8,128)} custom-call(s32[1]{0:T(128)} %bitcast.ids.refs_0_, f32[2048,256]{1,0:T(8,128)} %bitcast.13, bf16[128,192]{1,0:T(8,128)(2,1)} %constant.16.clone.les_at.les_mat.refs_7_.refs_11_.refs_8_, bf16[2,296,512]{2,1,0:T(8,128)(2,1)} %constant.18.clone.interp_at, s32[4,64]{1,0:T(4,128)} %bitcast.35), custom_call_target="tpu_custom_call" | custom-call | tf_op jit(solution)/shard_map/pallas_call | solution.py:776
  5.9 0.0 copy-start
  5.9 11.9 %all-to-all-start = ((f32[64,32,128]{2,1,0:T(8,128)}), f32[64,32,128]{2,1,0:T(8,128)}, u32[]{:S(2)}, u32[]{:S(2)}) async-start(f32[64,32,128]{2,1,0:T(8,128)} %bitcast.34), calls=%async_computation | async-start | bytes 2097152 | tf_op jit(solution)/shard_map/all_to_all | solution.py:808
  17.9 0.0 copy-start.1
  17.9 1.4 %copy-done.1 = f32[3,512,256]{2,1,0:T(8,128)S(1)} copy-done((f32[3,512,256]{2,1,0:T(8,128)S(1)}, f32[3,512,256]{2,1,0:T(8,128)}, u32[]{:S(2)}) %copy-start.1) | copy-done | bytes 1572888
  19.3 0.6 shard_map.110
  19.9 1.6 %collective-permute-start = (f32[328,128]{1,0:T(8,128)S(1)}, f32[328,128]{1,0:T(8,128)S(1)}, u32[]{:S(2)}, u32[]{:S(2)}) collective-permute-start(f32[328,128]{1,0:T(8,128)S(1)} %get-tuple-element.33), channel_id=1, source_target_pairs={{0,1},{1,2},{2,3},{3,4},{4,5},{5,6},{6,7},{7,8},{8,9},{9,10},{10,1... | collective-permute-start | bytes 503816 | tf_op jit(solution)/shard_map/ppermute | solution.py:771
  21.4 6.0 %collective-permute-start.1 = (f32[328,128]{1,0:T(8,128)S(1)}, f32[328,128]{1,0:T(8,128)S(1)}, u32[]{:S(2)}, u32[]{:S(2)}) collective-permute-start(f32[328,128]{1,0:T(8,128)S(1)} %get-tuple-element.34), channel_id=1, source_target_pairs={{1,0},{2,1},{3,2},{4,3},{5,4},{6,5},{7,6},{8,7},{9,8},{10,9},{11,1... | collective-permute-start | bytes 503816 | tf_op jit(solution)/shard_map/ppermute | solution.py:772
  27.4 7.5 %collective-permute-done.from_below = f32[328,128]{1,0:T(8,128)S(1)} collective-permute-done((f32[328,128]{1,0:T(8,128)S(1)}, f32[328,128]{1,0:T(8,128)S(1)}, u32[]{:S(2)}, u32[]{:S(2)}) %collective-permute-start) | collective-permute-done | bytes 167968 | tf_op jit(solution)/shard_map/ppermute | solution.py:771
  34.9 0.0 collective-permute-done.1.from_above
  34.9 0.0 all-to-all-done
  34.9 1.3 %collective-permute-start.2 = (f32[2048,128]{1,0:T(8,128)}, f32[2048,128]{1,0:T(8,128)S(1)}, u32[]{:S(2)}, u32[]{:S(2)}) collective-permute-start(f32[2048,128]{1,0:T(8,128)} %bitcast.5), channel_id=1, source_target_pairs={{0,64},{1,65},{2,66},{3,67},{4,68},{5,69},{6,70},{7,71},{8,72},{9,... | collective-permute-start | bytes 3145736 | tf_op jit(solution)/shard_map/ppermute | solution.py:819
  36.2 0.0 copy-start.2
  36.2 1.4 %copy-done.2 = f32[3,512,256]{2,1,0:T(8,128)S(1)} copy-done((f32[3,512,256]{2,1,0:T(8,128)S(1)}, f32[3,512,256]{2,1,0:T(8,128)}, u32[]{:S(2)}) %copy-start.2) | copy-done | bytes 1572888
  37.6 2.5 %shard_map.111 = (f32[4096,128]{1,0:T(8,128)S(1)}, f32[512,256]{1,0:T(8,128)S(1)}, f32[1024,128]{1,0:T(8,128)S(1)}) custom-call(s32[1]{0:T(128)} %bitcast.ids.refs_0_, f32[2048,256]{1,0:T(8,128)S(1)} %bitcast.15, f32[512,256]{1,0:T(8,128)S(1)} %bitcast.31, f32[1536,256]{1,0:T(8,128)S(1)} %bitcast.23, bf16[128,192]{1,0:T(8,128)(2,1)S(1)} %copy-done.4, ...), custom_call_target="tpu_custom_call" | custom-call | tf_op jit(solution)/shard_map/pallas_call | solution.py:734
  40.2 0.0 collective-permute-done.2.block
  40.2 1.5 %shard_map.112 = (f32[2048,256]{1,0:T(8,128)S(1)}, f32[1024,128]{1,0:T(8,128)S(1)}, f32[2048,256]{1,0:T(8,128)S(1)}, f32[2048,256]{1,0:T(8,128)S(1)}, f32[512,12...) custom-call(s32[1]{0:T(128)} %bitcast.ids.refs_0_, f32[2048,128]{1,0:T(8,128)S(1)} %collective-permute-done.2.block, ...), custom_call_target="tpu_custom_call" | custom-call | tf_op jit(solution)/shard_map/pallas_call | solution.py:820
  41.7 0.1 collective-permute-start.3
  41.8 7.4 %collective-permute-start.4 = (f32[256,128]{1,0:T(8,128)S(1)}, f32[256,128]{1,0:T(8,128)S(1)}, u32[]{:S(2)}, u32[]{:S(2)}) collective-permute-start(f32[256,128]{1,0:T(8,128)S(1)} %get-tuple-element.43.refs_3_), channel_id=1, source_target_pairs={{1,0},{2,1},{3,2},{4,3},{5,4},{6,5},{7,6},{8,7},{9,8},{10,9},{11,1... | collective-permute-start | bytes 393224 | tf_op jit(solution)/shard_map/ppermute | solution.py:772
  49.3 3.0 %shard_map.113 = (f32[2048,256]{1,0:T(8,128)S(1)}, f32[2048,256]{1,0:T(8,128)S(1)}) custom-call(s32[1]{0:T(128)} %bitcast.ids.refs_0_, f32[2048,256]{1,0:T(8,128)S(1)} %get-tuple-element.44.refs_1_, f32[2048,256]{1,0:T(8,128)S(1)} %get-tuple-element.45.refs_2_.refs_6_.refs_3_, f32[2048,256]{1,0:T(8,128)S(1)} %bitcast.17, ...), custom_call_target="tpu_custom_call" | custom-call | tf_op jit(solution)/shard_map/pallas_call | solution.py:734
  52.3 0.8 %collective-permute-done.3.refs_1_ = f32[256,128]{1,0:T(8,128)S(1)} collective-permute-done((f32[256,128]{1,0:T(8,128)S(1)}, f32[256,128]{1,0:T(8,128)S(1)}, u32[]{:S(2)}, u32[]{:S(2)}) %collective-permute-start.3) | collective-permute-done | bytes 131104 | tf_op jit(solution)/shard_map/ppermute | solution.py:771
  53.1 0.6 shard_map.114
  53.7 0.1 collective-permute-start.5
  53.7 7.4 %collective-permute-start.6 = (f32[256,128]{1,0:T(8,128)S(1)}, f32[256,128]{1,0:T(8,128)S(1)}, u32[]{:S(2)}, u32[]{:S(2)}) collective-permute-start(f32[256,128]{1,0:T(8,128)S(1)} %get-tuple-element.51.refs_3_), channel_id=1, source_target_pairs={{1,0},{2,1},{3,2},{4,3},{5,4},{6,5},{7,6},{8,7},{9,8},{10,9},{11,1... | collective-permute-start | bytes 393224 | tf_op jit(solution)/shard_map/ppermute | solution.py:772
  61.2 3.3 %shard_map.115 = (f32[2048,256]{1,0:T(8,128)S(1)}, f32[2048,256]{1,0:T(8,128)S(1)}) custom-call(s32[1]{0:T(128)} %bitcast.ids.refs_0_, f32[2048,256]{1,0:T(8,128)S(1)} %get-tuple-element.48.refs_5_.refs_1_, f32[512,128]{1,0:T(8,128)S(1)} %get-tuple-element.52.refs_2_, f32[2048,256]{1,0:T(8,128)S(1)} %get-tuple-element.45.refs_2_.refs_6_.refs_3_, ...), custom_call_target="tpu_custom_call" | custom-call | tf_op jit(solution)/shard_map/pallas_call | solution.py:734
  64.5 0.0 collective-permute-done.5.refs_1_
  64.6 0.6 shard_map.116
  65.2 0.1 collective-permute-start.7
  65.2 7.4 %collective-permute-start.8 = (f32[256,128]{1,0:T(8,128)S(1)}, f32[256,128]{1,0:T(8,128)S(1)}, u32[]{:S(2)}, u32[]{:S(2)}) collective-permute-start(f32[256,128]{1,0:T(8,128)S(1)} %get-tuple-element.57.down), channel_id=1, source_target_pairs={{1,0},{2,1},{3,2},{4,3},{5,4},{6,5},{7,6},{8,7},{9,8},{10,9},{11,1... | collective-permute-start | bytes 393224 | tf_op jit(solution)/shard_map/ppermute | solution.py:772
  72.7 3.9 %shard_map.117.inner = f32[2048,256]{1,0:T(8,128)} custom-call(s32[1]{0:T(128)} %bitcast.ids.refs_0_, f32[2048,256]{1,0:T(8,128)S(1)} %get-tuple-element.54.refs_5_.refs_1_, f32[512,128]{1,0:T(8,128)S(1)} %get-tuple-element.59.refs_2_, f32[2048,256]{1,0:T(8,128)S(1)} %get-tuple-element.45.refs_2_.refs_6_.refs_3_, f32[2048,256]{1,0:T(8,128)S(1)} %bitcast.21, ...), custom_call_target="tpu_custom_call" | custom-call | tf_op jit(solution)/shard_map/pallas_call | solution.py:854
  76.6 0.0 collective-permute-done.8.from_above
  76.7 0.8 %shard_map.118 = f32[2048,256]{1,0:T(8,128)} custom-call(s32[1]{0:T(128)} %bitcast.ids.refs_0_, f32[256,128]{1,0:T(8,128)S(1)} %collective-permute-done.7.from_below, f32[256,128]{1,0:T(8,128)S(1)} %collective-permute-done.8.from_above, f32[256,128]{1,0:T(8,128)S(1)} %get-tuple-element.57.down, ...), custom_call_target="tpu_custom_call", output_to_operand_aliasing={{}: (7, {})} | custom-call | tf_op jit(solution)/shard_map/pallas_call | solution.py:872
  (20 shorter events, 0.0 us)
Async XLA Ops:
  0.0 17.8 %copy-start.4 = (bf16[128,192]{1,0:T(8,128)(2,1)S(1)}, bf16[128,192]{1,0:T(8,128)(2,1)}, u32[]{:S(2)}) copy-start(bf16[128,192]{1,0:T(8,128)(2,1)} %constant.16.clone.les_at.les_mat.refs_7_.refs_11_.refs_8_) | copy-start | bytes 147460
  0.0 17.8 %copy-start.5 = (bf16[96,144]{1,0:T(8,128)(2,1)S(1)}, bf16[96,144]{1,0:T(8,128)(2,1)}, u32[]{:S(2)}) copy-start(bf16[96,144]{1,0:T(8,128)(2,1)} %constant.17.clone.ape_mat.refs_8_.refs_12_.refs_9_) | copy-start | bytes 82948
  0.0 17.8 %copy-start.6 = (f32[1,512,256]{2,1,0:T(8,128)S(1)}, f32[1,512,256]{2,1,0:T(8,128)}, u32[]{:S(2)}) copy-start(f32[1,512,256]{2,1,0:T(8,128)} %param.13) | copy-start | bytes 1572868
  0.0 17.8 %copy-start.9 = (s32[1,64,4]{1,2,0:T(4,128)S(1)}, s32[1,64,4]{1,2,0:T(4,128)}, u32[]{:S(2)}) copy-start(s32[1,64,4]{1,2,0:T(4,128)} %param.15) | copy-start | bytes 3076
  0.0 17.8 %copy-start.10 = (s32[1,64]{1,0:T(1,128)S(1)}, s32[1,64]{1,0:T(1,128)}, u32[]{:S(2)}) copy-start(s32[1,64]{1,0:T(1,128)} %count.3) | copy-start | bytes 772
  5.9 12.0 %copy-start = (f32[1,4,512,256]{3,2,1,0:T(8,128)S(1)}, f32[1,4,512,256]{3,2,1,0:T(8,128)}, u32[]{:S(2)}) copy-start(f32[1,4,512,256]{3,2,1,0:T(8,128)} %param.11) | copy-start | bytes 6291460
  5.9 29.0 %all-to-all-start = ((f32[64,32,128]{2,1,0:T(8,128)}), f32[64,32,128]{2,1,0:T(8,128)}, u32[]{:S(2)}, u32[]{:S(2)}) async-start(f32[64,32,128]{2,1,0:T(8,128)} %bitcast.34), calls=%async_computation | async-start | bytes 2097152 | tf_op jit(solution)/shard_map/all_to_all | solution.py:808
  17.9 1.4 %copy-start.1 = (f32[3,512,256]{2,1,0:T(8,128)S(1)}, f32[3,512,256]{2,1,0:T(8,128)}, u32[]{:S(2)}) copy-start(f32[3,512,256]{2,1,0:T(8,128)} %param.12) | copy-start | bytes 4718596
  19.9 15.0 %collective-permute-start = (f32[328,128]{1,0:T(8,128)S(1)}, f32[328,128]{1,0:T(8,128)S(1)}, u32[]{:S(2)}, u32[]{:S(2)}) collective-permute-start(f32[328,128]{1,0:T(8,128)S(1)} %get-tuple-element.33), channel_id=1, source_target_pairs={{0,1},{1,2},{2,3},{3,4},{4,5},{5,6},{6,7},{7,8},{8,9},{9,10},{10,1... | collective-permute-start | bytes 503816 | tf_op jit(solution)/shard_map/ppermute | solution.py:771
  21.4 13.5 %collective-permute-start.1 = (f32[328,128]{1,0:T(8,128)S(1)}, f32[328,128]{1,0:T(8,128)S(1)}, u32[]{:S(2)}, u32[]{:S(2)}) collective-permute-start(f32[328,128]{1,0:T(8,128)S(1)} %get-tuple-element.34), channel_id=1, source_target_pairs={{1,0},{2,1},{3,2},{4,3},{5,4},{6,5},{7,6},{8,7},{9,8},{10,9},{11,1... | collective-permute-start | bytes 503816 | tf_op jit(solution)/shard_map/ppermute | solution.py:772
  34.9 5.3 %collective-permute-start.2 = (f32[2048,128]{1,0:T(8,128)}, f32[2048,128]{1,0:T(8,128)S(1)}, u32[]{:S(2)}, u32[]{:S(2)}) collective-permute-start(f32[2048,128]{1,0:T(8,128)} %bitcast.5), channel_id=1, source_target_pairs={{0,64},{1,65},{2,66},{3,67},{4,68},{5,69},{6,70},{7,71},{8,72},{9,... | collective-permute-start | bytes 3145736 | tf_op jit(solution)/shard_map/ppermute | solution.py:819
  36.2 1.4 %copy-start.2 = (f32[3,512,256]{2,1,0:T(8,128)S(1)}, f32[3,512,256]{2,1,0:T(8,128)}, u32[]{:S(2)}) copy-start(f32[3,512,256]{2,1,0:T(8,128)} %param.12) | copy-start | bytes 4718596
  37.6 2.5 %copy-start.3 = (f32[3,512,256]{2,1,0:T(8,128)S(1)}, f32[3,512,256]{2,1,0:T(8,128)}, u32[]{:S(2)}) copy-start(f32[3,512,256]{2,1,0:T(8,128)} %param.12) | copy-start | bytes 4718596
  37.6 2.5 %copy-start.7 = (bf16[384,432]{1,0:T(8,128)(2,1)S(1)}, bf16[384,432]{1,0:T(8,128)(2,1)}, u32[]{:S(2)}) copy-start(bf16[384,432]{1,0:T(8,128)(2,1)} %constant.19.clone.place) | copy-start | bytes 995332
  37.6 2.6 %copy-start.8 = (bf16[64,80]{1,0:T(8,128)(2,1)S(1)}, bf16[64,80]{1,0:T(8,128)(2,1)}, u32[]{:S(2)}) copy-start(bf16[64,80]{1,0:T(8,128)(2,1)} %constant.20.clone.place_edge) | copy-start | bytes 30724
  41.7 11.4 %collective-permute-start.3 = (f32[256,128]{1,0:T(8,128)S(1)}, f32[256,128]{1,0:T(8,128)S(1)}, u32[]{:S(2)}, u32[]{:S(2)}) collective-permute-start(f32[256,128]{1,0:T(8,128)S(1)} %get-tuple-element.42.refs_4_), channel_id=1, source_target_pairs={{0,1},{1,2},{2,3},{3,4},{4,5},{5,6},{6,7},{7,8},{8,9},{9,10},{10,1... | collective-permute-start | bytes 393224 | tf_op jit(solution)/shard_map/ppermute | solution.py:771
  41.8 11.3 %collective-permute-start.4 = (f32[256,128]{1,0:T(8,128)S(1)}, f32[256,128]{1,0:T(8,128)S(1)}, u32[]{:S(2)}, u32[]{:S(2)}) collective-permute-start(f32[256,128]{1,0:T(8,128)S(1)} %get-tuple-element.43.refs_3_), channel_id=1, source_target_pairs={{1,0},{2,1},{3,2},{4,3},{5,4},{6,5},{7,6},{8,7},{9,8},{10,9},{11,1... | collective-permute-start | bytes 393224 | tf_op jit(solution)/shard_map/ppermute | solution.py:772
  53.7 10.9 %collective-permute-start.5 = (f32[256,128]{1,0:T(8,128)S(1)}, f32[256,128]{1,0:T(8,128)S(1)}, u32[]{:S(2)}, u32[]{:S(2)}) collective-permute-start(f32[256,128]{1,0:T(8,128)S(1)} %get-tuple-element.50.refs_4_), channel_id=1, source_target_pairs={{0,1},{1,2},{2,3},{3,4},{4,5},{5,6},{6,7},{7,8},{8,9},{9,10},{10,1... | collective-permute-start | bytes 393224 | tf_op jit(solution)/shard_map/ppermute | solution.py:771
  53.7 10.8 %collective-permute-start.6 = (f32[256,128]{1,0:T(8,128)S(1)}, f32[256,128]{1,0:T(8,128)S(1)}, u32[]{:S(2)}, u32[]{:S(2)}) collective-permute-start(f32[256,128]{1,0:T(8,128)S(1)} %get-tuple-element.51.refs_3_), channel_id=1, source_target_pairs={{1,0},{2,1},{3,2},{4,3},{5,4},{6,5},{7,6},{8,7},{9,8},{10,9},{11,1... | collective-permute-start | bytes 393224 | tf_op jit(solution)/shard_map/ppermute | solution.py:772
  65.2 11.5 %collective-permute-start.7 = (f32[256,128]{1,0:T(8,128)S(1)}, f32[256,128]{1,0:T(8,128)S(1)}, u32[]{:S(2)}, u32[]{:S(2)}) collective-permute-start(f32[256,128]{1,0:T(8,128)S(1)} %get-tuple-element.56.up_planes), channel_id=1, source_target_pairs={{0,1},{1,2},{2,3},{3,4},{4,5},{5,6},{6,7},{7,8},{8,9},{9,10},{10,1... | collective-permute-start | bytes 393224 | tf_op jit(solution)/shard_map/ppermute | solution.py:771
  65.2 11.4 %collective-permute-start.8 = (f32[256,128]{1,0:T(8,128)S(1)}, f32[256,128]{1,0:T(8,128)S(1)}, u32[]{:S(2)}, u32[]{:S(2)}) collective-permute-start(f32[256,128]{1,0:T(8,128)S(1)} %get-tuple-element.57.down), channel_id=1, source_target_pairs={{1,0},{2,1},{3,2},{4,3},{5,4},{6,5},{7,6},{8,7},{9,8},{10,9},{11,1... | collective-permute-start | bytes 393224 | tf_op jit(solution)/shard_map/ppermute | solution.py:772

commit v4 on v3

--- a/solution.py
+++ b/solution.py
@@ -454,7 +454,9 @@
         copies[2].wait()
         for m in range(3):
             high, low = split(lamb[m * NODES : (m + 1) * NODES, :])
-            got = dot(interp[0], high) + dot(interp[0], low) + dot(interp[1], high)
+            size = COMP + 2 * EDGE
+            both = dot(interp[...].reshape(2 * size, NODES), high)
+            got = both[:size] + both[size:] + dot(interp[0], low)
             comp[m * COMP : (m + 1) * COMP, :] = got[:COMP]
             comp[EDGE_LO + m * EDGE : EDGE_LO + (m + 1) * EDGE, :] = got[COMP : COMP + EDGE]
             comp[EDGE_HI + m * EDGE : EDGE_HI + (m + 1) * EDGE, :] = got[COMP + EDGE :]

time: 77.9 us -> 77.9 us (level)
  no operation moved by 1% of the time
where the time goes in v4:
time: 77.9 us; the launch traced here: 77.6 us
  starting transfers between devices  43.4 us (56%)
  Pallas kernels  22.4 us (29%)
  waiting for transfers between devices  8.6 us (11%)
  local copies, waits for them, and re-layouts  2.84 us (4%)
    ppermute x4, starting transfers between devices, exchange(): lax.ppermute(down_planes, 'elem', down_pairs)  28.3 us
    all_to_all x1, starting transfers between devices, on_device(): lax.all_to_all(block, 'elem', split_axis=0, concat_axis=0, tiled=True)  11.9 us
    pallas_call x5, Pallas kernels, call(): pl.pallas_call(kernel, out_shape=[jax.ShapeDtypeStruct(s, f32) for s in o...  10 us
    ppermute x4, waiting for transfers between devices, exchange(): lax.ppermute(up_planes, 'elem', up_pairs)  8.58 us
    pallas_call x1, Pallas kernels, on_device(): pl.pallas_call(block_kernel, out_shape=[jax.ShapeDtypeStruct((TILES * cap...  5.57 us
    pallas_call x1, Pallas kernels, on_device(): pl.pallas_call(inner, out_shape=jax.ShapeDtypeStruct(full, f32), in_specs...  3.94 us
    unnamed x22, local copies, waits for them, and re-layouts  2.84 us
    ppermute x4, starting transfers between devices, exchange(): lax.ppermute(up_planes, 'elem', up_pairs)  1.79 us
  transfers between devices with their start and end apart: 10, of which 2 were waited for; matrix products, arithmetic and copies ran while one was open for 0% of the time, Pallas kernels for 17%

profile of v4, /device:TPU:0, one launch (start us, length us, event | category | flops | bytes accessed | tf_op | source)
XLA Modules:
  0.0 77.6 jit_solution(10162385139528560102)
XLA Ops:
  0.0 5.6 %shard_map.109 = f32[2048,128]{1,0:T(8,128)} custom-call(s32[1]{0:T(128)} %bitcast.ids.refs_0_, f32[2048,256]{1,0:T(8,128)} %bitcast.13, bf16[128,192]{1,0:T(8,128)(2,1)} %constant.16.clone.les_at.les_mat.refs_7_.refs_11_.refs_8_, bf16[2,296,512]{2,1,0:T(8,128)(2,1)} %constant.18.clone.interp_at, s32[4,64]{1,0:T(4,128)} %bitcast.35), custom_call_target="tpu_custom_call" | custom-call | tf_op jit(solution)/shard_map/pallas_call | solution.py:778
  5.6 0.0 copy-start
  5.6 11.9 %all-to-all-start = ((f32[64,32,128]{2,1,0:T(8,128)}), f32[64,32,128]{2,1,0:T(8,128)}, u32[]{:S(2)}, u32[]{:S(2)}) async-start(f32[64,32,128]{2,1,0:T(8,128)} %bitcast.34), calls=%async_computation | async-start | bytes 2097152 | tf_op jit(solution)/shard_map/all_to_all | solution.py:810
  17.6 0.0 copy-start.1
  17.6 1.4 %copy-done.1 = f32[3,512,256]{2,1,0:T(8,128)S(1)} copy-done((f32[3,512,256]{2,1,0:T(8,128)S(1)}, f32[3,512,256]{2,1,0:T(8,128)}, u32[]{:S(2)}) %copy-start.1) | copy-done | bytes 1572888
  19.0 0.6 shard_map.110
  19.6 1.6 %collective-permute-start = (f32[328,128]{1,0:T(8,128)S(1)}, f32[328,128]{1,0:T(8,128)S(1)}, u32[]{:S(2)}, u32[]{:S(2)}) collective-permute-start(f32[328,128]{1,0:T(8,128)S(1)} %get-tuple-element.33), channel_id=1, source_target_pairs={{0,1},{1,2},{2,3},{3,4},{4,5},{5,6},{6,7},{7,8},{8,9},{9,10},{10,1... | collective-permute-start | bytes 503816 | tf_op jit(solution)/shard_map/ppermute | solution.py:773
  21.1 6.0 %collective-permute-start.1 = (f32[328,128]{1,0:T(8,128)S(1)}, f32[328,128]{1,0:T(8,128)S(1)}, u32[]{:S(2)}, u32[]{:S(2)}) collective-permute-start(f32[328,128]{1,0:T(8,128)S(1)} %get-tuple-element.34), channel_id=1, source_target_pairs={{1,0},{2,1},{3,2},{4,3},{5,4},{6,5},{7,6},{8,7},{9,8},{10,9},{11,1... | collective-permute-start | bytes 503816 | tf_op jit(solution)/shard_map/ppermute | solution.py:774
  27.1 7.8 %collective-permute-done.from_below = f32[328,128]{1,0:T(8,128)S(1)} collective-permute-done((f32[328,128]{1,0:T(8,128)S(1)}, f32[328,128]{1,0:T(8,128)S(1)}, u32[]{:S(2)}, u32[]{:S(2)}) %collective-permute-start) | collective-permute-done | bytes 167968 | tf_op jit(solution)/shard_map/ppermute | solution.py:773
  34.9 0.0 collective-permute-done.1.from_above
  34.9 0.0 all-to-all-done
  34.9 1.3 %collective-permute-start.2 = (f32[2048,128]{1,0:T(8,128)}, f32[2048,128]{1,0:T(8,128)S(1)}, u32[]{:S(2)}, u32[]{:S(2)}) collective-permute-start(f32[2048,128]{1,0:T(8,128)} %bitcast.5), channel_id=1, source_target_pairs={{0,64},{1,65},{2,66},{3,67},{4,68},{5,69},{6,70},{7,71},{8,72},{9,... | collective-permute-start | bytes 3145736 | tf_op jit(solution)/shard_map/ppermute | solution.py:821
  36.2 0.0 copy-start.2
  36.2 1.4 %copy-done.2 = f32[3,512,256]{2,1,0:T(8,128)S(1)} copy-done((f32[3,512,256]{2,1,0:T(8,128)S(1)}, f32[3,512,256]{2,1,0:T(8,128)}, u32[]{:S(2)}) %copy-start.2) | copy-done | bytes 1572888
  37.6 2.5 %shard_map.111 = (f32[4096,128]{1,0:T(8,128)S(1)}, f32[512,256]{1,0:T(8,128)S(1)}, f32[1024,128]{1,0:T(8,128)S(1)}) custom-call(s32[1]{0:T(128)} %bitcast.ids.refs_0_, f32[2048,256]{1,0:T(8,128)S(1)} %bitcast.15, f32[512,256]{1,0:T(8,128)S(1)} %bitcast.31, f32[1536,256]{1,0:T(8,128)S(1)} %bitcast.23, bf16[128,192]{1,0:T(8,128)(2,1)S(1)} %copy-done.4, ...), custom_call_target="tpu_custom_call" | custom-call | tf_op jit(solution)/shard_map/pallas_call | solution.py:736
  40.2 0.0 collective-permute-done.2.block
  40.2 1.5 %shard_map.112 = (f32[2048,256]{1,0:T(8,128)S(1)}, f32[1024,128]{1,0:T(8,128)S(1)}, f32[2048,256]{1,0:T(8,128)S(1)}, f32[2048,256]{1,0:T(8,128)S(1)}, f32[512,12...) custom-call(s32[1]{0:T(128)} %bitcast.ids.refs_0_, f32[2048,128]{1,0:T(8,128)S(1)} %collective-permute-done.2.block, ...), custom_call_target="tpu_custom_call" | custom-call | tf_op jit(solution)/shard_map/pallas_call | solution.py:822
  41.7 0.1 collective-permute-start.3
  41.8 7.4 %collective-permute-start.4 = (f32[256,128]{1,0:T(8,128)S(1)}, f32[256,128]{1,0:T(8,128)S(1)}, u32[]{:S(2)}, u32[]{:S(2)}) collective-permute-start(f32[256,128]{1,0:T(8,128)S(1)} %get-tuple-element.43.refs_3_), channel_id=1, source_target_pairs={{1,0},{2,1},{3,2},{4,3},{5,4},{6,5},{7,6},{8,7},{9,8},{10,9},{11,1... | collective-permute-start | bytes 393224 | tf_op jit(solution)/shard_map/ppermute | solution.py:774
  49.3 3.0 %shard_map.113 = (f32[2048,256]{1,0:T(8,128)S(1)}, f32[2048,256]{1,0:T(8,128)S(1)}) custom-call(s32[1]{0:T(128)} %bitcast.ids.refs_0_, f32[2048,256]{1,0:T(8,128)S(1)} %get-tuple-element.44.refs_1_, f32[2048,256]{1,0:T(8,128)S(1)} %get-tuple-element.45.refs_2_.refs_6_.refs_3_, f32[2048,256]{1,0:T(8,128)S(1)} %bitcast.17, ...), custom_call_target="tpu_custom_call" | custom-call | tf_op jit(solution)/shard_map/pallas_call | solution.py:736
  52.3 0.8 %collective-permute-done.3.refs_1_ = f32[256,128]{1,0:T(8,128)S(1)} collective-permute-done((f32[256,128]{1,0:T(8,128)S(1)}, f32[256,128]{1,0:T(8,128)S(1)}, u32[]{:S(2)}, u32[]{:S(2)}) %collective-permute-start.3) | collective-permute-done | bytes 131104 | tf_op jit(solution)/shard_map/ppermute | solution.py:773
  53.1 0.6 shard_map.114
  53.7 0.1 collective-permute-start.5
  53.7 7.4 %collective-permute-start.6 = (f32[256,128]{1,0:T(8,128)S(1)}, f32[256,128]{1,0:T(8,128)S(1)}, u32[]{:S(2)}, u32[]{:S(2)}) collective-permute-start(f32[256,128]{1,0:T(8,128)S(1)} %get-tuple-element.51.refs_3_), channel_id=1, source_target_pairs={{1,0},{2,1},{3,2},{4,3},{5,4},{6,5},{7,6},{8,7},{9,8},{10,9},{11,1... | collective-permute-start | bytes 393224 | tf_op jit(solution)/shard_map/ppermute | solution.py:774
  61.2 3.3 %shard_map.115 = (f32[2048,256]{1,0:T(8,128)S(1)}, f32[2048,256]{1,0:T(8,128)S(1)}) custom-call(s32[1]{0:T(128)} %bitcast.ids.refs_0_, f32[2048,256]{1,0:T(8,128)S(1)} %get-tuple-element.48.refs_5_.refs_1_, f32[512,128]{1,0:T(8,128)S(1)} %get-tuple-element.52.refs_2_, f32[2048,256]{1,0:T(8,128)S(1)} %get-tuple-element.45.refs_2_.refs_6_.refs_3_, ...), custom_call_target="tpu_custom_call" | custom-call | tf_op jit(solution)/shard_map/pallas_call | solution.py:736
  64.5 0.0 collective-permute-done.5.refs_1_
  64.6 0.6 shard_map.116
  65.2 0.1 collective-permute-start.7
  65.2 7.4 %collective-permute-start.8 = (f32[256,128]{1,0:T(8,128)S(1)}, f32[256,128]{1,0:T(8,128)S(1)}, u32[]{:S(2)}, u32[]{:S(2)}) collective-permute-start(f32[256,128]{1,0:T(8,128)S(1)} %get-tuple-element.57.down), channel_id=1, source_target_pairs={{1,0},{2,1},{3,2},{4,3},{5,4},{6,5},{7,6},{8,7},{9,8},{10,9},{11,1... | collective-permute-start | bytes 393224 | tf_op jit(solution)/shard_map/ppermute | solution.py:774
  72.7 3.9 %shard_map.117.inner = f32[2048,256]{1,0:T(8,128)} custom-call(s32[1]{0:T(128)} %bitcast.ids.refs_0_, f32[2048,256]{1,0:T(8,128)S(1)} %get-tuple-element.54.refs_5_.refs_1_, f32[512,128]{1,0:T(8,128)S(1)} %get-tuple-element.59.refs_2_, f32[2048,256]{1,0:T(8,128)S(1)} %get-tuple-element.45.refs_2_.refs_6_.refs_3_, f32[2048,256]{1,0:T(8,128)S(1)} %bitcast.21, ...), custom_call_target="tpu_custom_call" | custom-call | tf_op jit(solution)/shard_map/pallas_call | solution.py:856
  76.6 0.0 collective-permute-done.8.from_above
  76.7 0.8 %shard_map.118 = f32[2048,256]{1,0:T(8,128)} custom-call(s32[1]{0:T(128)} %bitcast.ids.refs_0_, f32[256,128]{1,0:T(8,128)S(1)} %collective-permute-done.7.from_below, f32[256,128]{1,0:T(8,128)S(1)} %collective-permute-done.8.from_above, f32[256,128]{1,0:T(8,128)S(1)} %get-tuple-element.57.down, ...), custom_call_target="tpu_custom_call", output_to_operand_aliasing={{}: (7, {})} | custom-call | tf_op jit(solution)/shard_map/pallas_call | solution.py:874
  (20 shorter events, 0.0 us)
Async XLA Ops:
  0.0 17.5 %copy-start.4 = (bf16[128,192]{1,0:T(8,128)(2,1)S(1)}, bf16[128,192]{1,0:T(8,128)(2,1)}, u32[]{:S(2)}) copy-start(bf16[128,192]{1,0:T(8,128)(2,1)} %constant.16.clone.les_at.les_mat.refs_7_.refs_11_.refs_8_) | copy-start | bytes 147460
  0.0 17.5 %copy-start.5 = (bf16[96,144]{1,0:T(8,128)(2,1)S(1)}, bf16[96,144]{1,0:T(8,128)(2,1)}, u32[]{:S(2)}) copy-start(bf16[96,144]{1,0:T(8,128)(2,1)} %constant.17.clone.ape_mat.refs_8_.refs_12_.refs_9_) | copy-start | bytes 82948
  0.0 17.6 %copy-start.6 = (f32[1,512,256]{2,1,0:T(8,128)S(1)}, f32[1,512,256]{2,1,0:T(8,128)}, u32[]{:S(2)}) copy-start(f32[1,512,256]{2,1,0:T(8,128)} %param.13) | copy-start | bytes 1572868
  0.0 17.6 %copy-start.9 = (s32[1,64,4]{1,2,0:T(4,128)S(1)}, s32[1,64,4]{1,2,0:T(4,128)}, u32[]{:S(2)}) copy-start(s32[1,64,4]{1,2,0:T(4,128)} %param.15) | copy-start | bytes 3076
  0.0 17.6 %copy-start.10 = (s32[1,64]{1,0:T(1,128)S(1)}, s32[1,64]{1,0:T(1,128)}, u32[]{:S(2)}) copy-start(s32[1,64]{1,0:T(1,128)} %count.3) | copy-start | bytes 772
  5.6 12.0 %copy-start = (f32[1,4,512,256]{3,2,1,0:T(8,128)S(1)}, f32[1,4,512,256]{3,2,1,0:T(8,128)}, u32[]{:S(2)}) copy-start(f32[1,4,512,256]{3,2,1,0:T(8,128)} %param.11) | copy-start | bytes 6291460
  5.6 29.3 %all-to-all-start = ((f32[64,32,128]{2,1,0:T(8,128)}), f32[64,32,128]{2,1,0:T(8,128)}, u32[]{:S(2)}, u32[]{:S(2)}) async-start(f32[64,32,128]{2,1,0:T(8,128)} %bitcast.34), calls=%async_computation | async-start | bytes 2097152 | tf_op jit(solution)/shard_map/all_to_all | solution.py:810
  17.6 1.4 %copy-start.1 = (f32[3,512,256]{2,1,0:T(8,128)S(1)}, f32[3,512,256]{2,1,0:T(8,128)}, u32[]{:S(2)}) copy-start(f32[3,512,256]{2,1,0:T(8,128)} %param.12) | copy-start | bytes 4718596
  19.6 15.3 %collective-permute-start = (f32[328,128]{1,0:T(8,128)S(1)}, f32[328,128]{1,0:T(8,128)S(1)}, u32[]{:S(2)}, u32[]{:S(2)}) collective-permute-start(f32[328,128]{1,0:T(8,128)S(1)} %get-tuple-element.33), channel_id=1, source_target_pairs={{0,1},{1,2},{2,3},{3,4},{4,5},{5,6},{6,7},{7,8},{8,9},{9,10},{10,1... | collective-permute-start | bytes 503816 | tf_op jit(solution)/shard_map/ppermute | solution.py:773
  21.1 13.7 %collective-permute-start.1 = (f32[328,128]{1,0:T(8,128)S(1)}, f32[328,128]{1,0:T(8,128)S(1)}, u32[]{:S(2)}, u32[]{:S(2)}) collective-permute-start(f32[328,128]{1,0:T(8,128)S(1)} %get-tuple-element.34), channel_id=1, source_target_pairs={{1,0},{2,1},{3,2},{4,3},{5,4},{6,5},{7,6},{8,7},{9,8},{10,9},{11,1... | collective-permute-start | bytes 503816 | tf_op jit(solution)/shard_map/ppermute | solution.py:774
  34.9 5.3 %collective-permute-start.2 = (f32[2048,128]{1,0:T(8,128)}, f32[2048,128]{1,0:T(8,128)S(1)}, u32[]{:S(2)}, u32[]{:S(2)}) collective-permute-start(f32[2048,128]{1,0:T(8,128)} %bitcast.5), channel_id=1, source_target_pairs={{0,64},{1,65},{2,66},{3,67},{4,68},{5,69},{6,70},{7,71},{8,72},{9,... | collective-permute-start | bytes 3145736 | tf_op jit(solution)/shard_map/ppermute | solution.py:821
  36.2 1.4 %copy-start.2 = (f32[3,512,256]{2,1,0:T(8,128)S(1)}, f32[3,512,256]{2,1,0:T(8,128)}, u32[]{:S(2)}) copy-start(f32[3,512,256]{2,1,0:T(8,128)} %param.12) | copy-start | bytes 4718596
  37.6 2.5 %copy-start.3 = (f32[3,512,256]{2,1,0:T(8,128)S(1)}, f32[3,512,256]{2,1,0:T(8,128)}, u32[]{:S(2)}) copy-start(f32[3,512,256]{2,1,0:T(8,128)} %param.12) | copy-start | bytes 4718596
  37.6 2.5 %copy-start.7 = (bf16[384,432]{1,0:T(8,128)(2,1)S(1)}, bf16[384,432]{1,0:T(8,128)(2,1)}, u32[]{:S(2)}) copy-start(bf16[384,432]{1,0:T(8,128)(2,1)} %constant.19.clone.place) | copy-start | bytes 995332
  37.6 2.6 %copy-start.8 = (bf16[64,80]{1,0:T(8,128)(2,1)S(1)}, bf16[64,80]{1,0:T(8,128)(2,1)}, u32[]{:S(2)}) copy-start(bf16[64,80]{1,0:T(8,128)(2,1)} %constant.20.clone.place_edge) | copy-start | bytes 30724
  41.7 11.4 %collective-permute-start.3 = (f32[256,128]{1,0:T(8,128)S(1)}, f32[256,128]{1,0:T(8,128)S(1)}, u32[]{:S(2)}, u32[]{:S(2)}) collective-permute-start(f32[256,128]{1,0:T(8,128)S(1)} %get-tuple-element.42.refs_4_), channel_id=1, source_target_pairs={{0,1},{1,2},{2,3},{3,4},{4,5},{5,6},{6,7},{7,8},{8,9},{9,10},{10,1... | collective-permute-start | bytes 393224 | tf_op jit(solution)/shard_map/ppermute | solution.py:773
  41.8 11.3 %collective-permute-start.4 = (f32[256,128]{1,0:T(8,128)S(1)}, f32[256,128]{1,0:T(8,128)S(1)}, u32[]{:S(2)}, u32[]{:S(2)}) collective-permute-start(f32[256,128]{1,0:T(8,128)S(1)} %get-tuple-element.43.refs_3_), channel_id=1, source_target_pairs={{1,0},{2,1},{3,2},{4,3},{5,4},{6,5},{7,6},{8,7},{9,8},{10,9},{11,1... | collective-permute-start | bytes 393224 | tf_op jit(solution)/shard_map/ppermute | solution.py:774
  53.7 10.9 %collective-permute-start.5 = (f32[256,128]{1,0:T(8,128)S(1)}, f32[256,128]{1,0:T(8,128)S(1)}, u32[]{:S(2)}, u32[]{:S(2)}) collective-permute-start(f32[256,128]{1,0:T(8,128)S(1)} %get-tuple-element.50.refs_4_), channel_id=1, source_target_pairs={{0,1},{1,2},{2,3},{3,4},{4,5},{5,6},{6,7},{7,8},{8,9},{9,10},{10,1... | collective-permute-start | bytes 393224 | tf_op jit(solution)/shard_map/ppermute | solution.py:773
  53.7 10.8 %collective-permute-start.6 = (f32[256,128]{1,0:T(8,128)S(1)}, f32[256,128]{1,0:T(8,128)S(1)}, u32[]{:S(2)}, u32[]{:S(2)}) collective-permute-start(f32[256,128]{1,0:T(8,128)S(1)} %get-tuple-element.51.refs_3_), channel_id=1, source_target_pairs={{1,0},{2,1},{3,2},{4,3},{5,4},{6,5},{7,6},{8,7},{9,8},{10,9},{11,1... | collective-permute-start | bytes 393224 | tf_op jit(solution)/shard_map/ppermute | solution.py:774
  65.2 11.5 %collective-permute-start.7 = (f32[256,128]{1,0:T(8,128)S(1)}, f32[256,128]{1,0:T(8,128)S(1)}, u32[]{:S(2)}, u32[]{:S(2)}) collective-permute-start(f32[256,128]{1,0:T(8,128)S(1)} %get-tuple-element.56.up_planes), channel_id=1, source_target_pairs={{0,1},{1,2},{2,3},{3,4},{4,5},{5,6},{6,7},{7,8},{8,9},{9,10},{10,1... | collective-permute-start | bytes 393224 | tf_op jit(solution)/shard_map/ppermute | solution.py:773
  65.2 11.4 %collective-permute-start.8 = (f32[256,128]{1,0:T(8,128)S(1)}, f32[256,128]{1,0:T(8,128)S(1)}, u32[]{:S(2)}, u32[]{:S(2)}) collective-permute-start(f32[256,128]{1,0:T(8,128)S(1)} %get-tuple-element.57.down), channel_id=1, source_target_pairs={{1,0},{2,1},{3,2},{4,3},{5,4},{6,5},{7,6},{8,7},{9,8},{10,9},{11,1... | collective-permute-start | bytes 393224 | tf_op jit(solution)/shard_map/ppermute | solution.py:774
